TPU v7x, 32 devices: a whole 2x2x4 slice. The times are simulated.
32 devices in a mesh: dp: 4 (over y, core), wide: 8 (over z, x).
Axes of the slice: x: 2, y: 2, z: 4, core: 2. Of those that a mesh axis runs over, the one named last changes fastest.
Arguments:
- tokens: bfloat16 [32768, 768], P(('dp', 'wide')), may hold values from -6 to 6
- segments: int32 [32768], P(('dp', 'wide')), may hold values from 0 to 15, as said below
- counts: int32 [32], P(('dp', 'wide')), may hold values from 256 to 1024, as said below
- out_grad: bfloat16 [32768, 768], P(('dp', 'wide')), may hold values from -6 to 6
- attn_param: float32 [2363136], P(('dp', 'wide')), may hold values from -2.5 to 2.5
- attn_moment: float32 [2363136], P(('dp', 'wide')), may hold values from -0.03125 to 0.03125
- attn_square: float32 [2363136], P(('dp', 'wide')), may hold values from 1e-09 to 1e-07
- attn_shadow: float32 [2363136], P(('dp', 'wide')), may hold values from -0.75 to 0.75
- ffn_param: float32 [4723968], P(('dp', 'wide')), may hold values from -1.5 to 1.5
- ffn_moment: float32 [4723968], P(('dp', 'wide')), may hold values from -0.03125 to 0.03125
- ffn_square: float32 [4723968], P(('dp', 'wide')), may hold values from 1e-09 to 1e-07
- ffn_shadow: float32 [4723968], P(('dp', 'wide')), may hold values from -0.75 to 0.75
Outputs:
- activations: bfloat16 [32768, 768], P(('dp', 'wide'))
- pooled: float32 [512, 768], P(('dp', 'wide'))
- token_grad: bfloat16 [32768, 768], P(('dp', 'wide'))
- attn_grad: float32 [2363136], P(('dp', 'wide'))
- ffn_grad: float32 [4723968], P(('dp', 'wide'))
- attn_change: float32 [2363136], P(('dp', 'wide'))
- ffn_change: float32 [4723968], P(('dp', 'wide'))
- moment_attn: float32 [2363136], P(('dp', 'wide'))
- moment_ffn: float32 [4723968], P(('dp', 'wide'))
- square_attn: float32 [2363136], P(('dp', 'wide'))
- square_ffn: float32 [4723968], P(('dp', 'wide'))
- drift_attn: float32 [2363136], P(('dp', 'wide'))
- drift_ffn: float32 [4723968], P(('dp', 'wide'))
Inputs may be any that keep to these rules, and one draw needn't show every extreme that they name: `counts`: true tokens of each row of 1024 positions; the later positions of the row are padding. `segments`: starts at 0 and never falls within each row of 1024 positions; a run of one number is 64 to 256 positions long, the last run of a row possibly shorter.
All inputs are finite; a program needn't handle non-finite values.
Results may differ from a plain program's by a relative error of at most 0.012.
The roundings to bfloat16 on the way count: a program that leaves them out, or rounds other values in their place, can miss the bound.
Values may be sent and summed in bfloat16 or wider, within the bound.
No kernel may reach another device: no remote copies, remote signals or barrier semaphores. Data moves between devices by JAX's collectives and lax.ppermute only.
A program may use at most 256 MiB of HBM per device.

v0:
```python
import functools

import jax
import jax.numpy as jnp
from jax import lax
from jax.experimental import pallas as pl
from jax.experimental.pallas import tpu as pltpu
from jax.sharding import PartitionSpec as P

D = 768
FF = 3072
HEAD = 64
HEADS = 12
ROW = 1024
STEP = 10
CROPS = 16

NORM_EPSILON = 1e-12
NEGATIVE = -1e30
MOMENT_DECAY = 0.9
SQUARE_DECAY = 0.999
LEARN_RATE = 0.001
WEIGHT_DECAY = 0.01
ADAM_EPSILON = 1e-08
SHADOW_RATE = 0.9995
SCALE = HEAD ** (-0.5)

AXES = ("dp", "wide")
BF = jnp.bfloat16
F32 = jnp.float32
UP_CHUNKS = FF // D
ATTN_ROWS = 4 * D
FFN_ROWS = 2 * FF
ATTN_TAIL = 5 * D
FFN_TAIL = FF + 3 * D
AHEAD_PAIRS = (2, 2, 2)
PAIRS = (2, 4)
VEC_ROWS = 16
COUNT_ROW = 12
MIB = 1 << 20
BACK_VMEM = 24 * MIB
TERMS_VMEM = 24 * MIB
TOKEN_VMEM = 24 * MIB
FFN_VMEM = 56 * MIB
ADD_VMEM = 24 * MIB


def dot(left, right, left_dim, right_dim):
    return lax.dot_general(
        left, right, (((left_dim,), (right_dim,)), ((), ())), preferred_element_type=F32
    )


class Places:
    def __init__(self, mesh):
        self.dp, self.wide = mesh.shape["dp"], mesh.shape["wide"]
        self.count = self.dp * self.wide
        self.size = {"c": 2, "y": self.dp // 2}
        self.size["x"] = self.size["y"]
        self.size["z"] = self.wide // self.size["x"]

    def staged(self):
        exact = self.dp == 4 and self.wide % self.size["x"] == 0
        return exact and D % (16 * UP_CHUNKS * self.wide // 2) == 0

    def index(self, y, c, z, x):
        return (y * 2 + c) * self.wide + z * self.size["x"] + x

    def rotation(self, axis, step):
        pairs = []
        extent = self.size
        for y in range(extent["y"]):
            for c in range(2):
                along = axis if len(axis) == 1 else axis[c]
                for z in range(extent["z"]):
                    for x in range(extent["x"]):
                        at = {"y": y, "c": c, "z": z, "x": x}
                        to = dict(at)
                        to[along] = (at[along] + step) % extent[along]
                        pairs.append((self.index(**at), self.index(**to)))
        return pairs

    def send(self, array, axis, step):
        return lax.ppermute(array, AXES, self.rotation(axis, step))

    def here(self):
        outer, inner = lax.axis_index("dp"), lax.axis_index("wide")
        extent = self.size["x"]
        return {"y": outer // 2, "c": outer % 2, "z": inner // extent, "x": inner % extent}


def order(array, *before):
    return lax.optimization_barrier((array,) + before)[0]


class Gathered:
    def __init__(self, places, rows):
        self.places, self.rows = places, rows
        self.deep = places.size["z"] * rows

    def start_z(self, own):
        extent = self.places.size["z"]
        return [own] + [self.places.send(own, "z", k) for k in range(1, extent)]

    def join_z(self, here, blocks):
        rows, extent = self.rows, self.places.size["z"]
        near = jnp.zeros((self.deep, D), BF)
        for k, block in enumerate(blocks):
            at = lax.rem(here["z"] + (extent - k), extent) * rows
            near = lax.dynamic_update_slice_in_dim(near, block[:rows], at, 0)
        return jnp.concatenate([near, self.total([b[rows:] for b in blocks])], 0)

    def join_parts(self, me, parts):
        extent, count = self.places.size["z"], len(parts)
        share = self.rows // count

        def kernel(me_ref, *refs):
            out, sem = refs[-2:]
            for p in range(count):
                for k in range(extent):
                    at = lax.rem(me_ref[2] + (extent - k), extent)
                    pltpu.make_async_copy(
                        refs[p * extent + k], out.at[at, pl.ds(p * share, share)], sem
                    ).start()
            pltpu.make_async_copy(out, out, sem).wait()

        blocks = [b for part in parts for b in part]
        return pl.pallas_call(
            kernel,
            in_specs=[pl.BlockSpec(memory_space=pltpu.SMEM)]
            + [pl.BlockSpec(memory_space=pl.ANY)] * len(blocks),
            out_specs=pl.BlockSpec(memory_space=pltpu.VMEM),
            out_shape=jax.ShapeDtypeStruct((extent, self.rows, D), BF),
            scratch_shapes=[pltpu.SemaphoreType.DMA],
            compiler_params=pltpu.CompilerParams(vmem_limit_bytes=16 * MIB),
            cost_estimate=cost(2),
            name="join",
        )(me, *blocks).reshape(self.deep, D)

    def along_first(self, near):
        places, extent = self.places, self.places.size
        blocks = [near] + [places.send(near, "xy", k) for k in range(1, extent["x"])]
        parts = [b[: self.deep] for b in blocks]
        if near.shape[0] > self.deep:
            parts.append(self.total([b[self.deep :] for b in blocks]))
        return jnp.concatenate(parts, 0)

    def along_second(self, near):
        return [self.places.send(near, "yx", k) for k in range(1, self.places.size["x"])]

    def from_core(self, groups):
        return [self.places.send(g, "c", 1) for g in groups]

    def total(self, arrays):
        result = arrays[0].astype(F32)
        for a in arrays[1:]:
            result = result + a.astype(F32)
        return result.astype(BF)

    def place(self, here, far, first, second):
        extent = self.places.size

        def back(axis, step):
            return lax.rem(here[axis] + (extent[axis] - step), extent[axis])

        core = here["c"] if far == 0 else 1 - here["c"]
        y = jnp.where(core == 0, back("y", second), back("y", first))
        x = jnp.where(core == 0, back("x", first), back("x", second))
        return y, core, x


def read_here(me_ref):
    return {"y": me_ref[0], "c": me_ref[1], "z": me_ref[2], "x": me_ref[3]}


def add_routed(me, keep, arrived, grid, routes, source_block, target_block, target_lead, micros):
    rows, width = keep.shape[-2:]

    def kernel(me_ref, *refs):
        for i in range(len(routes)):
            total = refs[2 * i][...].astype(F32) + refs[2 * i + 1][...].astype(F32)
            refs[2 * len(routes) + i][...] = total.astype(BF)

    def source(route):
        return pl.BlockSpec(source_block + (rows, width), lambda *at: route(*at) + (0, 0))

    target = pl.BlockSpec(target_block[0] + (rows, width), lambda *at: target_block[1](*at) + (0, 0))
    return pl.pallas_call(
        kernel,
        grid_spec=pltpu.PrefetchScalarGridSpec(
            num_scalar_prefetch=1,
            grid=grid,
            in_specs=[source(r) for r in routes for _ in range(2)],
            out_specs=[target] * len(routes),
        ),
        out_shape=[jax.ShapeDtypeStruct(target_lead + (rows, width), BF)] * len(routes),
        compiler_params=pltpu.CompilerParams(vmem_limit_bytes=ADD_VMEM),
        cost_estimate=cost(micros),
        name="add_routed",
    )(me, *([keep, arrived] * len(routes)))


class Scattered:
    def __init__(self, places, me, micros):
        self.places, self.me, self.micros = places, me, micros
        self.z = places.size["z"]

    def core(self, give):
        return self.places.send(give, "c", 1)

    def first(self, keep, arrived):
        deep = 2

        def route(far):
            def pick_block(z, e, me):
                y, x = jnp.abs(me[0] - far), jnp.abs(me[3] - far)
                return jnp.where(me[1] == 0, e, y), z, jnp.where(me[1] == 0, x, e)

            return pick_block

        own, cut = add_routed(
            self.me,
            keep,
            arrived,
            (self.z // deep, 2),
            [route(0), route(1)],
            (None, deep, None),
            ((deep, None), lambda z, e, me: (z, e)),
            (self.z, 2),
            4 * self.micros,
        )
        return own, cut

    def second(self, keep, arrived):
        deep = 2

        def route(far):
            return lambda z, me: (z, jnp.abs(jnp.where(me[1] == 0, me[0], me[3]) - far))

        own, cut = add_routed(
            self.me,
            keep,
            arrived,
            (self.z // deep,),
            [route(0), route(1)],
            (deep, None),
            ((deep,), lambda z, me: (z,)),
            (self.z,),
            2 * self.micros,
        )
        return own, cut

    def along_z(self, keep, arrived):
        def route(k):
            return lambda i, me: (lax.rem(me[2] + k, self.z),)

        own, *cuts = add_routed(
            self.me,
            keep,
            arrived,
            (1,),
            [route(k) for k in range(self.z)],
            (None,),
            ((None,), lambda i, me: (0,)),
            (1,),
            self.micros,
        )
        return own, cuts

    def send(self, cut, *before):
        return self.places.send(order(cut, *before), "xy", 1)

    def send_second(self, cut, *before):
        return self.places.send(order(cut, *before), "yx", 1)

    def send_z(self, cuts, *before):
        return [self.places.send(order(c, *before), "z", k + 1) for k, c in enumerate(cuts)]

    def result(self, own, arrived):
        total = own[0].astype(F32)
        for a in arrived:
            total = total + a[0].astype(F32)
        return total


def to_rows(places, me, flat, rows, tail):
    count = places.count
    block = rows // count * D
    slack = tail // count
    before = lax.ppermute(flat[-tail:], AXES, [(i, i + 1) for i in range(count - 1)])
    joined = jnp.concatenate([before, flat])
    return lax.dynamic_slice_in_dim(joined, tail - me * slack, block).reshape(rows // count, D)


def to_flat(places, me, block, vectors, tail):
    count = places.count
    slack = tail // count
    after = lax.ppermute(block[: tail // D], AXES, [(i + 1, i) for i in range(count - 1)])
    after = jnp.where(me == count - 1, vectors, after)
    joined = jnp.concatenate([block, after], 0).reshape(-1)
    return lax.dynamic_slice_in_dim(joined, me * slack, block.size + slack)


def project_body(step, tokens, weights, vec, query, key, value):
    held = tokens[...]
    query[...] = (dot(held, weights[0:D], 1, 0) + vec[0:1]).astype(BF)
    key[...] = dot(held, weights[D : 2 * D], 1, 0).astype(BF)
    value[...] = (dot(held, weights[2 * D : 3 * D], 1, 0) + vec[1:2]).astype(BF)


def project_kernel(gathered, number, after, me, tokens, *refs):
    groups = refs[:number]
    query, key, value, vec, whole, weights, extras, sem, extra_sem, out_sem = refs[number + after :]
    step = pl.program_id(0)
    extent = gathered.places.size
    rows, deep = gathered.rows, gathered.rows * extent["z"]

    @pl.when(step == 0)
    def _():
        here = read_here(me)
        for g, ref in enumerate(groups):
            pltpu.make_async_copy(
                ref.at[pl.ds(extent["x"] * deep, VEC_ROWS)], extras.at[g], extra_sem
            ).start()
        shape = (extent["y"], 2, extent["z"], extent["x"], rows, D)
        for g, ref in enumerate(groups):
            far, second = divmod(g, extent["x"])
            for first in range(extent["x"]):
                y, core, x = gathered.place(here, far, first, second)
                pltpu.make_async_copy(
                    ref.at[pl.ds(first * deep, deep)].reshape(extent["z"], rows, D),
                    weights.reshape(*shape).at[y, core, :, x],
                    sem,
                ).start()
        pltpu.make_async_copy(extras, extras, extra_sem).wait()
        total = extras[0].astype(F32)
        for g in range(1, number):
            total = total + extras[g].astype(F32)
        vec[...] = total
        pltpu.make_async_copy(weights, weights, sem).wait()
        pltpu.make_async_copy(weights, whole, out_sem).start()

    project_body(step, tokens, weights, vec, query, key, value)

    @pl.when(step == pl.num_programs(0) - 1)
    def _():
        pltpu.make_async_copy(weights, whole, out_sem).wait()


PROJECT_ROWS = 256


def project(tokens, me, gathered, groups, after):
    rows = tokens.shape[0]
    tile = pl.BlockSpec((PROJECT_ROWS, D), lambda i: (i, 0))
    number = len(groups)
    return pl.pallas_call(
        functools.partial(project_kernel, gathered, number, len(after)),
        grid=(rows // PROJECT_ROWS,),
        in_specs=[pl.BlockSpec(memory_space=pltpu.SMEM), tile]
        + [pl.BlockSpec(memory_space=pl.ANY)] * (number + len(after)),
        out_specs=[tile] * 3
        + [pl.BlockSpec((VEC_ROWS, D), lambda i: (0, 0)), pl.BlockSpec(memory_space=pl.ANY)],
        out_shape=[jax.ShapeDtypeStruct((rows, D), BF)] * 3
        + [jax.ShapeDtypeStruct((VEC_ROWS, D), F32), jax.ShapeDtypeStruct((ATTN_ROWS, D), BF)],
        scratch_shapes=[
            pltpu.VMEM((ATTN_ROWS, D), BF),
            pltpu.VMEM((number, VEC_ROWS, D), BF),
            pltpu.SemaphoreType.DMA,
            pltpu.SemaphoreType.DMA,
            pltpu.SemaphoreType.DMA,
        ],
        compiler_params=pltpu.CompilerParams(vmem_limit_bytes=24 * MIB),
        cost_estimate=cost(8),
        name="project",
    )(me, tokens, *groups, *after)


def project_whole(tokens, weights, vec):
    rows = tokens.shape[0]
    tile = pl.BlockSpec((PROJECT_ROWS, D), lambda i: (i, 0))
    return pl.pallas_call(
        lambda *refs: project_body(None, *refs),
        grid=(rows // PROJECT_ROWS,),
        in_specs=[
            tile,
            pl.BlockSpec((ATTN_ROWS, D), lambda i: (0, 0), pipeline_mode=pl.Buffered(1)),
            pl.BlockSpec((VEC_ROWS, D), lambda i: (0, 0)),
        ],
        out_specs=[tile] * 3,
        out_shape=[jax.ShapeDtypeStruct((rows, D), BF)] * 3,
        compiler_params=pltpu.CompilerParams(vmem_limit_bytes=24 * MIB),
        name="project",
    )(tokens, weights, vec)


QUERY_BLOCK = 256
QUERY_BLOCKS = ROW // QUERY_BLOCK


def window(block):
    low = max(0, block - 1) * QUERY_BLOCK
    return low, min(QUERY_BLOCKS, block + 2) * QUERY_BLOCK


def fill_bias(bias, seg_column, seg_row, count):
    for block in range(QUERY_BLOCKS):
        low, high = window(block)
        at = slice(block * QUERY_BLOCK, (block + 1) * QUERY_BLOCK)
        shape = (high - low, QUERY_BLOCK)
        key_pos = low + lax.broadcasted_iota(jnp.int32, shape, 0)
        query_pos = block * QUERY_BLOCK + lax.broadcasted_iota(jnp.int32, shape, 1)
        same = seg_column[low:high, 0:1] == seg_row[0:1, at]
        allowed = (same & (key_pos < count)) | (key_pos == query_pos)
        bias[0 : high - low, at] = jnp.where(allowed, 0.0, NEGATIVE).astype(F32)


def one_head(transposed):
    zero = jnp.zeros((HEAD, transposed.shape[1]), transposed.dtype)
    return (
        jnp.concatenate([transposed[:HEAD], zero], 0),
        jnp.concatenate([zero, transposed[HEAD:]], 0),
    )


def attend_kernel(count, seg_column, seg_row, query, key, value, *refs):
    mixed, log_total, bias = refs[-3:]

    @pl.when(pl.program_id(0) == 0)
    def _():
        fill_bias(bias, seg_column, seg_row, count[0])

    value_t = value[...].T
    query_t = one_head((query[...] * jnp.asarray(SCALE, BF)).T)
    for block in range(QUERY_BLOCKS):
        low, high = window(block)
        at = slice(block * QUERY_BLOCK, (block + 1) * QUERY_BLOCK)
        parts = []
        for h in range(2):
            scores = dot(key[low:high, :], query_t[h][:, at], 1, 0) + bias[0 : high - low, at]
            top = jnp.max(scores, axis=0, keepdims=True)
            shifted = jnp.exp(scores - top)
            total = jnp.sum(shifted, axis=0, keepdims=True)
            part = dot(value_t[h * HEAD : (h + 1) * HEAD, low:high], shifted.astype(BF), 1, 0)
            parts.append(part * (1.0 / total))
            log_total[0, h : h + 1, at] = top + jnp.log(total)
        mixed[at, :] = jnp.concatenate(parts, 0).T.astype(BF)


def attend_specs():
    return [
        pl.BlockSpec(memory_space=pltpu.SMEM),
        pl.BlockSpec((ROW, 1), lambda h: (0, 0)),
        pl.BlockSpec((1, ROW), lambda h: (0, 0)),
    ]


def attend(query, key, value, segments, count, first, pairs, after):
    pair = pl.BlockSpec((ROW, 2 * HEAD), lambda h: (0, h + first))
    return pl.pallas_call(
        attend_kernel,
        grid=(pairs,),
        in_specs=attend_specs() + [pair] * 3 + [pl.BlockSpec(memory_space=pl.ANY)] * len(after),
        out_specs=[
            pl.BlockSpec((ROW, 2 * HEAD), lambda h: (0, h)),
            pl.BlockSpec((1, 8, ROW), lambda h: (h, 0, 0)),
        ],
        out_shape=[
            jax.ShapeDtypeStruct((ROW, pairs * 2 * HEAD), BF),
            jax.ShapeDtypeStruct((pairs, 8, ROW), F32),
        ],
        scratch_shapes=[pltpu.VMEM((3 * QUERY_BLOCK, ROW), F32)],
        compiler_params=pltpu.CompilerParams(vmem_limit_bytes=24 * MIB),
        cost_estimate=cost(25 * pairs / 6),
        name="attend",
    )(count, segments.reshape(ROW, 1), segments.reshape(1, ROW), query, key, value, *after)


def attend_back_kernel(
    count, seg_column, seg_row, query, key, value, grad, log_total, *refs
):
    grads, sums, bias, key_sum, value_sum = refs[-5:]

    @pl.when(pl.program_id(0) == 0)
    def _():
        fill_bias(bias, seg_column, seg_row, count[0])

    query_t = (query[...] * jnp.asarray(SCALE, BF)).T
    key_t = key[...].T
    grad_t = grad[...].T
    query_one, grad_one = one_head(query_t), one_head(grad_t)
    key_sum[...] = jnp.zeros_like(key_sum)
    value_sum[...] = jnp.zeros_like(value_sum)
    for block in range(QUERY_BLOCKS):
        low, high = window(block)
        at = slice(block * QUERY_BLOCK, (block + 1) * QUERY_BLOCK)
        parts = []
        for h in range(2):
            rows = slice(h * HEAD, (h + 1) * HEAD)
            scores = dot(key[low:high, :], query_one[h][:, at], 1, 0) + bias[0 : high - low, at]
            probs = jnp.exp(scores - log_total[0, h : h + 1, at])
            grad_probs = dot(value[low:high, :], grad_one[h][:, at], 1, 0)
            weighted = probs * grad_probs
            total = jnp.sum(weighted, axis=0, keepdims=True)
            grad_scores = (weighted - probs * total).astype(BF)
            parts.append(dot(key_t[rows, low:high], grad_scores, 1, 0))
            key_sum[rows, low:high] += dot(query_t[rows, at], grad_scores, 1, 1)
            value_sum[rows, low:high] += dot(grad_t[rows, at], probs.astype(BF), 1, 1)
        grads[0, at, :] = (jnp.concatenate(parts, 0) * SCALE).T.astype(BF)
    grads[1] = key_sum[...].T.astype(BF)
    grads[2] = value_sum[...].T.astype(BF)
    sums[...] = jnp.zeros_like(sums)
    sums[0:1] = column_sum(grads[0].astype(F32))
    sums[1:2] = column_sum(grads[2].astype(F32))


def attend_back(query, key, value, grad, log_total, segments, count, first, pairs, after, micros):
    pair = pl.BlockSpec((ROW, 2 * HEAD), lambda h: (0, h + first))
    return pl.pallas_call(
        attend_back_kernel,
        grid=(pairs,),
        in_specs=attend_specs()
        + [pair] * 4
        + [pl.BlockSpec((1, 8, ROW), lambda h: (h + first, 0, 0))]
        + [pl.BlockSpec(memory_space=pl.ANY)] * len(after),
        out_specs=[
            pl.BlockSpec((3, ROW, 2 * HEAD), lambda h: (0, 0, h)),
            pl.BlockSpec((8, 2 * HEAD), lambda h: (0, h)),
        ],
        out_shape=[
            jax.ShapeDtypeStruct((3, ROW, pairs * 2 * HEAD), BF),
            jax.ShapeDtypeStruct((8, pairs * 2 * HEAD), F32),
        ],
        scratch_shapes=[
            pltpu.VMEM((3 * QUERY_BLOCK, ROW), F32),
            pltpu.VMEM((2 * HEAD, ROW), F32),
            pltpu.VMEM((2 * HEAD, ROW), F32),
        ],
        compiler_params=pltpu.CompilerParams(vmem_limit_bytes=BACK_VMEM),
        cost_estimate=cost(micros),
        name="attend_back",
    )(
        count,
        segments.reshape(ROW, 1),
        segments.reshape(1, ROW),
        query,
        key,
        value,
        grad,
        log_total,
        *after,
    )


def normalise(resid):
    centred = resid - jnp.mean(resid, axis=-1, keepdims=True)
    spread = jnp.mean(centred * centred, axis=-1, keepdims=True)
    inverse = lax.rsqrt(spread + NORM_EPSILON)
    return centred * inverse, inverse


def normalise_back(cotangent, gain, normal, inverse):
    scaled = cotangent * gain
    mean = jnp.mean(scaled, axis=-1, keepdims=True)
    aligned = jnp.mean(scaled * normal, axis=-1, keepdims=True)
    return inverse * (scaled - mean - normal * aligned)


def cost(micros):
    return pl.CostEstimate(flops=int(micros * 1.1e9), bytes_accessed=MIB, transcendentals=0)


def column_sum(array):
    return jnp.sum(array, axis=0, keepdims=True)


MIDDLE_ROWS = 256


def middle_kernel(
    fetch,
    groups,
    count,
    me,
    seg_row,
    tokens,
    out_grad,
    w_out,
    vec,
    *refs,
):
    mixed = jnp.concatenate([ref[...] for ref in refs[: len(AHEAD_PAIRS)]], 1)
    refs = refs[len(AHEAD_PAIRS) :]

    (
        final_low,
        hidden_low,
        activated,
        grad_pre,
        grad_ffn_out,
        grad_attn_out,
        grad_mixed,
        grad_resid,
        vec_grad,
        crop_sums,
        slope,
        weights,
        sem,
    ) = refs[groups:]
    step = pl.program_id(0)

    @pl.when(step == 0)
    def _():
        vec_grad[...] = jnp.zeros_like(vec_grad)
        crop_sums[...] = jnp.zeros_like(crop_sums)
        fetch(read_here(me), refs[:groups], weights, sem)

    def row(i):
        return vec[i : i + 1]

    def chunk(j):
        return weights[j * D : (j + 1) * D]

    def note(i, value):
        vec_grad[i : i + 1] += value

    resid_one = tokens[...].astype(F32) + (dot(mixed, w_out[...], 1, 0) + row(2))
    normal_one, inverse_one = normalise(resid_one)
    hidden = normal_one * row(3) + row(4)
    low = hidden.astype(BF)
    hidden_low[...] = low
    total = hidden + row(9)

    def arrived(first, chunks, which):
        @pl.when(step == 0)
        def _():
            part = weights.at[pl.ds(first * D, chunks * D)]
            pltpu.make_async_copy(part, part, sem.at[which]).wait()

    for j in range(UP_CHUNKS):
        at = slice(j * D, (j + 1) * D)
        arrived(j, 1, j)
        pre = dot(low, chunk(j), 1, 0) + row(5 + j)
        share = 0.5 + 0.5 * lax.erf(pre * (0.5**0.5))
        density = jnp.exp(-0.5 * pre * pre) * 0.3989422804014327
        slope[:, at] = share + pre * density
        act = (pre * share).astype(BF)
        activated[:, at] = act
        if j == 0:
            arrived(UP_CHUNKS, UP_CHUNKS, UP_CHUNKS)
        total = total + dot(act, chunk(UP_CHUNKS + j), 1, 0)
    normal_two, inverse_two = normalise(total)
    final = normal_two * row(10) + row(11)
    final_low[...] = final.astype(BF)

    first = step * MIDDLE_ROWS
    across = (CROPS, MIDDLE_ROWS)
    position = first + lax.broadcasted_iota(jnp.int32, across, 1)
    crop = lax.broadcasted_iota(jnp.int32, across, 0)
    member = ((seg_row[...] == crop) & (position < count[0])).astype(BF)
    high = final.astype(BF)
    rest = final - high.astype(F32)
    mid = rest.astype(BF)
    tiny = (rest - mid.astype(F32)).astype(BF)
    crop_sums[...] += dot(member, high, 1, 0) + (dot(member, mid, 1, 0) + dot(member, tiny, 1, 0))

    position = first + lax.broadcasted_iota(jnp.int32, (MIDDLE_ROWS, 1), 0)
    valid = (position < count[0]).astype(F32)
    cotangent = out_grad[...].astype(F32) * valid
    note(10, column_sum(cotangent * normal_two))
    note(11, column_sum(cotangent))
    grad_two = normalise_back(cotangent, row(10), normal_two, inverse_two)
    grad_out = grad_two.astype(BF)
    grad_ffn_out[...] = grad_out
    note(9, column_sum(grad_out.astype(F32)))
    grad_hidden = grad_two
    for j in range(UP_CHUNKS):
        at = slice(j * D, (j + 1) * D)
        back = (dot(grad_out, chunk(UP_CHUNKS + j), 1, 1) * slope[:, at]).astype(BF)
        grad_pre[:, at] = back
        note(5 + j, column_sum(back.astype(F32)))
        grad_hidden = grad_hidden + dot(back, chunk(j), 1, 1)
    note(3, column_sum(grad_hidden * normal_one))
    note(4, column_sum(grad_hidden))
    grad_one = normalise_back(grad_hidden, row(3), normal_one, inverse_one)
    grad_resid[...] = grad_one
    grad_proj = grad_one.astype(BF)
    grad_attn_out[...] = grad_proj
    note(2, column_sum(grad_proj.astype(F32)))
    grad_mixed[...] = dot(grad_proj, w_out[...], 1, 1).astype(BF)


def middle(count, me, segments, mixed, tokens, out_grad, attn_whole, sources, fetch, vec):
    rows = tokens.shape[0]
    tile = pl.BlockSpec((MIDDLE_ROWS, D), lambda i: (i, 0))
    wide = pl.BlockSpec((MIDDLE_ROWS, FF), lambda i: (i, 0))
    small = pl.BlockSpec((VEC_ROWS, D), lambda i: (0, 0))

    def shape(width, kind):
        return jax.ShapeDtypeStruct((rows, width), kind)

    return pl.pallas_call(
        functools.partial(middle_kernel, fetch, len(sources)),
        grid=(rows // MIDDLE_ROWS,),
        in_specs=[
            pl.BlockSpec(memory_space=pltpu.SMEM),
            pl.BlockSpec(memory_space=pltpu.SMEM),
            pl.BlockSpec((1, MIDDLE_ROWS), lambda i: (0, i)),
            tile,
            tile,
            pl.BlockSpec((D, D), lambda i: (3, 0), pipeline_mode=pl.Buffered(1)),
            small,
        ]
        + [pl.BlockSpec((MIDDLE_ROWS, 2 * HEAD * p), lambda i: (i, 0)) for p in AHEAD_PAIRS]
        + [pl.BlockSpec(memory_space=pl.ANY)] * len(sources),
        out_specs=[tile, tile, wide, wide, tile, tile, tile, tile, small, small],
        out_shape=[
            shape(D, BF),
            shape(D, BF),
            shape(FF, BF),
            shape(FF, BF),
            shape(D, BF),
            shape(D, BF),
            shape(D, BF),
            shape(D, F32),
            jax.ShapeDtypeStruct((VEC_ROWS, D), F32),
            jax.ShapeDtypeStruct((CROPS, D), F32),
        ],
        scratch_shapes=[
            pltpu.VMEM((MIDDLE_ROWS, FF), F32),
            pltpu.VMEM((FFN_ROWS, D), BF),
            pltpu.SemaphoreType.DMA((UP_CHUNKS + 1,)),
        ],
        compiler_params=pltpu.CompilerParams(vmem_limit_bytes=44 * MIB),
        cost_estimate=cost(40),
        name="middle",
    )(count, me, segments.reshape(1, rows), tokens, out_grad, attn_whole, vec, *mixed, *sources)


WIDTH = D // 3


def ffn_terms_kernel(shares, me, hidden, activated, *refs):
    pre, out = refs[:shares], refs[shares : 2 * shares]
    keep, give, hidden_t, block, sem = refs[-5:]
    step = pl.program_id(0)
    slot = lax.rem(step, 2)
    owners, rows = keep.shape[1], keep.shape[2]
    up_rows = rows // UP_CHUNKS
    per_chunk = D // rows

    @pl.when(step == 0)
    def _():
        hidden_t[...] = hidden[...].T

    @pl.when(step >= 2)
    def _():
        pltpu.make_async_copy(block.at[slot], block.at[slot], sem.at[slot]).wait()

    def to(core, y, start):
        @pl.when(core == me[1])
        def _():
            start(keep.at[y])

        @pl.when(core != me[1])
        def _():
            start(give.at[y])

    @pl.when(step < UP_CHUNKS)
    def _():
        right = jnp.concatenate([ref[...] for ref in pre], 1)
        block[slot] = dot(hidden_t[...], right, 1, 0).astype(BF)
        for core in range(2):
            source = block.at[slot, pl.ds(core * (D // 2), D // 2)]
            source = source.reshape(owners, up_rows, block.shape[2])

            def start(target):
                at = pl.ds(pl.multiple_of(step * up_rows, 16), up_rows)
                pltpu.make_async_copy(source, target.at[:, at], sem.at[slot]).start()

            to(core, 0, start)

    @pl.when(step >= UP_CHUNKS)
    def _():
        right = jnp.concatenate([ref[...] for ref in out], 1)
        block[slot] = dot(activated[...], right, 0, 0).astype(BF)
        chunk = step - UP_CHUNKS
        source = block.at[slot].reshape(per_chunk, rows, block.shape[2])

        def start(target):
            at = pl.ds(lax.rem(chunk, 2) * per_chunk, per_chunk)
            pltpu.make_async_copy(source, target.at[at], sem.at[slot]).start()

        to(lax.div(chunk, 2), 1, start)

    @pl.when(step == pl.num_programs(0) - 1)
    def _():
        for s in range(2):
            pltpu.make_async_copy(block.at[s], block.at[s], sem.at[s]).wait()


def ffn_terms(places, me, hidden, activated, grad_pre, grad_out, thirds, after):
    owners = places.wide
    rows = FFN_ROWS // places.count
    shares = len(thirds)
    width = shares * WIDTH
    shape = jax.ShapeDtypeStruct((2, owners, rows, width), BF)

    def pre_spec(third):
        return pl.BlockSpec((ROW, WIDTH), lambda i: (0, 3 * jnp.minimum(i, UP_CHUNKS - 1) + third))

    def out_spec(third):
        return pl.BlockSpec((ROW, WIDTH), lambda i: (0, third))

    def kernel(me_ref, hidden_ref, activated_ref, *refs):
        used = refs[: 2 * shares] + refs[2 * shares + len(after) :]
        ffn_terms_kernel(shares, me_ref, hidden_ref, activated_ref, *used)

    return pl.pallas_call(
        kernel,
        grid=(2 * UP_CHUNKS,),
        in_specs=[
            pl.BlockSpec(memory_space=pltpu.SMEM),
            pl.BlockSpec((ROW, D), lambda i: (0, 0), pipeline_mode=pl.Buffered(1)),
            pl.BlockSpec((ROW, D), lambda i: (0, jnp.maximum(i - UP_CHUNKS, 0))),
        ]
        + [pre_spec(t) for t in thirds]
        + [out_spec(t) for t in thirds]
        + [pl.BlockSpec(memory_space=pl.ANY)] * len(after),
        out_specs=[pl.BlockSpec(memory_space=pl.ANY)] * 2,
        out_shape=[shape] * 2,
        scratch_shapes=[
            pltpu.VMEM((D, ROW), BF),
            pltpu.VMEM((2, D, width), BF),
            pltpu.SemaphoreType.DMA((2,)),
        ],
        compiler_params=pltpu.CompilerParams(vmem_limit_bytes=FFN_VMEM),
        cost_estimate=cost(5 * shares),
        name="ffn_terms",
    )(me, hidden, activated, *([grad_pre] * shares), *([grad_out] * shares), *after)


def attn_terms(places, me, tokens, mixed, grads, grad_proj, vectors, after):
    owners = places.wide
    rows = ATTN_ROWS // places.count
    parts, extra = len(AHEAD_PAIRS), vectors.shape[0]
    shape = jax.ShapeDtypeStruct((2, owners, rows + extra, D), BF)

    def kernel(me_ref, tokens_ref, vectors_ref, proj_ref, *refs):
        mixed_refs, grad_refs, refs = refs[:parts], refs[parts : parts + len(PAIRS)], refs[parts + len(PAIRS) :]
        keep, give, tokens_t, block, below, sem, below_sem = refs[len(after) :]
        step = pl.program_id(0)
        slot = lax.rem(step, 2)

        @pl.when(step == 0)
        def _():
            tokens_t[...] = tokens_ref[...].T
            below[...] = jnp.broadcast_to(vectors_ref[...].astype(BF)[None], below.shape)
            for target in (keep, give):
                for y in range(2):
                    pltpu.make_async_copy(
                        below, target.at[y, :, pl.ds(rows, extra)], below_sem
                    ).start()

        @pl.when(step >= 2)
        def _():
            pltpu.make_async_copy(block.at[slot], block.at[slot], sem.at[slot]).wait()

        @pl.when(step < 3)
        def _():
            right = jnp.concatenate([ref[0] for ref in grad_refs], 1)
            block[slot] = dot(tokens_t[...], right, 1, 0).astype(BF)

        @pl.when(step == 3)
        def _():
            left = jnp.concatenate([ref[...] for ref in mixed_refs], 1)
            block[slot] = dot(left, proj_ref[...], 0, 0).astype(BF)

        source = block.at[slot].reshape(owners, rows, D)
        y, core = lax.div(step, 2), lax.rem(step, 2)

        @pl.when(core == me_ref[1])
        def _():
            pltpu.make_async_copy(source, keep.at[y, :, pl.ds(0, rows)], sem.at[slot]).start()

        @pl.when(core != me_ref[1])
        def _():
            pltpu.make_async_copy(source, give.at[y, :, pl.ds(0, rows)], sem.at[slot]).start()

        @pl.when(step == 3)
        def _():
            for s in range(2):
                pltpu.make_async_copy(block.at[s], block.at[s], sem.at[s]).wait()
            for _ in range(4):
                pltpu.make_async_copy(below, below, below_sem).wait()

    def whole(width):
        return pl.BlockSpec((ROW, width), lambda i: (0, 0), pipeline_mode=pl.Buffered(1))

    return pl.pallas_call(
        kernel,
        grid=(4,),
        in_specs=[
            pl.BlockSpec(memory_space=pltpu.SMEM),
            whole(D),
            pl.BlockSpec((extra, D), lambda i: (0, 0)),
            whole(D),
        ]
        + [whole(2 * HEAD * p) for p in AHEAD_PAIRS]
        + [pl.BlockSpec((1, ROW, 2 * HEAD * p), lambda i: (jnp.minimum(i, 2), 0, 0)) for p in PAIRS]
        + [pl.BlockSpec(memory_space=pl.ANY)] * len(after),
        out_specs=[pl.BlockSpec(memory_space=pl.ANY)] * 2,
        out_shape=[shape] * 2,
        scratch_shapes=[
            pltpu.VMEM((D, ROW), BF),
            pltpu.VMEM((2, D, D), BF),
            pltpu.VMEM((owners, extra, D), BF),
            pltpu.SemaphoreType.DMA((2,)),
            pltpu.SemaphoreType.DMA,
        ],
        compiler_params=pltpu.CompilerParams(vmem_limit_bytes=TERMS_VMEM),
        cost_estimate=cost(6),
        name="attn_terms",
    )(me, tokens, vectors, grad_proj, *mixed, *grads, *after)


def token_grad_kernel(resid, weights, *refs):
    out = refs[-1]
    total = resid[...]
    for m in range(3):
        grad = jnp.concatenate([ref[m] for ref in refs[: len(PAIRS)]], 1)
        total = total + dot(grad, weights[m * D : (m + 1) * D], 1, 1)
    out[...] = total.astype(BF)


def token_gradient(resid, weights, grads, after):
    step = 256
    tile = pl.BlockSpec((step, D), lambda i: (i, 0))
    return pl.pallas_call(
        token_grad_kernel,
        grid=(ROW // step,),
        in_specs=[tile, pl.BlockSpec((3 * D, D), lambda i: (0, 0), pipeline_mode=pl.Buffered(1))]
        + [pl.BlockSpec((3, step, 2 * HEAD * p), lambda i: (0, i, 0)) for p in PAIRS]
        + [pl.BlockSpec(memory_space=pl.ANY)] * len(after),
        out_specs=tile,
        out_shape=jax.ShapeDtypeStruct((ROW, D), BF),
        compiler_params=pltpu.CompilerParams(vmem_limit_bytes=TOKEN_VMEM),
        cost_estimate=cost(2),
        name="token_grad",
    )(resid, weights, *grads, *after)


def adam_update(param, gradient, moment, square, shadow):
    step_float = float(STEP)
    moment_next = MOMENT_DECAY * moment + (1.0 - MOMENT_DECAY) * gradient
    square_next = SQUARE_DECAY * square + (1.0 - SQUARE_DECAY) * gradient * gradient
    moment_hat = moment_next / (1.0 - MOMENT_DECAY**step_float)
    square_hat = square_next / (1.0 - SQUARE_DECAY**step_float)
    change = -LEARN_RATE * (
        moment_hat / (jnp.sqrt(square_hat) + ADAM_EPSILON) + WEIGHT_DECAY * param
    )
    updated = param + change
    drift = (1.0 - SHADOW_RATE) * (updated - shadow)
    return (change, moment_next, square_next, drift)


def contract_rows(left, right):
    return dot(left, right, 0, 0)


def on_device(
    places,
    tokens,
    segments,
    counts,
    out_grad,
    attn_param,
    attn_moment,
    attn_square,
    attn_shadow,
    ffn_param,
    ffn_moment,
    ffn_square,
    ffn_shadow,
):
    assert counts.shape[0] == 1 and tokens.shape[0] == ROW
    number = places.count
    here = places.here()
    place_list = jnp.stack([here[a] for a in ("y", "c", "z", "x")]).astype(jnp.int32)
    me = lax.axis_index("dp") * places.wide + lax.axis_index("wide")
    staged = places.staged()
    attn_rows, ffn_rows = ATTN_ROWS // number, FFN_ROWS // number
    up_rows = ffn_rows // UP_CHUNKS
    holds_up = me < number // 2

    last = me == number - 1
    ends = jnp.concatenate([attn_param[-ATTN_TAIL:], ffn_param[-FFN_TAIL:]]).astype(BF)
    ends = jnp.where(last, ends, jnp.zeros_like(ends))
    if staged:
        digits = [lax.rem(lax.shift_right_logical(counts[0], 3 * i), 8) for i in range(4)]
        count_row = jnp.concatenate([jnp.stack(digits).astype(BF), jnp.zeros((D - 4,), BF)])
        filler = jnp.zeros(((VEC_ROWS - COUNT_ROW - 1) * D,), BF)
        extra = jnp.concatenate([ends, count_row, filler]).reshape(VEC_ROWS, D)
        attn_own = to_rows(places, me, attn_param, ATTN_ROWS, ATTN_TAIL).astype(BF)
        attn_set = Gathered(places, attn_rows)
        blocks = attn_set.start_z(jnp.concatenate([attn_own, extra], 0))
        ffn_own = to_rows(places, me, order(ffn_param, blocks[1]), FFN_ROWS, FFN_TAIL).astype(BF)
        by_chunk = ffn_own.reshape(up_rows, UP_CHUNKS, D).transpose(1, 0, 2).reshape(ffn_rows, D)
        ffn_own = jnp.where(holds_up, by_chunk, ffn_own)
        column = attn_set.join_z(here, blocks)
        half_rows = ffn_rows // 2
        ffn_set = Gathered(places, half_rows)
        blocks = ffn_set.start_z(order(ffn_own[:half_rows], column))
        near = [ffn_set.join_parts(place_list, [blocks])]
        plane = order(attn_set.along_first(column), *blocks)
        blocks = ffn_set.start_z(order(ffn_own[half_rows:], plane, near[0]))
        aside = [places.send(near[0], "xy", 1)]
        crossed = [places.send(near[0], "c", 1)]
        groups = [plane]
        groups += [order(g, aside[0], *blocks) for g in attn_set.along_second(plane)]
        attn_groups = groups + attn_set.from_core(groups)
        near.append(ffn_set.join_parts(place_list, [blocks]))
        aside.append(places.send(near[1], "xy", 1))
        across = [places.send(near[0], "yx", 1)]
        corner = [places.send(aside[0], "yx", 1)]
        query, key, value, vec, attn_whole = project(
            tokens, place_list, attn_set, attn_groups, [aside[0], near[1], crossed[0]]
        )
        token_total = sum(vec[COUNT_ROW, i] * float(8**i) for i in range(4))
        aside = [order(a, query) for a in aside]
        near[1] = order(near[1], query)
        crossed += [places.send(near[1], "c", 1)] + [places.send(a, "c", 1) for a in aside]
        across.append(places.send(near[1], "yx", 1))
        corner.append(places.send(aside[1], "yx", 1))
        extent = places.size
        per_half = UP_CHUNKS // 2
        piece = (extent["z"], per_half, up_rows, D)
        half = extent["y"] // 2

        def fetch(place, refs, weights, sem):
            side = (half, 2, extent["z"], extent["x"])
            up = weights.at[pl.ds(0, FF)].reshape(*((UP_CHUNKS,) + side + (up_rows, D)))
            down = weights.at[pl.ds(FF, FF)].reshape(*(side + (UP_CHUNKS, up_rows, D)))
            ways = [(far, i, j) for far in range(2) for i in range(2) for j in range(2)]
            for i, ref in enumerate(refs):
                h, way = divmod(i, len(ways))
                y, core, x = ffn_set.place(place, *ways[way])

                @pl.when(y < half)
                def _():
                    for part in range(per_half):
                        chunk = h * per_half + part
                        pltpu.make_async_copy(
                            ref.at[:, part], up.at[chunk, y, core, :, x], sem.at[chunk]
                        ).start()

                @pl.when(y >= half)
                def _():
                    chunks = pl.ds(h * per_half, per_half)
                    pltpu.make_async_copy(
                        ref, down.at[y - half, core, :, x, chunks], sem.at[UP_CHUNKS]
                    ).start()

    else:
        token_total = lax.psum(counts[0].astype(F32), AXES)
        vec = lax.psum(ends.astype(F32), AXES).reshape(COUNT_ROW, D)
        vec = jnp.concatenate([vec, jnp.zeros((VEC_ROWS - COUNT_ROW, D), F32)], 0)
        flat = lax.all_gather(attn_param.astype(BF), AXES, axis=0, tiled=True)
        attn_whole = flat[: ATTN_ROWS * D].reshape(ATTN_ROWS, D)
        flat = lax.all_gather(ffn_param.astype(BF), AXES, axis=0, tiled=True)
        w_up = flat[: FF * D].reshape(D, UP_CHUNKS, D).transpose(1, 0, 2).reshape(FF, D)
        w_down = flat[FF * D : FFN_ROWS * D].reshape(FF, D)
        sources = [w_up, w_down]

        def fetch(place, refs, weights, sem):
            w_up, w_down = refs
            for j in range(UP_CHUNKS):
                rows = pl.ds(j * D, D)
                pltpu.make_async_copy(w_up.at[rows], weights.at[rows], sem.at[j]).start()
            down = weights.at[pl.ds(FF, FF)]
            pltpu.make_async_copy(w_down, down, sem.at[UP_CHUNKS]).start()

        query, key, value = project_whole(tokens, attn_whole, vec)

    ahead = []
    for i, pairs in enumerate(AHEAD_PAIRS):
        after = [aside[1]] if staged and i == 0 else []
        first = sum(AHEAD_PAIRS[:i])
        ahead.append(attend(query, key, value, segments, counts, first, pairs, after))
    mixed = [a[0] for a in ahead]
    log_total = jnp.concatenate([a[1] for a in ahead], 0)
    if staged:
        sources = []
        for h in range(2):
            across[h], corner[h] = order(across[h], mixed[h]), order(corner[h], mixed[h])
            mine = [near[h], across[h], aside[h], corner[h]]
            theirs = [crossed[h], places.send(across[h], "c", 1)]
            theirs += [crossed[2 + h], places.send(corner[h], "c", 1)]
            sources += [a.reshape(piece) for a in mine + theirs]
    (
        final_low,
        hidden_low,
        activated,
        grad_pre,
        grad_ffn_out,
        grad_attn_out,
        grad_mixed,
        grad_resid,
        vec_grad,
        crop_sums,
    ) = middle(
        counts,
        place_list,
        segments,
        mixed,
        tokens,
        out_grad,
        attn_whole,
        sources,
        fetch,
        vec,
    )
    is_valid = jnp.arange(ROW, dtype=jnp.int32) < counts[0]
    member = (segments[None, :] == jnp.arange(CROPS, dtype=jnp.int32)[:, None]) & is_valid[None, :]
    crop_sizes = jnp.sum(member.astype(F32), axis=1)
    pooled = crop_sums / jnp.maximum(crop_sizes, 1.0)[:, None]

    def back(i, after, micros):
        return attend_back(
            query,
            key,
            value,
            grad_mixed,
            log_total,
            segments,
            counts,
            sum(PAIRS[:i]),
            PAIRS[i],
            after,
            micros,
        )

    if staged:
        ffn_sums, attn_sums = Scattered(places, place_list, 1.2), Scattered(places, place_list, 0.5)

        def spread(terms):
            return terms.reshape(2, extent["z"], extent["x"], *terms.shape[2:])

        def ffn_side(thirds, after):
            operands = (hidden_low, activated, grad_pre, grad_ffn_out)
            terms = ffn_terms(places, place_list, *operands, thirds, after)
            return [spread(t) for t in terms]

        keep_a, give_a = ffn_side([0, 1, 2], [])
        core_a = ffn_sums.core(give_a)
        back_0 = back(0, [give_a], 12)
        own_a, cut_a = ffn_sums.first(keep_a, order(core_a, back_0[0]))
        first_a = ffn_sums.send(cut_a)
        back_1 = back(1, [cut_a], 15)
        vectors = jnp.concatenate([back_0[1], back_1[1]], 1)[:2]
        vec_grad = jnp.concatenate([vectors, vec_grad[2:]], 0)
        grads = [back_0[0], back_1[0]]
        operands = (tokens, mixed, grads, grad_attn_out, vec_grad)
        terms = attn_terms(places, place_list, *operands, [])
        keep_c, give_c = [spread(t) for t in terms]
        core_c = attn_sums.core(give_c)
        own_a, cut_a = ffn_sums.second(own_a, order(first_a, give_c))
        second_a = ffn_sums.send_second(cut_a)
        token_grad = token_gradient(grad_resid, attn_whole, grads, [give_c, cut_a])
        own_c, cut_c = attn_sums.first(keep_c, order(core_c, token_grad))
        own_a, cuts_a = ffn_sums.along_z(own_a, order(second_a, cut_c))
        up_z_a = ffn_sums.send_z(cuts_a)
        first_c = attn_sums.send(cut_c, *cuts_a)
        own_c, cut_c = attn_sums.second(own_c, order(first_c, up_z_a[1]))
        second_c = attn_sums.send_second(cut_c)
        own_c, cuts_c = attn_sums.along_z(own_c, second_c)
        up_z_c = attn_sums.send_z(cuts_c)
        ffn_block = ffn_sums.result(own_a, up_z_a)
        block_c = attn_sums.result(own_c, up_z_c)
        attn_block, vec_sum = block_c[:attn_rows], block_c[attn_rows:]
        by_row = ffn_block.reshape(UP_CHUNKS, up_rows, D).transpose(1, 0, 2).reshape(ffn_rows, D)
        ffn_block = jnp.where(holds_up, by_row, ffn_block)
        ffn_summed = to_flat(places, me, ffn_block, vec_sum[5:12], FFN_TAIL)
        attn_summed = to_flat(places, me, attn_block, vec_sum[:5], ATTN_TAIL)
    else:
        backs = [back(i, [], 12) for i in range(len(PAIRS))]
        grads = [b[0] for b in backs]
        token_grad = token_gradient(grad_resid, attn_whole, grads, [])
        grads = jnp.concatenate(grads, 2)
        mats = [contract_rows(tokens, grads[i]) for i in range(3)]
        mats.append(contract_rows(jnp.concatenate(mixed, 1), grad_attn_out))
        vectors = jnp.concatenate([b[1] for b in backs], 1)[:2]
        vec_grad = jnp.concatenate([vectors, vec_grad[2:]], 0)
        attn_full = jnp.concatenate([g.reshape(-1) for g in mats + [vec_grad[:5]]])
        up = contract_rows(hidden_low, grad_pre)
        down = contract_rows(activated, grad_ffn_out)
        ffn_full = jnp.concatenate([g.reshape(-1) for g in (up, down, vec_grad[5:12])])
        attn_summed = lax.psum_scatter(attn_full, AXES, scatter_dimension=0, tiled=True)
        ffn_summed = lax.psum_scatter(ffn_full, AXES, scatter_dimension=0, tiled=True)
    attn_grad = attn_summed / token_total
    ffn_grad = ffn_summed / token_total
    attn_change, moment_attn, square_attn, drift_attn = adam_update(
        attn_param, attn_grad, attn_moment, attn_square, attn_shadow
    )
    ffn_change, moment_ffn, square_ffn, drift_ffn = adam_update(
        ffn_param, ffn_grad, ffn_moment, ffn_square, ffn_shadow
    )
    return (
        final_low,
        pooled,
        token_grad,
        attn_grad,
        ffn_grad,
        attn_change,
        ffn_change,
        moment_attn,
        moment_ffn,
        square_attn,
        square_ffn,
        drift_attn,
        drift_ffn,
    )


def solution(mesh):
    rows, flat = P(AXES, None), P(AXES)
    return jax.shard_map(
        functools.partial(on_device, Places(mesh)),
        mesh=mesh,
        in_specs=(rows, flat, flat, rows) + (flat,) * 8,
        out_specs=(rows, rows, rows) + (flat,) * 10,
        check_vma=False,
    )
```

profile of v0, /device:TPU:8, one launch (start us, length us, event | category | flops | bytes accessed | tf_op | source)
XLA Modules:
  0.0 311.7 jit_solution(12365914688732636617)
XLA Ops:
  1.5 3.4 %collective-permute-start = (bf16[3840]{0:T(1024)(128)(2,1)S(1)}, bf16[3840]{0:T(1024)(128)(2,1)S(1)}, u32[]{:S(2)}, u32[]{:S(2)}) collective-permute-start(bf16[3840]{0:T(1024)(128)(2,1)S(1)} %slice.161), channel_id=1, source_target_pairs={{0,1},{1,2},{2,3},{3,4},{4,5},{5,6},{6,7},{7,8},{8,9},{9,10},{10,1... | collective-permute-start | bytes 23048 | tf_op jit(solution)/shard_map/ppermute | solution.py:290
  11.4 2.6 collective-permute-start.2
  14.0 2.2 collective-permute-done.1
  16.3 9.0 %collective-permute-start.5 = (bf16[5376]{0:T(1024)(128)(2,1)S(1)}, bf16[5376]{0:T(1024)(128)(2,1)S(1)}, u32[]{:S(2)}, u32[]{:S(2)}) collective-permute-start(bf16[5376]{0:T(1024)(128)(2,1)S(1)} %slice.100), channel_id=1, source_target_pairs={{0,1},{1,2},{2,3},{3,4},{4,5},{5,6},{6,7},{7,8},{8,9},{9,10},{10,1... | collective-permute-start | bytes 32264 | tf_op jit(solution)/shard_map/ppermute | solution.py:290
  27.5 2.5 collective-permute-start.6
  30.0 2.6 collective-permute-start.7
  33.2 2.5 collective-permute-done.4
  35.8 4.5 %collective-permute-done.6.refs_1_ = bf16[96,768]{1,0:T(8,128)(2,1)S(1)} collective-permute-done((bf16[96,768]{1,0:T(8,128)(2,1)S(1)}, bf16[96,768]{1,0:T(8,128)(2,1)S(1)}, u32[]{:S(2)}, u32[]{:S(2)}) %collective-permute-start.6) | collective-permute-done | bytes 147488 | tf_op jit(solution)/shard_map/ppermute | solution.py:84
  46.7 2.4 collective-permute-start.10
  52.3 11.2 %collective-permute-done.10.refs_4_ = bf16[384,768]{1,0:T(8,128)(2,1)S(1)} collective-permute-done((bf16[384,768]{1,0:T(8,128)(2,1)}, bf16[384,768]{1,0:T(8,128)(2,1)S(1)}, u32[]{:S(2)}, u32[]{:S(2)}) %collective-permute-start.10) | collective-permute-done | bytes 589856 | tf_op jit(solution)/shard_map/ppermute | solution.py:84
  64.2 2.8 collective-permute-done.9.refs_1_
  73.9 7.5 %project.1 = (bf16[1024,768]{1,0:T(8,128)(2,1)S(1)}, bf16[1024,768]{1,0:T(8,128)(2,1)S(1)}, bf16[1024,768]{1,0:T(8,128)(2,1)S(1)}, f32[16,768]{1,0:T(8,128)S(1)}, bf16[3072,768]{1,0:T(8,128)(2,1)S(1)}) custom-call(s32[4]{0:T(128)S(1)} %pad_add_fusion.me_ref.me, bf16[1024,768]{1,0:T(8,128)(2,1)S(1)} %copy-done.6, ...), custom_call_target="tpu_custom_call" | custom-call | flops 8800000000 | bytes 1048576 | tf_op jit(solution)/shard_map/project/pallas_call | solution.py:357
  82.5 6.0 %collective-permute-done.17.refs_0_ = bf16[384,768]{1,0:T(8,128)(2,1)S(1)} collective-permute-done((bf16[384,768]{1,0:T(8,128)(2,1)S(1)}, bf16[384,768]{1,0:T(8,128)(2,1)S(1)}, u32[]{:S(2)}, u32[]{:S(2)}) %collective-permute-start.17) | collective-permute-done | bytes 589856 | tf_op jit(solution)/shard_map/ppermute | solution.py:84
  89.1 8.6 %attend.3 = (bf16[1024,256]{1,0:T(8,128)(2,1)S(1)}, f32[2,8,1024]{2,1,0:T(8,128)S(1)}) custom-call(s32[1]{0:T(128)} %copy.47.count, s32[1024,1]{1,0:T(8,128)S(1)} %copy.34.seg_column, s32[1,1024]{1,0:T(1,128)S(1)} %bitcast.66, bf16[1024,768]{1,0:T(8,128)(2,1)S(1)} %get-tuple-element.83.query, bf16[1024,768]{1,0:T(8,128)(2,1)S(1)} %get-tuple-element.84.key, ...), custom_call_target="tpu_custom_call" | custom-call | flops 9166666752 | bytes 1048576 | tf_op jit(solution)/shard_map/attend/pallas_call | solution.py:460
  98.3 8.6 %attend.4 = (bf16[1024,256]{1,0:T(8,128)(2,1)S(1)}, f32[2,8,1024]{2,1,0:T(8,128)S(1)}) custom-call(s32[1]{0:T(128)} %copy.47.count, s32[1024,1]{1,0:T(8,128)S(1)} %copy.34.seg_column, s32[1,1024]{1,0:T(1,128)S(1)} %bitcast.67, bf16[1024,768]{1,0:T(8,128)(2,1)S(1)} %get-tuple-element.83.query, bf16[1024,768]{1,0:T(8,128)(2,1)S(1)} %get-tuple-element.84.key, ...), custom_call_target="tpu_custom_call" | custom-call | flops 9166666752 | bytes 1048576 | tf_op jit(solution)/shard_map/attend/pallas_call | solution.py:460
  108.1 9.0 %attend.5 = (bf16[1024,256]{1,0:T(8,128)(2,1)S(1)}, f32[2,8,1024]{2,1,0:T(8,128)S(1)}) custom-call(s32[1]{0:T(128)} %copy.47.count, s32[1024,1]{1,0:T(8,128)S(1)} %copy.34.seg_column, s32[1,1024]{1,0:T(1,128)S(1)} %bitcast.68, bf16[1024,768]{1,0:T(8,128)(2,1)S(1)} %get-tuple-element.83.query, bf16[1024,768]{1,0:T(8,128)(2,1)S(1)} %get-tuple-element.84.key, ...), custom_call_target="tpu_custom_call" | custom-call | flops 9166666752 | bytes 1048576 | tf_op jit(solution)/shard_map/attend/pallas_call | solution.py:460
  118.3 41.0 %middle.1 = (bf16[1024,768]{1,0:T(8,128)(2,1)}, bf16[1024,768]{1,0:T(8,128)(2,1)}, bf16[1024,3072]{1,0:T(8,128)(2,1)}, bf16[1024,3072]{1,0:T(8,128)(2,1)}, bf16[...) custom-call(s32[1]{0:T(128)} %copy.47.count, ...), custom_call_target="tpu_custom_call" | custom-call | flops 44000002048 | bytes 1048576 | tf_op jit(solution)/shard_map/middle/pallas_call | solution.py:702
  159.4 17.5 %ffn_terms.1 = (bf16[2,8,192,768]{3,2,1,0:T(8,128)(2,1)}, bf16[2,8,192,768]{3,2,1,0:T(8,128)(2,1)}) custom-call(s32[4]{0:T(128)} %copy-done.3, bf16[1024,768]{1,0:T(8,128)(2,1)} %get-tuple-element.103.hidden_ref, bf16[1024,3072]{1,0:T(8,128)(2,1)} %get-tuple-element.104.activated_ref, bf16[1024,3072]{1,0:T(8,128)(2,1)} %get-tuple-element.105.refs_0_.refs_1_.refs_2_, ...), custom_call_target="tpu_custom_call" | custom-call | flops 16499999744 | bytes 1048576 | tf_op jit(solution)/shard_map/ffn_terms/pallas_call | solution.py:819
  177.2 2.3 copy-done.5
  180.9 11.5 %attend_back.2 = (bf16[3,1024,256]{2,1,0:T(8,128)(2,1)S(1)}, f32[8,256]{1,0:T(8,128)S(1)}) custom-call(s32[1]{0:T(128)} %copy.47.count, s32[1024,1]{1,0:T(8,128)S(1)} %copy.34.seg_column, s32[1,1024]{1,0:T(1,128)S(1)} %bitcast.70, bf16[1024,768]{1,0:T(8,128)(2,1)S(1)} %copy-done.13, bf16[1024,768]{1,0:T(8,128)(2,1)S(1)} %copy-done.15, ...), custom_call_target="tpu_custom_call" | custom-call | flops 13200000000 | bytes 1048576 | tf_op jit(solution)/shard_map/attend_back/pallas_call | solution.py:519
  192.5 3.0 add_routed.6
  197.6 22.3 %attend_back.3 = (bf16[3,1024,512]{2,1,0:T(8,128)(2,1)S(1)}, f32[8,512]{1,0:T(8,128)S(1)}) custom-call(s32[1]{0:T(128)} %copy.47.count, s32[1024,1]{1,0:T(8,128)S(1)} %copy.34.seg_column, s32[1,1024]{1,0:T(1,128)S(1)} %bitcast.71, bf16[1024,768]{1,0:T(8,128)(2,1)S(1)} %copy-done.13, bf16[1024,768]{1,0:T(8,128)(2,1)S(1)} %copy-done.16, ...), custom_call_target="tpu_custom_call" | custom-call | flops 16499999744 | bytes 1048576 | tf_op jit(solution)/shard_map/attend_back/pallas_call | solution.py:519
  220.0 7.5 %attn_terms.1 = (bf16[2,8,112,768]{3,2,1,0:T(8,128)(2,1)S(1)}, bf16[2,8,112,768]{3,2,1,0:T(8,128)(2,1)S(1)}) custom-call(s32[4]{0:T(128)S(1)} %copy-done.4, bf16[1024,768]{1,0:T(8,128)(2,1)S(1)} %copy-done.7, f32[16,768]{1,0:T(8,128)S(1)} %fusion.7.vectors_ref, bf16[1024,768]{1,0:T(8,128)(2,1)S(1)} %copy-done.11, bf16[1024,256]{1,0:T(8,128)(2,1)S(1)} %copy-done.21, ...), custom_call_target="tpu_custom_call" | custom-call | flops 6600000000 | bytes 1048576 | tf_op jit(solution)/shard_map/attn_terms/pallas_call | solution.py:900
  230.9 5.6 %token_grad.1 = bf16[1024,768]{1,0:T(8,128)(2,1)} custom-call(f32[1024,768]{1,0:T(8,128)S(1)} %copy-done.1, bf16[3072,768]{1,0:T(8,128)(2,1)S(1)} %bitcast.62, bf16[3,1024,256]{2,1,0:T(8,128)(2,1)S(1)} %get-tuple-element.108.refs_3_.refs_0_, bf16[3,1024,512]{2,1,0:T(8,128)(2,1)S(1)} %get-tuple-element.112.refs_4_.refs_1_, ...), custom_call_target="tpu_custom_call" | custom-call | flops 2200000000 | bytes 1048576 | tf_op jit(solution)/shard_map/token_grad/pallas_call | solution.py:939
  238.7 6.8 %collective-permute-done.32.refs_1_.refs_3_.refs_5_.refs_7_ = bf16[4,192,768]{2,1,0:T(8,128)(2,1)S(1)} collective-permute-done((bf16[4,192,768]{2,1,0:T(8,128)(2,1)S(1)}, bf16[4,192,768]{2,1,0:T(8,128)(2,1)S(1)}, u32[]{:S(2)}, u32[]{:S(2)}) %collective-permute-start.32) | collective-permute-done | bytes 1179680 | tf_op jit(solution)/shard_map/ppermute | solution.py:84
  249.1 10.9 %collective-permute-done.34 = bf16[1,192,768]{2,1,0:T(8,128)(2,1)S(1)} collective-permute-done((bf16[1,192,768]{2,1,0:T(8,128)(2,1)S(1)}, bf16[1,192,768]{2,1,0:T(8,128)(2,1)S(1)}, u32[]{:S(2)}, u32[]{:S(2)}) %collective-permute-start.34) | collective-permute-done | bytes 294944 | tf_op jit(solution)/shard_map/ppermute | solution.py:84
  260.0 4.7 %collective-permute-done.33.refs_1_.refs_3_ = bf16[4,2,112,768]{3,2,1,0:T(8,128)(2,1)S(1)} collective-permute-done((bf16[4,2,112,768]{3,2,1,0:T(8,128)(2,1)S(1)}, bf16[4,2,112,768]{3,2,1,0:T(8,128)(2,1)S(1)}, u32[]{:S(2)}, u32[]{:S(2)}) %collective-permute-start.33) | collective-permute-done | bytes 1376288 | tf_op jit(solution)/shard_map/ppermute | solution.py:84
  273.0 7.4 %collective-permute-done.41 = bf16[1,192,768]{2,1,0:T(8,128)(2,1)S(1)} collective-permute-done((bf16[1,192,768]{2,1,0:T(8,128)(2,1)S(1)}, bf16[1,192,768]{2,1,0:T(8,128)(2,1)S(1)}, u32[]{:S(2)}, u32[]{:S(2)}) %collective-permute-start.41) | collective-permute-done | bytes 294944 | tf_op jit(solution)/shard_map/ppermute | solution.py:84
  288.2 3.4 %collective-permute-start.42 = (f32[7,768]{1,0:T(8,128)S(1)}, f32[7,768]{1,0:T(8,128)S(1)}, u32[]{:S(2)}, u32[]{:S(2)}) collective-permute-start(f32[7,768]{1,0:T(8,128)S(1)} %slice.133), channel_id=1, source_target_pairs={{1,0},{2,1},{3,2},{4,3},{5,4},{6,5},{7,6},{8,7},{9,8},{10,9},{11,1... | collective-permute-start | bytes 64520 | tf_op jit(solution)/shard_map/ppermute | solution.py:298
  291.7 7.1 %collective-permute-done.38 = bf16[1,112,768]{2,1,0:T(8,128)(2,1)S(1)} collective-permute-done((bf16[1,112,768]{2,1,0:T(8,128)(2,1)S(1)}, bf16[1,112,768]{2,1,0:T(8,128)(2,1)S(1)}, u32[]{:S(2)}, u32[]{:S(2)}) %collective-permute-start.38) | collective-permute-done | bytes 172064 | tf_op jit(solution)/shard_map/ppermute | solution.py:84
  299.2 6.0 %collective-permute-start.39 = (f32[5,768]{1,0:T(8,128)S(1)}, f32[5,768]{1,0:T(8,128)S(1)}, u32[]{:S(2)}, u32[]{:S(2)}) collective-permute-start(f32[5,768]{1,0:T(8,128)S(1)} %slice_bitcast_fusion.2), channel_id=1, source_target_pairs={{1,0},{2,1},{3,2},{4,3},{5,4},{6,5},{7,6},{8,7},{9,8},{10,9},{11,1... | collective-permute-start | bytes 46088 | tf_op jit(solution)/shard_map/ppermute | solution.py:298
  305.3 3.5 %subtract_multiply_fusion = (f32[147624]{0:T(1024)}, f32[147624]{0:T(1024)}, f32[147624]{0:T(1024)}, f32[147624]{0:T(1024)}, f32[147624]{0:T(1024)}) fusion(f32[147624]{0:T(1024)S(1)} %copy-done.32, f32[147624]{0:T(1024)S(1)} %copy-done.29, f32[147624]{0:T(1024)} %param.21, f32[147624]{0:T(1024)} %param.22, f32[]{:T(128)} %bitcast.38, ...), kind=kLoop, calls=%fused_computation.7 | loop fusion | flops 2657232 | bytes 5904968 | tf_op jit(solution)/shard_map/mul | solution.py:963
  (210 shorter events, 60.6 us)
Async XLA Ops:
  11.0 14.3 %collective-permute-start.3 = (bf16[112,768]{1,0:T(8,128)(2,1)S(1)}, bf16[112,768]{1,0:T(8,128)(2,1)S(1)}, u32[]{:S(2)}, u32[]{:S(2)}) collective-permute-start(bf16[112,768]{1,0:T(8,128)(2,1)S(1)} %constant_dynamic-update-slice_fusion), channel_id=1, source_target_pairs={{0,6},{1,7},{2,0},{3,1},{4,2},{5,3},{6,4},{7,5},{8,14},{9,15},{10,... | collective-permute-start | bytes 516104 | tf_op jit(solution)/shard_map/ppermute | solution.py:84
  11.4 13.9 %collective-permute-start.2 = (bf16[112,768]{1,0:T(8,128)(2,1)S(1)}, bf16[112,768]{1,0:T(8,128)(2,1)S(1)}, u32[]{:S(2)}, u32[]{:S(2)}) collective-permute-start(bf16[112,768]{1,0:T(8,128)(2,1)S(1)} %constant_dynamic-update-slice_fusion), channel_id=1, source_target_pairs={{0,4},{1,5},{2,6},{3,7},{4,0},{5,1},{6,2},{7,3},{8,12},{9,13},{10,... | collective-permute-start | bytes 516104 | tf_op jit(solution)/shard_map/ppermute | solution.py:84
  16.3 10.4 %collective-permute-start.5 = (bf16[5376]{0:T(1024)(128)(2,1)S(1)}, bf16[5376]{0:T(1024)(128)(2,1)S(1)}, u32[]{:S(2)}, u32[]{:S(2)}) collective-permute-start(bf16[5376]{0:T(1024)(128)(2,1)S(1)} %slice.100), channel_id=1, source_target_pairs={{0,1},{1,2},{2,3},{3,4},{4,5},{5,6},{6,7},{7,8},{8,9},{9,10},{10,1... | collective-permute-start | bytes 32264 | tf_op jit(solution)/shard_map/ppermute | solution.py:290
  25.5 10.2 %collective-permute-start.4 = (bf16[400,768]{1,0:T(8,128)(2,1)S(1)}, bf16[400,768]{1,0:T(8,128)(2,1)S(1)}, u32[]{:S(2)}, u32[]{:S(2)}) collective-permute-start(bf16[400,768]{1,0:T(8,128)(2,1)S(1)} %pad_maximum_fusion.1), channel_id=1, source_target_pairs={{0,1},{1,0},{2,3},{3,2},{4,5},{5,4},{6,7},{7,6},{8,24},{9,25},{10,... | collective-permute-start | bytes 1843208 | tf_op jit(solution)/shard_map/ppermute | solution.py:84
  27.5 12.8 %collective-permute-start.6 = (bf16[96,768]{1,0:T(8,128)(2,1)S(1)}, bf16[96,768]{1,0:T(8,128)(2,1)S(1)}, u32[]{:S(2)}, u32[]{:S(2)}) collective-permute-start(bf16[96,768]{1,0:T(8,128)(2,1)S(1)} %get-tuple-element.77.refs_0_), channel_id=1, source_target_pairs={{0,2},{1,3},{2,4},{3,5},{4,6},{5,7},{6,0},{7,1},{8,10},{9,11},{10,... | collective-permute-start | bytes 442376 | tf_op jit(solution)/shard_map/ppermute | solution.py:84
  30.0 12.1 %collective-permute-start.7 = (bf16[96,768]{1,0:T(8,128)(2,1)S(1)}, bf16[96,768]{1,0:T(8,128)(2,1)S(1)}, u32[]{:S(2)}, u32[]{:S(2)}) collective-permute-start(bf16[96,768]{1,0:T(8,128)(2,1)S(1)} %get-tuple-element.77.refs_0_), channel_id=1, source_target_pairs={{0,4},{1,5},{2,6},{3,7},{4,0},{5,1},{6,2},{7,3},{8,12},{9,13},{10,... | collective-permute-start | bytes 442376 | tf_op jit(solution)/shard_map/ppermute | solution.py:84
  32.6 11.5 %collective-permute-start.8 = (bf16[96,768]{1,0:T(8,128)(2,1)S(1)}, bf16[96,768]{1,0:T(8,128)(2,1)S(1)}, u32[]{:S(2)}, u32[]{:S(2)}) collective-permute-start(bf16[96,768]{1,0:T(8,128)(2,1)S(1)} %get-tuple-element.77.refs_0_), channel_id=1, source_target_pairs={{0,6},{1,7},{2,0},{3,1},{4,2},{5,3},{6,4},{7,5},{8,14},{9,15},{10,... | collective-permute-start | bytes 442376 | tf_op jit(solution)/shard_map/ppermute | solution.py:84
  44.1 22.9 %collective-permute-start.9 = (bf16[784,768]{1,0:T(8,128)(2,1)S(1)}, bf16[784,768]{1,0:T(8,128)(2,1)}, u32[]{:S(2)}, u32[]{:S(2)}) collective-permute-start(bf16[784,768]{1,0:T(8,128)(2,1)S(1)} %pad_maximum_fusion.refs_0_), channel_id=1, source_target_pairs={{0,16},{1,17},{2,18},{3,19},{4,20},{5,21},{6,22},{7,23},{8,9},{9,8... | collective-permute-start | bytes 3612680 | tf_op jit(solution)/shard_map/ppermute | solution.py:84
  46.7 16.9 %collective-permute-start.10 = (bf16[384,768]{1,0:T(8,128)(2,1)}, bf16[384,768]{1,0:T(8,128)(2,1)S(1)}, u32[]{:S(2)}, u32[]{:S(2)}) collective-permute-start(bf16[384,768]{1,0:T(8,128)(2,1)} %bitcast.12), channel_id=1, source_target_pairs={{0,1},{1,0},{2,3},{3,2},{4,5},{5,4},{6,7},{7,6},{8,24},{9,25},{10,... | collective-permute-start | bytes 1769480 | tf_op jit(solution)/shard_map/ppermute | solution.py:84
  49.1 14.5 %collective-permute-start.11 = (bf16[96,768]{1,0:T(8,128)(2,1)S(1)}, bf16[96,768]{1,0:T(8,128)(2,1)S(1)}, u32[]{:S(2)}, u32[]{:S(2)}) collective-permute-start(bf16[96,768]{1,0:T(8,128)(2,1)S(1)} %get-tuple-element.79.refs_0_), channel_id=1, source_target_pairs={{0,2},{1,3},{2,4},{3,5},{4,6},{5,7},{6,0},{7,1},{8,10},{9,11},{10,... | collective-permute-start | bytes 442376 | tf_op jit(solution)/shard_map/ppermute | solution.py:84
  49.1 14.5 %collective-permute-start.12 = (bf16[96,768]{1,0:T(8,128)(2,1)S(1)}, bf16[96,768]{1,0:T(8,128)(2,1)S(1)}, u32[]{:S(2)}, u32[]{:S(2)}) collective-permute-start(bf16[96,768]{1,0:T(8,128)(2,1)S(1)} %get-tuple-element.79.refs_0_), channel_id=1, source_target_pairs={{0,4},{1,5},{2,6},{3,7},{4,0},{5,1},{6,2},{7,3},{8,12},{9,13},{10,... | collective-permute-start | bytes 442376 | tf_op jit(solution)/shard_map/ppermute | solution.py:84
  50.7 12.8 %collective-permute-start.13 = (bf16[96,768]{1,0:T(8,128)(2,1)S(1)}, bf16[96,768]{1,0:T(8,128)(2,1)S(1)}, u32[]{:S(2)}, u32[]{:S(2)}) collective-permute-start(bf16[96,768]{1,0:T(8,128)(2,1)S(1)} %get-tuple-element.79.refs_0_), channel_id=1, source_target_pairs={{0,6},{1,7},{2,0},{3,1},{4,2},{5,3},{6,4},{7,5},{8,14},{9,15},{10,... | collective-permute-start | bytes 442376 | tf_op jit(solution)/shard_map/ppermute | solution.py:84
  63.5 10.4 %collective-permute-start.14 = (bf16[784,768]{1,0:T(8,128)(2,1)S(1)}, bf16[784,768]{1,0:T(8,128)(2,1)}, u32[]{:S(2)}, u32[]{:S(2)}) collective-permute-start(bf16[784,768]{1,0:T(8,128)(2,1)S(1)} %pad_maximum_fusion.refs_0_), channel_id=1, source_target_pairs={{0,8},{1,9},{2,10},{3,11},{4,12},{5,13},{6,14},{7,15},{8,0},{9,1},... | collective-permute-start | bytes 3612680 | tf_op jit(solution)/shard_map/ppermute | solution.py:84
  67.8 30.0 %collective-permute-start.18 = (bf16[384,768]{1,0:T(8,128)(2,1)}, bf16[384,768]{1,0:T(8,128)(2,1)S(1)}, u32[]{:S(2)}, u32[]{:S(2)}) collective-permute-start(bf16[384,768]{1,0:T(8,128)(2,1)} %bitcast.12), channel_id=1, source_target_pairs={{0,16},{1,17},{2,18},{3,19},{4,20},{5,21},{6,22},{7,23},{8,9},{9,8... | collective-permute-start | bytes 1769480 | tf_op jit(solution)/shard_map/ppermute | solution.py:84
  68.1 29.6 %collective-permute-start.19 = (bf16[384,768]{1,0:T(8,128)(2,1)S(1)}, bf16[384,768]{1,0:T(8,128)(2,1)S(1)}, u32[]{:S(2)}, u32[]{:S(2)}) collective-permute-start(bf16[384,768]{1,0:T(8,128)(2,1)S(1)} %collective-permute-done.10.refs_4_), channel_id=1, source_target_pairs={{0,16},{1,17},{2,18},{3,19},{4,20},{5,21},{6,22},{7,23},{8,9},{9,8... | collective-permute-start | bytes 1769480 | tf_op jit(solution)/shard_map/ppermute | solution.py:84
  72.1 16.3 %collective-permute-start.17 = (bf16[384,768]{1,0:T(8,128)(2,1)S(1)}, bf16[384,768]{1,0:T(8,128)(2,1)S(1)}, u32[]{:S(2)}, u32[]{:S(2)}) collective-permute-start(bf16[384,768]{1,0:T(8,128)(2,1)S(1)} %bitcast.78), channel_id=1, source_target_pairs={{0,1},{1,0},{2,3},{3,2},{4,5},{5,4},{6,7},{7,6},{8,24},{9,25},{10,... | collective-permute-start | bytes 1769480 | tf_op jit(solution)/shard_map/ppermute | solution.py:84
  81.4 25.5 %collective-permute-start.23 = (bf16[384,768]{1,0:T(8,128)(2,1)S(1)}, bf16[384,768]{1,0:T(8,128)(2,1)S(1)}, u32[]{:S(2)}, u32[]{:S(2)}) collective-permute-start(bf16[384,768]{1,0:T(8,128)(2,1)S(1)} %bitcast.80), channel_id=1, source_target_pairs={{0,16},{1,17},{2,18},{3,19},{4,20},{5,21},{6,22},{7,23},{8,9},{9,8... | collective-permute-start | bytes 1769480 | tf_op jit(solution)/shard_map/ppermute | solution.py:84
  82.5 34.7 %collective-permute-start.25 = (bf16[384,768]{1,0:T(8,128)(2,1)S(1)}, bf16[384,768]{1,0:T(8,128)(2,1)S(1)}, u32[]{:S(2)}, u32[]{:S(2)}) collective-permute-start(bf16[384,768]{1,0:T(8,128)(2,1)S(1)} %bitcast.81), channel_id=1, source_target_pairs={{0,8},{1,9},{2,10},{3,11},{4,12},{5,13},{6,14},{7,15},{8,0},{9,1},... | collective-permute-start | bytes 1769480 | tf_op jit(solution)/shard_map/ppermute | solution.py:84
  88.4 18.7 %collective-permute-start.24 = (bf16[384,768]{1,0:T(8,128)(2,1)S(1)}, bf16[384,768]{1,0:T(8,128)(2,1)S(1)}, u32[]{:S(2)}, u32[]{:S(2)}) collective-permute-start(bf16[384,768]{1,0:T(8,128)(2,1)S(1)} %collective-permute-done.17.refs_0_), channel_id=1, source_target_pairs={{0,16},{1,17},{2,18},{3,19},{4,20},{5,21},{6,22},{7,23},{8,9},{9,8... | collective-permute-start | bytes 1769480 | tf_op jit(solution)/shard_map/ppermute | solution.py:84
  107.0 10.2 %collective-permute-start.27 = (bf16[384,768]{1,0:T(8,128)(2,1)S(1)}, bf16[384,768]{1,0:T(8,128)(2,1)S(1)}, u32[]{:S(2)}, u32[]{:S(2)}) collective-permute-start(bf16[384,768]{1,0:T(8,128)(2,1)S(1)} %collective-permute-done.17.refs_0_), channel_id=1, source_target_pairs={{0,8},{1,9},{2,10},{3,11},{4,12},{5,13},{6,14},{7,15},{8,0},{9,1},... | collective-permute-start | bytes 1769480 | tf_op jit(solution)/shard_map/ppermute | solution.py:84
  176.9 15.5 %collective-permute-start.29 = (bf16[2,4,2,192,768]{4,3,2,1,0:T(8,128)(2,1)}, bf16[2,4,2,192,768]{4,3,2,1,0:T(8,128)(2,1)S(1)}, u32[]{:S(2)}, u32[]{:S(2)}) collective-permute-start(bf16[2,4,2,192,768]{4,3,2,1,0:T(8,128)(2,1)} %bitcast.72), channel_id=1, source_target_pairs={{0,8},{1,9},{2,10},{3,11},{4,12},{5,13},{6,14},{7,15},{8,0},{9,1},... | collective-permute-start | bytes 14155784 | tf_op jit(solution)/shard_map/ppermute | solution.py:84
  195.5 32.1 %collective-permute-start.30 = (bf16[4,2,192,768]{3,2,1,0:T(8,128)(2,1)S(1)}, bf16[4,2,192,768]{3,2,1,0:T(8,128)(2,1)S(1)}, u32[]{:S(2)}, u32[]{:S(2)}) collective-permute-start(bf16[4,2,192,768]{3,2,1,0:T(8,128)(2,1)S(1)} %get-tuple-element.111.refs_0_), channel_id=1, source_target_pairs={{0,1},{1,0},{2,3},{3,2},{4,5},{5,4},{6,7},{7,6},{8,24},{9,25},{10,... | collective-permute-start | bytes 7077896 | tf_op jit(solution)/shard_map/ppermute | solution.py:84
  229.2 16.3 %collective-permute-start.32 = (bf16[4,192,768]{2,1,0:T(8,128)(2,1)S(1)}, bf16[4,192,768]{2,1,0:T(8,128)(2,1)S(1)}, u32[]{:S(2)}, u32[]{:S(2)}) collective-permute-start(bf16[4,192,768]{2,1,0:T(8,128)(2,1)S(1)} %get-tuple-element.120.refs_3_), channel_id=1, source_target_pairs={{0,16},{1,17},{2,18},{3,19},{4,20},{5,21},{6,22},{7,23},{8,9},{9,8... | collective-permute-start | bytes 3538952 | tf_op jit(solution)/shard_map/ppermute | solution.py:84
  246.3 18.4 %collective-permute-start.33 = (bf16[4,2,112,768]{3,2,1,0:T(8,128)(2,1)S(1)}, bf16[4,2,112,768]{3,2,1,0:T(8,128)(2,1)S(1)}, u32[]{:S(2)}, u32[]{:S(2)}) collective-permute-start(bf16[4,2,112,768]{3,2,1,0:T(8,128)(2,1)S(1)} %get-tuple-element.130), channel_id=1, source_target_pairs={{0,1},{1,0},{2,3},{3,2},{4,5},{5,4},{6,7},{7,6},{8,24},{9,25},{10,... | collective-permute-start | bytes 4128776 | tf_op jit(solution)/shard_map/ppermute | solution.py:84
  247.5 12.5 %collective-permute-start.34 = (bf16[1,192,768]{2,1,0:T(8,128)(2,1)S(1)}, bf16[1,192,768]{2,1,0:T(8,128)(2,1)S(1)}, u32[]{:S(2)}, u32[]{:S(2)}) collective-permute-start(bf16[1,192,768]{2,1,0:T(8,128)(2,1)S(1)} %get-tuple-element.128), channel_id=1, source_target_pairs={{0,4},{1,5},{2,6},{3,7},{4,0},{5,1},{6,2},{7,3},{8,12},{9,13},{10,... | collective-permute-start | bytes 884744 | tf_op jit(solution)/shard_map/ppermute | solution.py:84
  265.9 18.0 %collective-permute-start.35 = (bf16[4,112,768]{2,1,0:T(8,128)(2,1)S(1)}, bf16[4,112,768]{2,1,0:T(8,128)(2,1)S(1)}, u32[]{:S(2)}, u32[]{:S(2)}) collective-permute-start(bf16[4,112,768]{2,1,0:T(8,128)(2,1)S(1)} %get-tuple-element.133), channel_id=1, source_target_pairs={{0,16},{1,17},{2,18},{3,19},{4,20},{5,21},{6,22},{7,23},{8,9},{9,8... | collective-permute-start | bytes 2064392 | tf_op jit(solution)/shard_map/ppermute | solution.py:84
  267.0 13.4 %collective-permute-start.41 = (bf16[1,192,768]{2,1,0:T(8,128)(2,1)S(1)}, bf16[1,192,768]{2,1,0:T(8,128)(2,1)S(1)}, u32[]{:S(2)}, u32[]{:S(2)}) collective-permute-start(bf16[1,192,768]{2,1,0:T(8,128)(2,1)S(1)} %get-tuple-element.129), channel_id=1, source_target_pairs={{0,6},{1,7},{2,0},{3,1},{4,2},{5,3},{6,4},{7,5},{8,14},{9,15},{10,... | collective-permute-start | bytes 884744 | tf_op jit(solution)/shard_map/ppermute | solution.py:84
  267.0 14.3 %collective-permute-start.40 = (bf16[1,192,768]{2,1,0:T(8,128)(2,1)S(1)}, bf16[1,192,768]{2,1,0:T(8,128)(2,1)S(1)}, u32[]{:S(2)}, u32[]{:S(2)}) collective-permute-start(bf16[1,192,768]{2,1,0:T(8,128)(2,1)S(1)} %get-tuple-element.127), channel_id=1, source_target_pairs={{0,2},{1,3},{2,4},{3,5},{4,6},{5,7},{6,0},{7,1},{8,10},{9,11},{10,... | collective-permute-start | bytes 884744 | tf_op jit(solution)/shard_map/ppermute | solution.py:84
  284.6 14.2 %collective-permute-start.38 = (bf16[1,112,768]{2,1,0:T(8,128)(2,1)S(1)}, bf16[1,112,768]{2,1,0:T(8,128)(2,1)S(1)}, u32[]{:S(2)}, u32[]{:S(2)}) collective-permute-start(bf16[1,112,768]{2,1,0:T(8,128)(2,1)S(1)} %get-tuple-element.137), channel_id=1, source_target_pairs={{0,6},{1,7},{2,0},{3,1},{4,2},{5,3},{6,4},{7,5},{8,14},{9,15},{10,... | collective-permute-start | bytes 516104 | tf_op jit(solution)/shard_map/ppermute | solution.py:84
  285.0 13.8 %collective-permute-start.37 = (bf16[1,112,768]{2,1,0:T(8,128)(2,1)S(1)}, bf16[1,112,768]{2,1,0:T(8,128)(2,1)S(1)}, u32[]{:S(2)}, u32[]{:S(2)}) collective-permute-start(bf16[1,112,768]{2,1,0:T(8,128)(2,1)S(1)} %get-tuple-element.136), channel_id=1, source_target_pairs={{0,4},{1,5},{2,6},{3,7},{4,0},{5,1},{6,2},{7,3},{8,12},{9,13},{10,... | collective-permute-start | bytes 516104 | tf_op jit(solution)/shard_map/ppermute | solution.py:84
  286.9 12.2 %collective-permute-start.36 = (bf16[1,112,768]{2,1,0:T(8,128)(2,1)S(1)}, bf16[1,112,768]{2,1,0:T(8,128)(2,1)S(1)}, u32[]{:S(2)}, u32[]{:S(2)}) collective-permute-start(bf16[1,112,768]{2,1,0:T(8,128)(2,1)S(1)} %get-tuple-element.135), channel_id=1, source_target_pairs={{0,2},{1,3},{2,4},{3,5},{4,6},{5,7},{6,0},{7,1},{8,10},{9,11},{10,... | collective-permute-start | bytes 516104 | tf_op jit(solution)/shard_map/ppermute | solution.py:84
  288.2 17.0 %collective-permute-start.42 = (f32[7,768]{1,0:T(8,128)S(1)}, f32[7,768]{1,0:T(8,128)S(1)}, u32[]{:S(2)}, u32[]{:S(2)}) collective-permute-start(f32[7,768]{1,0:T(8,128)S(1)} %slice.133), channel_id=1, source_target_pairs={{1,0},{2,1},{3,2},{4,3},{5,4},{6,5},{7,6},{8,7},{9,8},{10,9},{11,1... | collective-permute-start | bytes 64520 | tf_op jit(solution)/shard_map/ppermute | solution.py:298
  (52 other events, 636.8 us)
where the time goes:
time: 315 us; the launch traced here: 312 us
  Pallas kernels  152 us (48%)
  waiting for transfers between devices  73.1 us (23%)
  starting transfers between devices  59.3 us (19%)
  local copies, waits for them, and re-layouts  13.2 us (4%)
  other arithmetic  8.81 us (3%)
  between operations  5.18 us (2%)
    ppermute x39, waiting for transfers between devices, send(): return lax.ppermute(array, AXES, self.rotation(axis, step))  71.1 us
    pallas_call x1, Pallas kernels, middle(): pl.pallas_call(functools.partial(middle_kernel, fetch, len(sources)), gri...  41 us
    ppermute x39, starting transfers between devices, send(): return lax.ppermute(array, AXES, self.rotation(axis, step))  37.4 us
    pallas_call x2, Pallas kernels, attend_back(): pl.pallas_call(attend_back_kernel, grid=(pairs,), in_specs=attend_specs()...  33.8 us
    pallas_call x3, Pallas kernels, attend(): pl.pallas_call(attend_kernel, grid=(pairs,), in_specs=attend_specs() + [p...  26.3 us
    pallas_call x1, Pallas kernels, ffn_terms(): pl.pallas_call(kernel, grid=(2 * UP_CHUNKS,), in_specs=[pl.BlockSpec(memo...  17.5 us
    ppermute x2, starting transfers between devices, to_rows(): lax.ppermute(flat[-tail:], AXES, [(i, i + 1) for i in range(count - 1)])  12.4 us
    pallas_call x6, Pallas kernels, add_routed(): pl.pallas_call(kernel, grid_spec=pltpu.PrefetchScalarGridSpec(num_scalar_...  9.43 us
  transfers between devices with their start and end apart: 43, of which 17 were waited for; matrix products, arithmetic and copies ran while one was open for 3% of the time, Pallas kernels for 28%

commit v1 on v0

--- a/solution.py
+++ b/solution.py
@@ -432,19 +432,37 @@
 
     value_t = value[...].T
     query_t = one_head((query[...] * jnp.asarray(SCALE, BF)).T)
-    for block in range(QUERY_BLOCKS):
+    parts = []
+
+    def score(block, h):
         low, high = window(block)
         at = slice(block * QUERY_BLOCK, (block + 1) * QUERY_BLOCK)
-        parts = []
-        for h in range(2):
-            scores = dot(key[low:high, :], query_t[h][:, at], 1, 0) + bias[0 : high - low, at]
-            top = jnp.max(scores, axis=0, keepdims=True)
-            shifted = jnp.exp(scores - top)
-            total = jnp.sum(shifted, axis=0, keepdims=True)
-            part = dot(value_t[h * HEAD : (h + 1) * HEAD, low:high], shifted.astype(BF), 1, 0)
-            parts.append(part * (1.0 / total))
-            log_total[0, h : h + 1, at] = top + jnp.log(total)
-        mixed[at, :] = jnp.concatenate(parts, 0).T.astype(BF)
+        return dot(key[low:high, :], query_t[h][:, at], 1, 0) + bias[0 : high - low, at]
+
+    def mix(block, h, shifted, inverse):
+        low, high = window(block)
+        at = slice(block * QUERY_BLOCK, (block + 1) * QUERY_BLOCK)
+        part = dot(value_t[h * HEAD : (h + 1) * HEAD, low:high], shifted, 1, 0)
+        parts.append(part * inverse)
+        if h == 1:
+            mixed[at, :] = jnp.concatenate(parts, 0).T.astype(BF)
+            parts.clear()
+
+    items = [(block, h) for block in range(QUERY_BLOCKS) for h in range(2)]
+    ahead, behind = score(*items[0]), None
+    for n, (block, h) in enumerate(items):
+        at = slice(block * QUERY_BLOCK, (block + 1) * QUERY_BLOCK)
+        scores = ahead
+        if n + 1 < len(items):
+            ahead = score(*items[n + 1])
+        if behind is not None:
+            mix(*behind)
+        top = jnp.max(scores, axis=0, keepdims=True)
+        shifted = jnp.exp(scores - top)
+        total = jnp.sum(shifted, axis=0, keepdims=True)
+        log_total[0, h : h + 1, at] = top + jnp.log(total)
+        behind = (block, h, shifted.astype(BF), 1.0 / total)
+    mix(*behind)
 
 
 def attend_specs():
@@ -491,22 +509,39 @@
     query_one, grad_one = one_head(query_t), one_head(grad_t)
     key_sum[...] = jnp.zeros_like(key_sum)
     value_sum[...] = jnp.zeros_like(value_sum)
-    for block in range(QUERY_BLOCKS):
+    parts = []
+
+    def score(block, h):
         low, high = window(block)
         at = slice(block * QUERY_BLOCK, (block + 1) * QUERY_BLOCK)
-        parts = []
-        for h in range(2):
-            rows = slice(h * HEAD, (h + 1) * HEAD)
-            scores = dot(key[low:high, :], query_one[h][:, at], 1, 0) + bias[0 : high - low, at]
-            probs = jnp.exp(scores - log_total[0, h : h + 1, at])
-            grad_probs = dot(value[low:high, :], grad_one[h][:, at], 1, 0)
-            weighted = probs * grad_probs
-            total = jnp.sum(weighted, axis=0, keepdims=True)
-            grad_scores = (weighted - probs * total).astype(BF)
-            parts.append(dot(key_t[rows, low:high], grad_scores, 1, 0))
-            key_sum[rows, low:high] += dot(query_t[rows, at], grad_scores, 1, 1)
-            value_sum[rows, low:high] += dot(grad_t[rows, at], probs.astype(BF), 1, 1)
-        grads[0, at, :] = (jnp.concatenate(parts, 0) * SCALE).T.astype(BF)
+        scores = dot(key[low:high, :], query_one[h][:, at], 1, 0) + bias[0 : high - low, at]
+        return scores, dot(value[low:high, :], grad_one[h][:, at], 1, 0)
+
+    def spread(block, h, grad_scores, probs):
+        low, high = window(block)
+        at = slice(block * QUERY_BLOCK, (block + 1) * QUERY_BLOCK)
+        rows = slice(h * HEAD, (h + 1) * HEAD)
+        parts.append(dot(key_t[rows, low:high], grad_scores, 1, 0))
+        key_sum[rows, low:high] += dot(query_t[rows, at], grad_scores, 1, 1)
+        value_sum[rows, low:high] += dot(grad_t[rows, at], probs, 1, 1)
+        if h == 1:
+            grads[0, at, :] = (jnp.concatenate(parts, 0) * SCALE).T.astype(BF)
+            parts.clear()
+
+    items = [(block, h) for block in range(QUERY_BLOCKS) for h in range(2)]
+    ahead, behind = score(*items[0]), None
+    for n, (block, h) in enumerate(items):
+        at = slice(block * QUERY_BLOCK, (block + 1) * QUERY_BLOCK)
+        scores, grad_probs = ahead
+        if n + 1 < len(items):
+            ahead = score(*items[n + 1])
+        if behind is not None:
+            spread(*behind)
+        probs = jnp.exp(scores - log_total[0, h : h + 1, at])
+        weighted = probs * grad_probs
+        total = jnp.sum(weighted, axis=0, keepdims=True)
+        behind = (block, h, (weighted - probs * total).astype(BF), probs.astype(BF))
+    spread(*behind)
     grads[1] = key_sum[...].T.astype(BF)
     grads[2] = value_sum[...].T.astype(BF)
     sums[...] = jnp.zeros_like(sums)
@@ -589,9 +624,7 @@
     vec,
     *refs,
 ):
-    mixed = jnp.concatenate([ref[...] for ref in refs[: len(AHEAD_PAIRS)]], 1)
-    refs = refs[len(AHEAD_PAIRS) :]
-
+    mixed, refs = refs[: len(AHEAD_PAIRS)], refs[len(AHEAD_PAIRS) :]
     (
         final_low,
         hidden_low,
@@ -604,51 +637,112 @@
         vec_grad,
         crop_sums,
         slope,
+        hidden_one,
+        normals,
+        inverses,
         weights,
         sem,
     ) = refs[groups:]
     step = pl.program_id(0)
+
+    def row(i):
+        return vec[i : i + 1]
+
+    def chunk(j):
+        return weights[j * D : (j + 1) * D]
+
+    def note(i, value):
+        vec_grad[i : i + 1] += value
 
     @pl.when(step == 0)
     def _():
         vec_grad[...] = jnp.zeros_like(vec_grad)
         crop_sums[...] = jnp.zeros_like(crop_sums)
         fetch(read_here(me), refs[:groups], weights, sem)
-
-    def row(i):
-        return vec[i : i + 1]
-
-    def chunk(j):
-        return weights[j * D : (j + 1) * D]
-
-    def note(i, value):
-        vec_grad[i : i + 1] += value
-
-    resid_one = tokens[...].astype(F32) + (dot(mixed, w_out[...], 1, 0) + row(2))
-    normal_one, inverse_one = normalise(resid_one)
-    hidden = normal_one * row(3) + row(4)
-    low = hidden.astype(BF)
-    hidden_low[...] = low
-    total = hidden + row(9)
-
-    def arrived(first, chunks, which):
-        @pl.when(step == 0)
-        def _():
-            part = weights.at[pl.ds(first * D, chunks * D)]
-            pltpu.make_async_copy(part, part, sem.at[which]).wait()
-
+        for first in range(0, ROW, MIDDLE_ROWS):
+            at = slice(first, first + MIDDLE_ROWS)
+            held = jnp.concatenate([ref[at] for ref in mixed], 1)
+            resid_one = tokens[at].astype(F32) + (dot(held, w_out[...], 1, 0) + row(2))
+            normal, inverse = normalise(resid_one)
+            hidden = normal * row(3) + row(4)
+            hidden_one[at] = hidden
+            hidden_low[at] = hidden.astype(BF)
+            normals[at] = normal
+            inverses[at] = jnp.broadcast_to(inverse, (MIDDLE_ROWS, 128))
+        for j in range(UP_CHUNKS):
+            part = weights.at[pl.ds(j * D, D)]
+            pltpu.make_async_copy(part, part, sem.at[j]).wait()
+        part = weights.at[pl.ds(FF, FF)]
+        pltpu.make_async_copy(part, part, sem.at[UP_CHUNKS]).wait()
+
+    @pl.when(step > 0)
+    def _():
+        middle_tile(
+            step - 1,
+            count,
+            seg_row,
+            out_grad,
+            w_out,
+            row,
+            chunk,
+            note,
+            final_low,
+            hidden_low,
+            activated,
+            grad_pre,
+            grad_ffn_out,
+            grad_attn_out,
+            grad_mixed,
+            grad_resid,
+            crop_sums,
+            slope,
+            hidden_one,
+            normals,
+            inverses,
+        )
+
+
+def middle_tile(
+    step,
+    count,
+    seg_row,
+    out_grad,
+    w_out,
+    row,
+    chunk,
+    note,
+    final_low,
+    hidden_low,
+    activated,
+    grad_pre,
+    grad_ffn_out,
+    grad_attn_out,
+    grad_mixed,
+    grad_resid,
+    crop_sums,
+    slope,
+    hidden_one,
+    normals,
+    inverses,
+):
+    at = pl.ds(pl.multiple_of(step * MIDDLE_ROWS, MIDDLE_ROWS), MIDDLE_ROWS)
+    low = hidden_low[at, :]
+    total = hidden_one[at, :] + row(9)
+    normal_one, inverse_one = normals[at, :], inverses[at, 0:1]
+    ahead, act = dot(low, chunk(0), 1, 0), None
     for j in range(UP_CHUNKS):
         at = slice(j * D, (j + 1) * D)
-        arrived(j, 1, j)
-        pre = dot(low, chunk(j), 1, 0) + row(5 + j)
+        pre = ahead + row(5 + j)
+        if j + 1 < UP_CHUNKS:
+            ahead = dot(low, chunk(j + 1), 1, 0)
+        if act is not None:
+            total = total + dot(act, chunk(UP_CHUNKS + j - 1), 1, 0)
         share = 0.5 + 0.5 * lax.erf(pre * (0.5**0.5))
         density = jnp.exp(-0.5 * pre * pre) * 0.3989422804014327
         slope[:, at] = share + pre * density
         act = (pre * share).astype(BF)
         activated[:, at] = act
-        if j == 0:
-            arrived(UP_CHUNKS, UP_CHUNKS, UP_CHUNKS)
-        total = total + dot(act, chunk(UP_CHUNKS + j), 1, 0)
+    total = total + dot(act, chunk(2 * UP_CHUNKS - 1), 1, 0)
     normal_two, inverse_two = normalise(total)
     final = normal_two * row(10) + row(11)
     final_low[...] = final.astype(BF)
@@ -674,12 +768,18 @@
     grad_ffn_out[...] = grad_out
     note(9, column_sum(grad_out.astype(F32)))
     grad_hidden = grad_two
+    ahead, back = dot(grad_out, chunk(UP_CHUNKS), 1, 1), None
     for j in range(UP_CHUNKS):
         at = slice(j * D, (j + 1) * D)
-        back = (dot(grad_out, chunk(UP_CHUNKS + j), 1, 1) * slope[:, at]).astype(BF)
+        grad_act = ahead
+        if j + 1 < UP_CHUNKS:
+            ahead = dot(grad_out, chunk(UP_CHUNKS + j + 1), 1, 1)
+        if back is not None:
+            grad_hidden = grad_hidden + dot(back, chunk(j - 1), 1, 1)
+        back = (grad_act * slope[:, at]).astype(BF)
         grad_pre[:, at] = back
         note(5 + j, column_sum(back.astype(F32)))
-        grad_hidden = grad_hidden + dot(back, chunk(j), 1, 1)
+    grad_hidden = grad_hidden + dot(back, chunk(UP_CHUNKS - 1), 1, 1)
     note(3, column_sum(grad_hidden * normal_one))
     note(4, column_sum(grad_hidden))
     grad_one = normalise_back(grad_hidden, row(3), normal_one, inverse_one)
@@ -692,8 +792,15 @@
 
 def middle(count, me, segments, mixed, tokens, out_grad, attn_whole, sources, fetch, vec):
     rows = tokens.shape[0]
-    tile = pl.BlockSpec((MIDDLE_ROWS, D), lambda i: (i, 0))
-    wide = pl.BlockSpec((MIDDLE_ROWS, FF), lambda i: (i, 0))
+
+    def tile_of(i):
+        return jnp.maximum(i - 1, 0)
+
+    def whole(width):
+        return pl.BlockSpec((rows, width), lambda i: (0, 0), pipeline_mode=pl.Buffered(1))
+
+    tile = pl.BlockSpec((MIDDLE_ROWS, D), lambda i: (tile_of(i), 0))
+    wide = pl.BlockSpec((MIDDLE_ROWS, FF), lambda i: (tile_of(i), 0))
     small = pl.BlockSpec((VEC_ROWS, D), lambda i: (0, 0))
 
     def shape(width, kind):
@@ -701,19 +808,19 @@
 
     return pl.pallas_call(
         functools.partial(middle_kernel, fetch, len(sources)),
-        grid=(rows // MIDDLE_ROWS,),
+        grid=(rows // MIDDLE_ROWS + 1,),
         in_specs=[
             pl.BlockSpec(memory_space=pltpu.SMEM),
             pl.BlockSpec(memory_space=pltpu.SMEM),
-            pl.BlockSpec((1, MIDDLE_ROWS), lambda i: (0, i)),
-            tile,
+            pl.BlockSpec((1, MIDDLE_ROWS), lambda i: (0, tile_of(i))),
+            whole(D),
             tile,
             pl.BlockSpec((D, D), lambda i: (3, 0), pipeline_mode=pl.Buffered(1)),
             small,
         ]
-        + [pl.BlockSpec((MIDDLE_ROWS, 2 * HEAD * p), lambda i: (i, 0)) for p in AHEAD_PAIRS]
+        + [whole(2 * HEAD * p) for p in AHEAD_PAIRS]
         + [pl.BlockSpec(memory_space=pl.ANY)] * len(sources),
-        out_specs=[tile, tile, wide, wide, tile, tile, tile, tile, small, small],
+        out_specs=[tile, whole(D), wide, wide, tile, tile, tile, tile, small, small],
         out_shape=[
             shape(D, BF),
             shape(D, BF),
@@ -728,10 +835,13 @@
         ],
         scratch_shapes=[
             pltpu.VMEM((MIDDLE_ROWS, FF), F32),
+            pltpu.VMEM((rows, D), F32),
+            pltpu.VMEM((rows, D), F32),
+            pltpu.VMEM((rows, 128), F32),
             pltpu.VMEM((FFN_ROWS, D), BF),
             pltpu.SemaphoreType.DMA((UP_CHUNKS + 1,)),
         ],
-        compiler_params=pltpu.CompilerParams(vmem_limit_bytes=44 * MIB),
+        compiler_params=pltpu.CompilerParams(vmem_limit_bytes=40 * MIB),
         cost_estimate=cost(40),
         name="middle",
     )(count, me, segments.reshape(1, rows), tokens, out_grad, attn_whole, vec, *mixed, *sources)
@@ -1016,10 +1126,10 @@
         blocks = ffn_set.start_z(order(ffn_own[half_rows:], plane, near[0]))
         aside = [places.send(near[0], "xy", 1)]
         crossed = [places.send(near[0], "c", 1)]
+        near.append(ffn_set.join_parts(place_list, [blocks]))
         groups = [plane]
-        groups += [order(g, aside[0], *blocks) for g in attn_set.along_second(plane)]
+        groups += [order(g, aside[0], near[1]) for g in attn_set.along_second(plane)]
         attn_groups = groups + attn_set.from_core(groups)
-        near.append(ffn_set.join_parts(place_list, [blocks]))
         aside.append(places.send(near[1], "xy", 1))
         across = [places.send(near[0], "yx", 1)]
         corner = [places.send(aside[0], "yx", 1)]

time: 315 us -> 298 us (0.946)
  Pallas kernels: 152 us -> 128 us
  waiting for transfers between devices: 73.1 us -> 78.3 us
  starting transfers between devices: 59.3 us -> 55.7 us
    pallas_call x3, Pallas kernels: 26.3 us -> 15.5 us  [attend(): pl.pallas_call(attend_kernel, grid=(pairs,), in_specs=attend_specs() + [p...]
    pallas_call x2, Pallas kernels: 33.8 us -> 24.5 us  [attend_back(): pl.pallas_call(attend_back_kernel, grid=(pairs,), in_specs=attend_specs()...]
    ppermute x39, waiting for transfers between devices: 71.1 us -> 76.3 us  [send(): return lax.ppermute(array, AXES, self.rotation(axis, step))]
    pallas_call x1, Pallas kernels: 41 us -> 37.1 us  [middle(): pl.pallas_call(functools.partial(middle_kernel, fetch, len(sources)), gri...]
  transfers between devices with their start and end apart: 43 -> 43, of which waited for: 17 -> 22; matrix products, arithmetic and copies ran while one was open for 3% -> 3% of each run, Pallas kernels for 28% -> 23%
where the time goes in v1:
time: 298 us; the launch traced here: 292 us
  Pallas kernels  128 us (43%)
  waiting for transfers between devices  78.3 us (26%)
  starting transfers between devices  55.7 us (19%)
  local copies, waits for them, and re-layouts  16.2 us (5%)
  other arithmetic  8.81 us (3%)
  between operations  5.1 us (2%)
    ppermute x39, waiting for transfers between devices, send(): return lax.ppermute(array, AXES, self.rotation(axis, step))  76.3 us
    pallas_call x1, Pallas kernels, middle(): pl.pallas_call(functools.partial(middle_kernel, fetch, len(sources)), gri...  37.1 us
    ppermute x39, starting transfers between devices, send(): return lax.ppermute(array, AXES, self.rotation(axis, step))  36.9 us
    pallas_call x2, Pallas kernels, attend_back(): pl.pallas_call(attend_back_kernel, grid=(pairs,), in_specs=attend_specs()...  24.5 us
    pallas_call x1, Pallas kernels, ffn_terms(): pl.pallas_call(kernel, grid=(2 * UP_CHUNKS,), in_specs=[pl.BlockSpec(memo...  17.7 us
    pallas_call x3, Pallas kernels, attend(): pl.pallas_call(attend_kernel, grid=(pairs,), in_specs=attend_specs() + [p...  15.5 us
    ppermute x2, starting transfers between devices, to_rows(): lax.ppermute(flat[-tail:], AXES, [(i, i + 1) for i in range(count - 1)])  12.4 us
    unnamed x84, local copies, waits for them, and re-layouts  11.2 us
  transfers between devices with their start and end apart: 43, of which 22 were waited for; matrix products, arithmetic and copies ran while one was open for 3% of the time, Pallas kernels for 23%

profile of v1, /device:TPU:8, one launch (start us, length us, event | category | flops | bytes accessed | tf_op | source)
XLA Modules:
  0.0 292.4 jit_solution(13765741565986912925)
XLA Ops:
  1.5 3.4 %collective-permute-start = (bf16[3840]{0:T(1024)(128)(2,1)S(1)}, bf16[3840]{0:T(1024)(128)(2,1)S(1)}, u32[]{:S(2)}, u32[]{:S(2)}) collective-permute-start(bf16[3840]{0:T(1024)(128)(2,1)S(1)} %slice.161), channel_id=1, source_target_pairs={{0,1},{1,2},{2,3},{3,4},{4,5},{5,6},{6,7},{7,8},{8,9},{9,10},{10,1... | collective-permute-start | bytes 23048 | tf_op jit(solution)/shard_map/ppermute | solution.py:290
  11.4 2.6 collective-permute-start.2
  16.3 9.0 %collective-permute-start.5 = (bf16[5376]{0:T(1024)(128)(2,1)S(1)}, bf16[5376]{0:T(1024)(128)(2,1)S(1)}, u32[]{:S(2)}, u32[]{:S(2)}) collective-permute-start(bf16[5376]{0:T(1024)(128)(2,1)S(1)} %slice.100), channel_id=1, source_target_pairs={{0,1},{1,2},{2,3},{3,4},{4,5},{5,6},{6,7},{7,8},{8,9},{9,10},{10,1... | collective-permute-start | bytes 32264 | tf_op jit(solution)/shard_map/ppermute | solution.py:290
  27.5 2.5 collective-permute-start.6
  30.0 2.6 collective-permute-start.7
  33.2 2.5 collective-permute-done.4
  35.8 4.5 %collective-permute-done.6.refs_1_ = bf16[96,768]{1,0:T(8,128)(2,1)S(1)} collective-permute-done((bf16[96,768]{1,0:T(8,128)(2,1)S(1)}, bf16[96,768]{1,0:T(8,128)(2,1)S(1)}, u32[]{:S(2)}, u32[]{:S(2)}) %collective-permute-start.6) | collective-permute-done | bytes 147488 | tf_op jit(solution)/shard_map/ppermute | solution.py:84
  46.7 2.4 collective-permute-start.10
  52.7 6.5 %collective-permute-done.11.refs_1_ = bf16[96,768]{1,0:T(8,128)(2,1)S(1)} collective-permute-done((bf16[96,768]{1,0:T(8,128)(2,1)S(1)}, bf16[96,768]{1,0:T(8,128)(2,1)S(1)}, u32[]{:S(2)}, u32[]{:S(2)}) %collective-permute-start.11) | collective-permute-done | bytes 147488 | tf_op jit(solution)/shard_map/ppermute | solution.py:84
  64.3 2.7 collective-permute-done.9.refs_1_
  74.9 7.5 %project.1 = (bf16[1024,768]{1,0:T(8,128)(2,1)S(1)}, bf16[1024,768]{1,0:T(8,128)(2,1)S(1)}, bf16[1024,768]{1,0:T(8,128)(2,1)S(1)}, f32[16,768]{1,0:T(8,128)S(1)}, bf16[3072,768]{1,0:T(8,128)(2,1)S(1)}) custom-call(s32[4]{0:T(128)S(1)} %pad_add_fusion.me_ref.me, bf16[1024,768]{1,0:T(8,128)(2,1)S(1)} %copy-done.6, ...), custom_call_target="tpu_custom_call" | custom-call | flops 8800000000 | bytes 1048576 | tf_op jit(solution)/shard_map/project/pallas_call | solution.py:357
  83.5 4.1 %collective-permute-done.17.refs_0_ = bf16[384,768]{1,0:T(8,128)(2,1)S(1)} collective-permute-done((bf16[384,768]{1,0:T(8,128)(2,1)}, bf16[384,768]{1,0:T(8,128)(2,1)S(1)}, u32[]{:S(2)}, u32[]{:S(2)}) %collective-permute-start.17) | collective-permute-done | bytes 589856 | tf_op jit(solution)/shard_map/ppermute | solution.py:84
  88.2 5.2 %attend.3 = (bf16[1024,256]{1,0:T(8,128)(2,1)S(1)}, f32[2,8,1024]{2,1,0:T(8,128)S(1)}) custom-call(s32[1]{0:T(128)} %copy.47.count, s32[1024,1]{1,0:T(8,128)S(1)} %copy.34.seg_column, s32[1,1024]{1,0:T(1,128)S(1)} %bitcast.66, bf16[1024,768]{1,0:T(8,128)(2,1)S(1)} %get-tuple-element.83.query, bf16[1024,768]{1,0:T(8,128)(2,1)S(1)} %get-tuple-element.84.key, ...), custom_call_target="tpu_custom_call" | custom-call | flops 9166666752 | bytes 1048576 | tf_op jit(solution)/shard_map/attend/pallas_call | solution.py:478
  93.9 5.1 %attend.4 = (bf16[1024,256]{1,0:T(8,128)(2,1)S(1)}, f32[2,8,1024]{2,1,0:T(8,128)S(1)}) custom-call(s32[1]{0:T(128)} %copy.47.count, s32[1024,1]{1,0:T(8,128)S(1)} %copy.34.seg_column, s32[1,1024]{1,0:T(1,128)S(1)} %bitcast.67, bf16[1024,768]{1,0:T(8,128)(2,1)S(1)} %get-tuple-element.83.query, bf16[1024,768]{1,0:T(8,128)(2,1)S(1)} %get-tuple-element.84.key, ...), custom_call_target="tpu_custom_call" | custom-call | flops 9166666752 | bytes 1048576 | tf_op jit(solution)/shard_map/attend/pallas_call | solution.py:478
  99.3 3.9 %collective-permute-done.24 = bf16[384,768]{1,0:T(8,128)(2,1)S(1)} collective-permute-done((bf16[384,768]{1,0:T(8,128)(2,1)S(1)}, bf16[384,768]{1,0:T(8,128)(2,1)S(1)}, u32[]{:S(2)}, u32[]{:S(2)}) %collective-permute-start.24) | collective-permute-done | bytes 589856 | tf_op jit(solution)/shard_map/ppermute | solution.py:84
  103.8 5.2 %attend.5 = (bf16[1024,256]{1,0:T(8,128)(2,1)S(1)}, f32[2,8,1024]{2,1,0:T(8,128)S(1)}) custom-call(s32[1]{0:T(128)} %copy.47.count, s32[1024,1]{1,0:T(8,128)S(1)} %copy.34.seg_column, s32[1,1024]{1,0:T(1,128)S(1)} %bitcast.68, bf16[1024,768]{1,0:T(8,128)(2,1)S(1)} %get-tuple-element.83.query, bf16[1024,768]{1,0:T(8,128)(2,1)S(1)} %get-tuple-element.84.key, ...), custom_call_target="tpu_custom_call" | custom-call | flops 9166666752 | bytes 1048576 | tf_op jit(solution)/shard_map/attend/pallas_call | solution.py:478
  109.0 37.1 %middle.1 = (bf16[1024,768]{1,0:T(8,128)(2,1)}, bf16[1024,768]{1,0:T(8,128)(2,1)S(1)}, bf16[1024,3072]{1,0:T(8,128)(2,1)}, bf16[1024,3072]{1,0:T(8,128)(2,1)}, b...) custom-call(s32[1]{0:T(128)} %copy.47.count, ...), custom_call_target="tpu_custom_call" | custom-call | flops 44000002048 | bytes 1048576 | tf_op jit(solution)/shard_map/middle/pallas_call | solution.py:809
  148.5 17.7 %ffn_terms.1 = (bf16[2,8,192,768]{3,2,1,0:T(8,128)(2,1)}, bf16[2,8,192,768]{3,2,1,0:T(8,128)(2,1)}) custom-call(s32[4]{0:T(128)} %copy-done.3, bf16[1024,768]{1,0:T(8,128)(2,1)} %copy-done.26, bf16[1024,3072]{1,0:T(8,128)(2,1)} %get-tuple-element.104.activated_ref, bf16[1024,3072]{1,0:T(8,128)(2,1)} %get-tuple-element.105.refs_0_.refs_1_.refs_2_, ...), custom_call_target="tpu_custom_call" | custom-call | flops 16499999744 | bytes 1048576 | tf_op jit(solution)/shard_map/ffn_terms/pallas_call | solution.py:929
  170.5 8.3 %attend_back.2 = (bf16[3,1024,256]{2,1,0:T(8,128)(2,1)S(1)}, f32[8,256]{1,0:T(8,128)S(1)}) custom-call(s32[1]{0:T(128)} %copy.47.count, s32[1024,1]{1,0:T(8,128)S(1)} %copy.34.seg_column, s32[1,1024]{1,0:T(1,128)S(1)} %bitcast.70, bf16[1024,768]{1,0:T(8,128)(2,1)S(1)} %copy-done.17, bf16[1024,768]{1,0:T(8,128)(2,1)S(1)} %copy-done.19, ...), custom_call_target="tpu_custom_call" | custom-call | flops 13200000000 | bytes 1048576 | tf_op jit(solution)/shard_map/attend_back/pallas_call | solution.py:554
  178.9 3.0 %add_routed.6 = (bf16[4,2,192,768]{3,2,1,0:T(8,128)(2,1)S(1)}, bf16[4,2,192,768]{3,2,1,0:T(8,128)(2,1)S(1)}) custom-call(s32[4]{0:T(128)S(1)} %copy-done.4, bf16[2,4,2,192,768]{4,3,2,1,0:T(8,128)(2,1)S(1)} %bitcast.92, bf16[2,4,2,192,768]{4,3,2,1,0:T(8,128)(2,1)S(1)} %collective-permute-done.29.refs_1_.refs_3_, bf16[2,4,2,192,768]{4,3,2,1,0:T(8,128)(2,1)S(1)} %bitcast.93, ...), custom_call_target="tpu_custom_call" | custom-call | flops 5280000000 | bytes 1048576 | tf_op jit(solution)/shard_map/add_routed/pallas_call | solution.py:188
  183.6 16.2 %attend_back.3 = (bf16[3,1024,512]{2,1,0:T(8,128)(2,1)S(1)}, f32[8,512]{1,0:T(8,128)S(1)}) custom-call(s32[1]{0:T(128)} %copy.47.count, s32[1024,1]{1,0:T(8,128)S(1)} %copy.34.seg_column, s32[1,1024]{1,0:T(1,128)S(1)} %bitcast.71, bf16[1024,768]{1,0:T(8,128)(2,1)S(1)} %copy-done.17, bf16[1024,768]{1,0:T(8,128)(2,1)S(1)} %copy-done.20, ...), custom_call_target="tpu_custom_call" | custom-call | flops 16499999744 | bytes 1048576 | tf_op jit(solution)/shard_map/attend_back/pallas_call | solution.py:554
  199.9 7.6 %attn_terms.1 = (bf16[2,8,112,768]{3,2,1,0:T(8,128)(2,1)S(1)}, bf16[2,8,112,768]{3,2,1,0:T(8,128)(2,1)S(1)}) custom-call(s32[4]{0:T(128)S(1)} %copy-done.4, bf16[1024,768]{1,0:T(8,128)(2,1)S(1)} %copy-done.7, f32[16,768]{1,0:T(8,128)S(1)} %fusion.7.vectors_ref, bf16[1024,768]{1,0:T(8,128)(2,1)S(1)} %copy-done.15, ...), custom_call_target="tpu_custom_call" | custom-call | flops 6600000000 | bytes 1048576 | tf_op jit(solution)/shard_map/attn_terms/pallas_call | solution.py:1010
  207.5 3.2 %collective-permute-done.30.refs_1_.refs_3_ = bf16[4,2,192,768]{3,2,1,0:T(8,128)(2,1)S(1)} collective-permute-done((bf16[4,2,192,768]{3,2,1,0:T(8,128)(2,1)S(1)}, bf16[4,2,192,768]{3,2,1,0:T(8,128)(2,1)S(1)}, u32[]{:S(2)}, u32[]{:S(2)}) %collective-permute-start.30) | collective-permute-done | bytes 2359328 | tf_op jit(solution)/shard_map/ppermute | solution.py:84
  214.1 5.6 %token_grad.1 = bf16[1024,768]{1,0:T(8,128)(2,1)} custom-call(f32[1024,768]{1,0:T(8,128)S(1)} %copy-done.1, bf16[3072,768]{1,0:T(8,128)(2,1)S(1)} %bitcast.62, bf16[3,1024,256]{2,1,0:T(8,128)(2,1)S(1)} %get-tuple-element.108.refs_3_.refs_0_, bf16[3,1024,512]{2,1,0:T(8,128)(2,1)S(1)} %get-tuple-element.112.refs_4_.refs_1_, ...), custom_call_target="tpu_custom_call" | custom-call | flops 2200000000 | bytes 1048576 | tf_op jit(solution)/shard_map/token_grad/pallas_call | solution.py:1049
  221.9 6.8 %collective-permute-done.32.refs_1_.refs_3_.refs_5_.refs_7_ = bf16[4,192,768]{2,1,0:T(8,128)(2,1)S(1)} collective-permute-done((bf16[4,192,768]{2,1,0:T(8,128)(2,1)S(1)}, bf16[4,192,768]{2,1,0:T(8,128)(2,1)S(1)}, u32[]{:S(2)}, u32[]{:S(2)}) %collective-permute-start.32) | collective-permute-done | bytes 1179680 | tf_op jit(solution)/shard_map/ppermute | solution.py:84
  232.8 8.9 %collective-permute-done.34 = bf16[1,192,768]{2,1,0:T(8,128)(2,1)S(1)} collective-permute-done((bf16[1,192,768]{2,1,0:T(8,128)(2,1)S(1)}, bf16[1,192,768]{2,1,0:T(8,128)(2,1)S(1)}, u32[]{:S(2)}, u32[]{:S(2)}) %collective-permute-start.34) | collective-permute-done | bytes 294944 | tf_op jit(solution)/shard_map/ppermute | solution.py:84
  241.7 6.1 %collective-permute-done.33.refs_1_.refs_3_ = bf16[4,2,112,768]{3,2,1,0:T(8,128)(2,1)S(1)} collective-permute-done((bf16[4,2,112,768]{3,2,1,0:T(8,128)(2,1)S(1)}, bf16[4,2,112,768]{3,2,1,0:T(8,128)(2,1)S(1)}, u32[]{:S(2)}, u32[]{:S(2)}) %collective-permute-start.33) | collective-permute-done | bytes 1376288 | tf_op jit(solution)/shard_map/ppermute | solution.py:84
  255.7 7.6 %collective-permute-done.41 = bf16[1,192,768]{2,1,0:T(8,128)(2,1)S(1)} collective-permute-done((bf16[1,192,768]{2,1,0:T(8,128)(2,1)S(1)}, bf16[1,192,768]{2,1,0:T(8,128)(2,1)S(1)}, u32[]{:S(2)}, u32[]{:S(2)}) %collective-permute-start.41) | collective-permute-done | bytes 294944 | tf_op jit(solution)/shard_map/ppermute | solution.py:84
  271.0 2.5 collective-permute-start.42
  273.6 8.1 %collective-permute-done.38 = bf16[1,112,768]{2,1,0:T(8,128)(2,1)S(1)} collective-permute-done((bf16[1,112,768]{2,1,0:T(8,128)(2,1)S(1)}, bf16[1,112,768]{2,1,0:T(8,128)(2,1)S(1)}, u32[]{:S(2)}, u32[]{:S(2)}) %collective-permute-start.38) | collective-permute-done | bytes 172064 | tf_op jit(solution)/shard_map/ppermute | solution.py:84
  282.1 3.8 %collective-permute-start.39 = (f32[5,768]{1,0:T(8,128)S(1)}, f32[5,768]{1,0:T(8,128)S(1)}, u32[]{:S(2)}, u32[]{:S(2)}) collective-permute-start(f32[5,768]{1,0:T(8,128)S(1)} %slice_bitcast_fusion.2), channel_id=1, source_target_pairs={{1,0},{2,1},{3,2},{4,3},{5,4},{6,5},{7,6},{8,7},{9,8},{10,9},{11,1... | collective-permute-start | bytes 46088 | tf_op jit(solution)/shard_map/ppermute | solution.py:298
  286.0 3.5 %subtract_multiply_fusion = (f32[147624]{0:T(1024)}, f32[147624]{0:T(1024)}, f32[147624]{0:T(1024)}, f32[147624]{0:T(1024)}, f32[147624]{0:T(1024)}) fusion(f32[147624]{0:T(1024)S(1)} %copy-done.34, f32[147624]{0:T(1024)S(1)} %copy-done.31, f32[147624]{0:T(1024)} %param.21, f32[147624]{0:T(1024)} %param.22, f32[]{:T(128)} %bitcast.38, ...), kind=kLoop, calls=%fused_computation.7 | loop fusion | flops 2657232 | bytes 5904968 | tf_op jit(solution)/shard_map/mul | solution.py:1073
  (210 shorter events, 71.9 us)
Async XLA Ops:
  11.0 14.3 %collective-permute-start.3 = (bf16[112,768]{1,0:T(8,128)(2,1)S(1)}, bf16[112,768]{1,0:T(8,128)(2,1)S(1)}, u32[]{:S(2)}, u32[]{:S(2)}) collective-permute-start(bf16[112,768]{1,0:T(8,128)(2,1)S(1)} %constant_dynamic-update-slice_fusion), channel_id=1, source_target_pairs={{0,6},{1,7},{2,0},{3,1},{4,2},{5,3},{6,4},{7,5},{8,14},{9,15},{10,... | collective-permute-start | bytes 516104 | tf_op jit(solution)/shard_map/ppermute | solution.py:84
  11.4 13.9 %collective-permute-start.2 = (bf16[112,768]{1,0:T(8,128)(2,1)S(1)}, bf16[112,768]{1,0:T(8,128)(2,1)S(1)}, u32[]{:S(2)}, u32[]{:S(2)}) collective-permute-start(bf16[112,768]{1,0:T(8,128)(2,1)S(1)} %constant_dynamic-update-slice_fusion), channel_id=1, source_target_pairs={{0,4},{1,5},{2,6},{3,7},{4,0},{5,1},{6,2},{7,3},{8,12},{9,13},{10,... | collective-permute-start | bytes 516104 | tf_op jit(solution)/shard_map/ppermute | solution.py:84
  16.3 10.4 %collective-permute-start.5 = (bf16[5376]{0:T(1024)(128)(2,1)S(1)}, bf16[5376]{0:T(1024)(128)(2,1)S(1)}, u32[]{:S(2)}, u32[]{:S(2)}) collective-permute-start(bf16[5376]{0:T(1024)(128)(2,1)S(1)} %slice.100), channel_id=1, source_target_pairs={{0,1},{1,2},{2,3},{3,4},{4,5},{5,6},{6,7},{7,8},{8,9},{9,10},{10,1... | collective-permute-start | bytes 32264 | tf_op jit(solution)/shard_map/ppermute | solution.py:290
  25.5 10.2 %collective-permute-start.4 = (bf16[400,768]{1,0:T(8,128)(2,1)S(1)}, bf16[400,768]{1,0:T(8,128)(2,1)S(1)}, u32[]{:S(2)}, u32[]{:S(2)}) collective-permute-start(bf16[400,768]{1,0:T(8,128)(2,1)S(1)} %pad_maximum_fusion.1), channel_id=1, source_target_pairs={{0,1},{1,0},{2,3},{3,2},{4,5},{5,4},{6,7},{7,6},{8,24},{9,25},{10,... | collective-permute-start | bytes 1843208 | tf_op jit(solution)/shard_map/ppermute | solution.py:84
  27.5 12.8 %collective-permute-start.6 = (bf16[96,768]{1,0:T(8,128)(2,1)S(1)}, bf16[96,768]{1,0:T(8,128)(2,1)S(1)}, u32[]{:S(2)}, u32[]{:S(2)}) collective-permute-start(bf16[96,768]{1,0:T(8,128)(2,1)S(1)} %get-tuple-element.77.refs_0_), channel_id=1, source_target_pairs={{0,2},{1,3},{2,4},{3,5},{4,6},{5,7},{6,0},{7,1},{8,10},{9,11},{10,... | collective-permute-start | bytes 442376 | tf_op jit(solution)/shard_map/ppermute | solution.py:84
  30.0 12.1 %collective-permute-start.7 = (bf16[96,768]{1,0:T(8,128)(2,1)S(1)}, bf16[96,768]{1,0:T(8,128)(2,1)S(1)}, u32[]{:S(2)}, u32[]{:S(2)}) collective-permute-start(bf16[96,768]{1,0:T(8,128)(2,1)S(1)} %get-tuple-element.77.refs_0_), channel_id=1, source_target_pairs={{0,4},{1,5},{2,6},{3,7},{4,0},{5,1},{6,2},{7,3},{8,12},{9,13},{10,... | collective-permute-start | bytes 442376 | tf_op jit(solution)/shard_map/ppermute | solution.py:84
  32.6 11.5 %collective-permute-start.8 = (bf16[96,768]{1,0:T(8,128)(2,1)S(1)}, bf16[96,768]{1,0:T(8,128)(2,1)S(1)}, u32[]{:S(2)}, u32[]{:S(2)}) collective-permute-start(bf16[96,768]{1,0:T(8,128)(2,1)S(1)} %get-tuple-element.77.refs_0_), channel_id=1, source_target_pairs={{0,6},{1,7},{2,0},{3,1},{4,2},{5,3},{6,4},{7,5},{8,14},{9,15},{10,... | collective-permute-start | bytes 442376 | tf_op jit(solution)/shard_map/ppermute | solution.py:84
  44.1 22.9 %collective-permute-start.9 = (bf16[784,768]{1,0:T(8,128)(2,1)S(1)}, bf16[784,768]{1,0:T(8,128)(2,1)}, u32[]{:S(2)}, u32[]{:S(2)}) collective-permute-start(bf16[784,768]{1,0:T(8,128)(2,1)S(1)} %pad_maximum_fusion.refs_0_), channel_id=1, source_target_pairs={{0,16},{1,17},{2,18},{3,19},{4,20},{5,21},{6,22},{7,23},{8,9},{9,8... | collective-permute-start | bytes 3612680 | tf_op jit(solution)/shard_map/ppermute | solution.py:84
  46.7 17.7 %collective-permute-start.10 = (bf16[384,768]{1,0:T(8,128)(2,1)}, bf16[384,768]{1,0:T(8,128)(2,1)S(1)}, u32[]{:S(2)}, u32[]{:S(2)}) collective-permute-start(bf16[384,768]{1,0:T(8,128)(2,1)} %bitcast.12), channel_id=1, source_target_pairs={{0,1},{1,0},{2,3},{3,2},{4,5},{5,4},{6,7},{7,6},{8,24},{9,25},{10,... | collective-permute-start | bytes 1769480 | tf_op jit(solution)/shard_map/ppermute | solution.py:84
  49.1 11.6 %collective-permute-start.12 = (bf16[96,768]{1,0:T(8,128)(2,1)S(1)}, bf16[96,768]{1,0:T(8,128)(2,1)S(1)}, u32[]{:S(2)}, u32[]{:S(2)}) collective-permute-start(bf16[96,768]{1,0:T(8,128)(2,1)S(1)} %get-tuple-element.79.refs_0_), channel_id=1, source_target_pairs={{0,4},{1,5},{2,6},{3,7},{4,0},{5,1},{6,2},{7,3},{8,12},{9,13},{10,... | collective-permute-start | bytes 442376 | tf_op jit(solution)/shard_map/ppermute | solution.py:84
  50.7 11.5 %collective-permute-start.13 = (bf16[96,768]{1,0:T(8,128)(2,1)S(1)}, bf16[96,768]{1,0:T(8,128)(2,1)S(1)}, u32[]{:S(2)}, u32[]{:S(2)}) collective-permute-start(bf16[96,768]{1,0:T(8,128)(2,1)S(1)} %get-tuple-element.79.refs_0_), channel_id=1, source_target_pairs={{0,6},{1,7},{2,0},{3,1},{4,2},{5,3},{6,4},{7,5},{8,14},{9,15},{10,... | collective-permute-start | bytes 442376 | tf_op jit(solution)/shard_map/ppermute | solution.py:84
  59.1 13.6 %collective-permute-start.14 = (bf16[784,768]{1,0:T(8,128)(2,1)S(1)}, bf16[784,768]{1,0:T(8,128)(2,1)}, u32[]{:S(2)}, u32[]{:S(2)}) collective-permute-start(bf16[784,768]{1,0:T(8,128)(2,1)S(1)} %pad_maximum_fusion.refs_0_), channel_id=1, source_target_pairs={{0,8},{1,9},{2,10},{3,11},{4,12},{5,13},{6,14},{7,15},{8,0},{9,1},... | collective-permute-start | bytes 3612680 | tf_op jit(solution)/shard_map/ppermute | solution.py:84
  67.7 25.6 %collective-permute-start.18 = (bf16[384,768]{1,0:T(8,128)(2,1)}, bf16[384,768]{1,0:T(8,128)(2,1)S(1)}, u32[]{:S(2)}, u32[]{:S(2)}) collective-permute-start(bf16[384,768]{1,0:T(8,128)(2,1)} %bitcast.12), channel_id=1, source_target_pairs={{0,16},{1,17},{2,18},{3,19},{4,20},{5,21},{6,22},{7,23},{8,9},{9,8... | collective-permute-start | bytes 1769480 | tf_op jit(solution)/shard_map/ppermute | solution.py:84
  68.1 25.2 %collective-permute-start.19 = (bf16[384,768]{1,0:T(8,128)(2,1)}, bf16[384,768]{1,0:T(8,128)(2,1)S(1)}, u32[]{:S(2)}, u32[]{:S(2)}) collective-permute-start(bf16[384,768]{1,0:T(8,128)(2,1)} %copy-done.8), channel_id=1, source_target_pairs={{0,16},{1,17},{2,18},{3,19},{4,20},{5,21},{6,22},{7,23},{8,9},{9,8... | collective-permute-start | bytes 1769480 | tf_op jit(solution)/shard_map/ppermute | solution.py:84
  71.1 16.5 %collective-permute-start.17 = (bf16[384,768]{1,0:T(8,128)(2,1)}, bf16[384,768]{1,0:T(8,128)(2,1)S(1)}, u32[]{:S(2)}, u32[]{:S(2)}) collective-permute-start(bf16[384,768]{1,0:T(8,128)(2,1)} %bitcast.75), channel_id=1, source_target_pairs={{0,1},{1,0},{2,3},{3,2},{4,5},{5,4},{6,7},{7,6},{8,24},{9,25},{10,... | collective-permute-start | bytes 1769480 | tf_op jit(solution)/shard_map/ppermute | solution.py:84
  82.4 16.7 %collective-permute-start.23 = (bf16[384,768]{1,0:T(8,128)(2,1)S(1)}, bf16[384,768]{1,0:T(8,128)(2,1)S(1)}, u32[]{:S(2)}, u32[]{:S(2)}) collective-permute-start(bf16[384,768]{1,0:T(8,128)(2,1)S(1)} %bitcast.77), channel_id=1, source_target_pairs={{0,16},{1,17},{2,18},{3,19},{4,20},{5,21},{6,22},{7,23},{8,9},{9,8... | collective-permute-start | bytes 1769480 | tf_op jit(solution)/shard_map/ppermute | solution.py:84
  83.5 25.5 %collective-permute-start.25 = (bf16[384,768]{1,0:T(8,128)(2,1)S(1)}, bf16[384,768]{1,0:T(8,128)(2,1)S(1)}, u32[]{:S(2)}, u32[]{:S(2)}) collective-permute-start(bf16[384,768]{1,0:T(8,128)(2,1)S(1)} %bitcast.78), channel_id=1, source_target_pairs={{0,8},{1,9},{2,10},{3,11},{4,12},{5,13},{6,14},{7,15},{8,0},{9,1},... | collective-permute-start | bytes 1769480 | tf_op jit(solution)/shard_map/ppermute | solution.py:84
  87.5 15.6 %collective-permute-start.24 = (bf16[384,768]{1,0:T(8,128)(2,1)S(1)}, bf16[384,768]{1,0:T(8,128)(2,1)S(1)}, u32[]{:S(2)}, u32[]{:S(2)}) collective-permute-start(bf16[384,768]{1,0:T(8,128)(2,1)S(1)} %collective-permute-done.17.refs_0_), channel_id=1, source_target_pairs={{0,16},{1,17},{2,18},{3,19},{4,20},{5,21},{6,22},{7,23},{8,9},{9,8... | collective-permute-start | bytes 1769480 | tf_op jit(solution)/shard_map/ppermute | solution.py:84
  93.5 10.2 %collective-permute-start.21 = (bf16[384,768]{1,0:T(8,128)(2,1)S(1)}, bf16[384,768]{1,0:T(8,128)(2,1)S(1)}, u32[]{:S(2)}, u32[]{:S(2)}) collective-permute-start(bf16[384,768]{1,0:T(8,128)(2,1)S(1)} %copy-done.9), channel_id=1, source_target_pairs={{0,8},{1,9},{2,10},{3,11},{4,12},{5,13},{6,14},{7,15},{8,0},{9,1},... | collective-permute-start | bytes 1769480 | tf_op jit(solution)/shard_map/ppermute | solution.py:84
  166.1 12.7 %collective-permute-start.29 = (bf16[2,4,2,192,768]{4,3,2,1,0:T(8,128)(2,1)}, bf16[2,4,2,192,768]{4,3,2,1,0:T(8,128)(2,1)S(1)}, u32[]{:S(2)}, u32[]{:S(2)}) collective-permute-start(bf16[2,4,2,192,768]{4,3,2,1,0:T(8,128)(2,1)} %bitcast.72), channel_id=1, source_target_pairs={{0,8},{1,9},{2,10},{3,11},{4,12},{5,13},{6,14},{7,15},{8,0},{9,1},... | collective-permute-start | bytes 14155784 | tf_op jit(solution)/shard_map/ppermute | solution.py:84
  181.9 28.9 %collective-permute-start.30 = (bf16[4,2,192,768]{3,2,1,0:T(8,128)(2,1)S(1)}, bf16[4,2,192,768]{3,2,1,0:T(8,128)(2,1)S(1)}, u32[]{:S(2)}, u32[]{:S(2)}) collective-permute-start(bf16[4,2,192,768]{3,2,1,0:T(8,128)(2,1)S(1)} %get-tuple-element.111.refs_0_), channel_id=1, source_target_pairs={{0,1},{1,0},{2,3},{3,2},{4,5},{5,4},{6,7},{7,6},{8,24},{9,25},{10,... | collective-permute-start | bytes 7077896 | tf_op jit(solution)/shard_map/ppermute | solution.py:84
  207.5 12.2 %collective-permute-start.31 = (bf16[2,4,2,112,768]{4,3,2,1,0:T(8,128)(2,1)S(1)}, bf16[2,4,2,112,768]{4,3,2,1,0:T(8,128)(2,1)S(1)}, u32[]{:S(2)}, u32[]{:S(2)}) collective-permute-start(bf16[2,4,2,112,768]{4,3,2,1,0:T(8,128)(2,1)S(1)} %bitcast.63), channel_id=1, source_target_pairs={{0,8},{1,9},{2,10},{3,11},{4,12},{5,13},{6,14},{7,15},{8,0},{9,1},... | collective-permute-start | bytes 8257544 | tf_op jit(solution)/shard_map/ppermute | solution.py:84
  212.4 16.3 %collective-permute-start.32 = (bf16[4,192,768]{2,1,0:T(8,128)(2,1)S(1)}, bf16[4,192,768]{2,1,0:T(8,128)(2,1)S(1)}, u32[]{:S(2)}, u32[]{:S(2)}) collective-permute-start(bf16[4,192,768]{2,1,0:T(8,128)(2,1)S(1)} %get-tuple-element.120.refs_3_), channel_id=1, source_target_pairs={{0,16},{1,17},{2,18},{3,19},{4,20},{5,21},{6,22},{7,23},{8,9},{9,8... | collective-permute-start | bytes 3538952 | tf_op jit(solution)/shard_map/ppermute | solution.py:84
  229.5 18.4 %collective-permute-start.33 = (bf16[4,2,112,768]{3,2,1,0:T(8,128)(2,1)S(1)}, bf16[4,2,112,768]{3,2,1,0:T(8,128)(2,1)S(1)}, u32[]{:S(2)}, u32[]{:S(2)}) collective-permute-start(bf16[4,2,112,768]{3,2,1,0:T(8,128)(2,1)S(1)} %get-tuple-element.130), channel_id=1, source_target_pairs={{0,1},{1,0},{2,3},{3,2},{4,5},{5,4},{6,7},{7,6},{8,24},{9,25},{10,... | collective-permute-start | bytes 4128776 | tf_op jit(solution)/shard_map/ppermute | solution.py:84
  231.2 10.5 %collective-permute-start.34 = (bf16[1,192,768]{2,1,0:T(8,128)(2,1)S(1)}, bf16[1,192,768]{2,1,0:T(8,128)(2,1)S(1)}, u32[]{:S(2)}, u32[]{:S(2)}) collective-permute-start(bf16[1,192,768]{2,1,0:T(8,128)(2,1)S(1)} %get-tuple-element.128), channel_id=1, source_target_pairs={{0,4},{1,5},{2,6},{3,7},{4,0},{5,1},{6,2},{7,3},{8,12},{9,13},{10,... | collective-permute-start | bytes 884744 | tf_op jit(solution)/shard_map/ppermute | solution.py:84
  249.1 17.7 %collective-permute-start.35 = (bf16[4,112,768]{2,1,0:T(8,128)(2,1)S(1)}, bf16[4,112,768]{2,1,0:T(8,128)(2,1)S(1)}, u32[]{:S(2)}, u32[]{:S(2)}) collective-permute-start(bf16[4,112,768]{2,1,0:T(8,128)(2,1)S(1)} %get-tuple-element.133), channel_id=1, source_target_pairs={{0,16},{1,17},{2,18},{3,19},{4,20},{5,21},{6,22},{7,23},{8,9},{9,8... | collective-permute-start | bytes 2064392 | tf_op jit(solution)/shard_map/ppermute | solution.py:84
  249.8 13.5 %collective-permute-start.41 = (bf16[1,192,768]{2,1,0:T(8,128)(2,1)S(1)}, bf16[1,192,768]{2,1,0:T(8,128)(2,1)S(1)}, u32[]{:S(2)}, u32[]{:S(2)}) collective-permute-start(bf16[1,192,768]{2,1,0:T(8,128)(2,1)S(1)} %get-tuple-element.129), channel_id=1, source_target_pairs={{0,6},{1,7},{2,0},{3,1},{4,2},{5,3},{6,4},{7,5},{8,14},{9,15},{10,... | collective-permute-start | bytes 884744 | tf_op jit(solution)/shard_map/ppermute | solution.py:84
  249.8 14.5 %collective-permute-start.40 = (bf16[1,192,768]{2,1,0:T(8,128)(2,1)S(1)}, bf16[1,192,768]{2,1,0:T(8,128)(2,1)S(1)}, u32[]{:S(2)}, u32[]{:S(2)}) collective-permute-start(bf16[1,192,768]{2,1,0:T(8,128)(2,1)S(1)} %get-tuple-element.127), channel_id=1, source_target_pairs={{0,2},{1,3},{2,4},{3,5},{4,6},{5,7},{6,0},{7,1},{8,10},{9,11},{10,... | collective-permute-start | bytes 884744 | tf_op jit(solution)/shard_map/ppermute | solution.py:84
  267.5 14.2 %collective-permute-start.38 = (bf16[1,112,768]{2,1,0:T(8,128)(2,1)S(1)}, bf16[1,112,768]{2,1,0:T(8,128)(2,1)S(1)}, u32[]{:S(2)}, u32[]{:S(2)}) collective-permute-start(bf16[1,112,768]{2,1,0:T(8,128)(2,1)S(1)} %get-tuple-element.137), channel_id=1, source_target_pairs={{0,6},{1,7},{2,0},{3,1},{4,2},{5,3},{6,4},{7,5},{8,14},{9,15},{10,... | collective-permute-start | bytes 516104 | tf_op jit(solution)/shard_map/ppermute | solution.py:84
  267.9 13.8 %collective-permute-start.37 = (bf16[1,112,768]{2,1,0:T(8,128)(2,1)S(1)}, bf16[1,112,768]{2,1,0:T(8,128)(2,1)S(1)}, u32[]{:S(2)}, u32[]{:S(2)}) collective-permute-start(bf16[1,112,768]{2,1,0:T(8,128)(2,1)S(1)} %get-tuple-element.136), channel_id=1, source_target_pairs={{0,4},{1,5},{2,6},{3,7},{4,0},{5,1},{6,2},{7,3},{8,12},{9,13},{10,... | collective-permute-start | bytes 516104 | tf_op jit(solution)/shard_map/ppermute | solution.py:84
  269.8 12.2 %collective-permute-start.36 = (bf16[1,112,768]{2,1,0:T(8,128)(2,1)S(1)}, bf16[1,112,768]{2,1,0:T(8,128)(2,1)S(1)}, u32[]{:S(2)}, u32[]{:S(2)}) collective-permute-start(bf16[1,112,768]{2,1,0:T(8,128)(2,1)S(1)} %get-tuple-element.135), channel_id=1, source_target_pairs={{0,2},{1,3},{2,4},{3,5},{4,6},{5,7},{6,0},{7,1},{8,10},{9,11},{10,... | collective-permute-start | bytes 516104 | tf_op jit(solution)/shard_map/ppermute | solution.py:84
  271.0 14.8 %collective-permute-start.42 = (f32[7,768]{1,0:T(8,128)S(1)}, f32[7,768]{1,0:T(8,128)S(1)}, u32[]{:S(2)}, u32[]{:S(2)}) collective-permute-start(f32[7,768]{1,0:T(8,128)S(1)} %slice.133), channel_id=1, source_target_pairs={{1,0},{2,1},{3,2},{4,3},{5,4},{6,5},{7,6},{8,7},{9,8},{10,9},{11,1... | collective-permute-start | bytes 64520 | tf_op jit(solution)/shard_map/ppermute | solution.py:298
  (52 other events, 515.2 us)

commit v2 on v1

--- a/solution.py
+++ b/solution.py
@@ -34,14 +34,14 @@
 ATTN_TAIL = 5 * D
 FFN_TAIL = FF + 3 * D
 AHEAD_PAIRS = (2, 2, 2)
-PAIRS = (2, 4)
+PAIRS = (1, 5)
 VEC_ROWS = 16
 COUNT_ROW = 12
 MIB = 1 << 20
 BACK_VMEM = 24 * MIB
 TERMS_VMEM = 24 * MIB
 TOKEN_VMEM = 24 * MIB
-FFN_VMEM = 56 * MIB
+FFN_VMEM = 30 * MIB
 ADD_VMEM = 24 * MIB
 
 
@@ -859,10 +859,6 @@
     up_rows = rows // UP_CHUNKS
     per_chunk = D // rows
 
-    @pl.when(step == 0)
-    def _():
-        hidden_t[...] = hidden[...].T
-
     @pl.when(step >= 2)
     def _():
         pltpu.make_async_copy(block.at[slot], block.at[slot], sem.at[slot]).wait()
@@ -876,32 +872,40 @@
         def _():
             start(give.at[y])
 
-    @pl.when(step < UP_CHUNKS)
+    def down():
+        right = jnp.concatenate([ref[...] for ref in out], 1)
+        block[slot] = dot(activated[...], right, 0, 0).astype(BF)
+        source = block.at[slot].reshape(per_chunk, rows, block.shape[2])
+
+        def start(target):
+            at = pl.ds(lax.rem(step, 2) * per_chunk, per_chunk)
+            pltpu.make_async_copy(source, target.at[at], sem.at[slot]).start()
+
+        to(lax.div(step, 2), 1, start)
+
+    @pl.when(step < UP_CHUNKS - 1)
+    def _():
+        down()
+
+    @pl.when(step == UP_CHUNKS - 1)
+    def _():
+        hidden_t[...] = hidden[...].T
+        down()
+
+    @pl.when(step >= UP_CHUNKS)
     def _():
         right = jnp.concatenate([ref[...] for ref in pre], 1)
         block[slot] = dot(hidden_t[...], right, 1, 0).astype(BF)
+        chunk = step - UP_CHUNKS
         for core in range(2):
             source = block.at[slot, pl.ds(core * (D // 2), D // 2)]
             source = source.reshape(owners, up_rows, block.shape[2])
 
             def start(target):
-                at = pl.ds(pl.multiple_of(step * up_rows, 16), up_rows)
+                at = pl.ds(pl.multiple_of(chunk * up_rows, 16), up_rows)
                 pltpu.make_async_copy(source, target.at[:, at], sem.at[slot]).start()
 
             to(core, 0, start)
-
-    @pl.when(step >= UP_CHUNKS)
-    def _():
-        right = jnp.concatenate([ref[...] for ref in out], 1)
-        block[slot] = dot(activated[...], right, 0, 0).astype(BF)
-        chunk = step - UP_CHUNKS
-        source = block.at[slot].reshape(per_chunk, rows, block.shape[2])
-
-        def start(target):
-            at = pl.ds(lax.rem(chunk, 2) * per_chunk, per_chunk)
-            pltpu.make_async_copy(source, target.at[at], sem.at[slot]).start()
-
-        to(lax.div(chunk, 2), 1, start)
 
     @pl.when(step == pl.num_programs(0) - 1)
     def _():
@@ -917,7 +921,7 @@
     shape = jax.ShapeDtypeStruct((2, owners, rows, width), BF)
 
     def pre_spec(third):
-        return pl.BlockSpec((ROW, WIDTH), lambda i: (0, 3 * jnp.minimum(i, UP_CHUNKS - 1) + third))
+        return pl.BlockSpec((ROW, WIDTH), lambda i: (0, 3 * jnp.maximum(i - UP_CHUNKS, 0) + third))
 
     def out_spec(third):
         return pl.BlockSpec((ROW, WIDTH), lambda i: (0, third))
@@ -932,7 +936,7 @@
         in_specs=[
             pl.BlockSpec(memory_space=pltpu.SMEM),
             pl.BlockSpec((ROW, D), lambda i: (0, 0), pipeline_mode=pl.Buffered(1)),
-            pl.BlockSpec((ROW, D), lambda i: (0, jnp.maximum(i - UP_CHUNKS, 0))),
+            pl.BlockSpec((ROW, D), lambda i: (0, jnp.minimum(i, UP_CHUNKS - 1))),
         ]
         + [pre_spec(t) for t in thirds]
         + [out_spec(t) for t in thirds]
@@ -1281,7 +1285,7 @@
         own_a, cuts_a = ffn_sums.along_z(own_a, order(second_a, cut_c))
         up_z_a = ffn_sums.send_z(cuts_a)
         first_c = attn_sums.send(cut_c, *cuts_a)
-        own_c, cut_c = attn_sums.second(own_c, order(first_c, up_z_a[1]))
+        own_c, cut_c = attn_sums.second(own_c, order(first_c, up_z_a[1], up_z_a[0]))
         second_c = attn_sums.send_second(cut_c)
         own_c, cuts_c = attn_sums.along_z(own_c, second_c)
         up_z_c = attn_sums.send_z(cuts_c)

time: 298 us -> 292 us (0.980)
  starting transfers between devices: 55.7 us -> 59.8 us
  waiting for transfers between devices: 78.3 us -> 74.3 us
    ppermute x39, waiting for transfers between devices: 76.3 us -> 72.3 us  [send(): return lax.ppermute(array, AXES, self.rotation(axis, step))]
    ppermute x2, starting transfers between devices: 6.33 us -> 10.3 us  [to_flat(): lax.ppermute(block[:tail // D], AXES, [(i + 1, i) for i in range(count -...]
    unnamed x84 -> x52, local copies, waits for them, and re-layouts: 11.2 us -> 7.6 us
  transfers between devices with their start and end apart: 43 -> 43, of which waited for: 22 -> 21; matrix products, arithmetic and copies ran while one was open for 3% -> 4% of each run, Pallas kernels for 23% -> 23%
where the time goes in v2:
time: 292 us; the launch traced here: 288 us
  Pallas kernels  126 us (43%)
  waiting for transfers between devices  74.3 us (25%)
  starting transfers between devices  59.8 us (20%)
  local copies, waits for them, and re-layouts  14.5 us (5%)
  other arithmetic  8.81 us (3%)
  between operations  4.97 us (2%)
    ppermute x39, waiting for transfers between devices, send(): return lax.ppermute(array, AXES, self.rotation(axis, step))  72.3 us
    pallas_call x1, Pallas kernels, middle(): pl.pallas_call(functools.partial(middle_kernel, fetch, len(sources)), gri...  37.1 us
    ppermute x39, starting transfers between devices, send(): return lax.ppermute(array, AXES, self.rotation(axis, step))  37.1 us
    pallas_call x2, Pallas kernels, attend_back(): pl.pallas_call(attend_back_kernel, grid=(pairs,), in_specs=attend_specs()...  24.3 us
    pallas_call x1, Pallas kernels, ffn_terms(): pl.pallas_call(kernel, grid=(2 * UP_CHUNKS,), in_specs=[pl.BlockSpec(memo...  15.5 us
    pallas_call x3, Pallas kernels, attend(): pl.pallas_call(attend_kernel, grid=(pairs,), in_specs=attend_specs() + [p...  15.4 us
    ppermute x2, starting transfers between devices, to_rows(): lax.ppermute(flat[-tail:], AXES, [(i, i + 1) for i in range(count - 1)])  12.4 us
    ppermute x2, starting transfers between devices, to_flat(): lax.ppermute(block[:tail // D], AXES, [(i + 1, i) for i in range(count -...  10.3 us
  transfers between devices with their start and end apart: 43, of which 21 were waited for; matrix products, arithmetic and copies ran while one was open for 4% of the time, Pallas kernels for 23%

profile of v2, /device:TPU:8, one launch (start us, length us, event | category | flops | bytes accessed | tf_op | source)
XLA Modules:
  0.0 288.1 jit_solution(1419310485260090956)
XLA Ops:
  1.5 3.4 %collective-permute-start = (bf16[3840]{0:T(1024)(128)(2,1)S(1)}, bf16[3840]{0:T(1024)(128)(2,1)S(1)}, u32[]{:S(2)}, u32[]{:S(2)}) collective-permute-start(bf16[3840]{0:T(1024)(128)(2,1)S(1)} %slice.161), channel_id=1, source_target_pairs={{0,1},{1,2},{2,3},{3,4},{4,5},{5,6},{6,7},{7,8},{8,9},{9,10},{10,1... | collective-permute-start | bytes 23048 | tf_op jit(solution)/shard_map/ppermute | solution.py:290
  11.4 2.6 collective-permute-start.2
  16.3 9.0 %collective-permute-start.5 = (bf16[5376]{0:T(1024)(128)(2,1)S(1)}, bf16[5376]{0:T(1024)(128)(2,1)S(1)}, u32[]{:S(2)}, u32[]{:S(2)}) collective-permute-start(bf16[5376]{0:T(1024)(128)(2,1)S(1)} %slice.100), channel_id=1, source_target_pairs={{0,1},{1,2},{2,3},{3,4},{4,5},{5,6},{6,7},{7,8},{8,9},{9,10},{10,1... | collective-permute-start | bytes 32264 | tf_op jit(solution)/shard_map/ppermute | solution.py:290
  27.5 2.5 collective-permute-start.6
  30.0 2.6 collective-permute-start.7
  35.8 4.5 %collective-permute-done.6.refs_1_ = bf16[96,768]{1,0:T(8,128)(2,1)S(1)} collective-permute-done((bf16[96,768]{1,0:T(8,128)(2,1)S(1)}, bf16[96,768]{1,0:T(8,128)(2,1)S(1)}, u32[]{:S(2)}, u32[]{:S(2)}) %collective-permute-start.6) | collective-permute-done | bytes 147488 | tf_op jit(solution)/shard_map/ppermute | solution.py:84
  52.7 6.5 %collective-permute-done.11.refs_1_ = bf16[96,768]{1,0:T(8,128)(2,1)S(1)} collective-permute-done((bf16[96,768]{1,0:T(8,128)(2,1)S(1)}, bf16[96,768]{1,0:T(8,128)(2,1)S(1)}, u32[]{:S(2)}, u32[]{:S(2)}) %collective-permute-start.11) | collective-permute-done | bytes 147488 | tf_op jit(solution)/shard_map/ppermute | solution.py:84
  64.3 2.7 collective-permute-done.9.refs_1_
  74.9 7.5 %project.1 = (bf16[1024,768]{1,0:T(8,128)(2,1)S(1)}, bf16[1024,768]{1,0:T(8,128)(2,1)S(1)}, bf16[1024,768]{1,0:T(8,128)(2,1)S(1)}, f32[16,768]{1,0:T(8,128)S(1)}, bf16[3072,768]{1,0:T(8,128)(2,1)S(1)}) custom-call(s32[4]{0:T(128)S(1)} %pad_add_fusion.me_ref.me, bf16[1024,768]{1,0:T(8,128)(2,1)S(1)} %copy-done.3, ...), custom_call_target="tpu_custom_call" | custom-call | flops 8800000000 | bytes 1048576 | tf_op jit(solution)/shard_map/project/pallas_call | solution.py:357
  83.4 4.1 %collective-permute-done.17.refs_0_ = bf16[384,768]{1,0:T(8,128)(2,1)S(1)} collective-permute-done((bf16[384,768]{1,0:T(8,128)(2,1)}, bf16[384,768]{1,0:T(8,128)(2,1)S(1)}, u32[]{:S(2)}, u32[]{:S(2)}) %collective-permute-start.17) | collective-permute-done | bytes 589856 | tf_op jit(solution)/shard_map/ppermute | solution.py:84
  88.2 5.1 %attend.3 = (bf16[1024,256]{1,0:T(8,128)(2,1)S(1)}, f32[2,8,1024]{2,1,0:T(8,128)S(1)}) custom-call(s32[1]{0:T(128)} %copy.47.count, s32[1024,1]{1,0:T(8,128)S(1)} %copy.34.seg_column, s32[1,1024]{1,0:T(1,128)S(1)} %bitcast.66, bf16[1024,768]{1,0:T(8,128)(2,1)S(1)} %get-tuple-element.83.query, bf16[1024,768]{1,0:T(8,128)(2,1)S(1)} %get-tuple-element.84.key, ...), custom_call_target="tpu_custom_call" | custom-call | flops 9166666752 | bytes 1048576 | tf_op jit(solution)/shard_map/attend/pallas_call | solution.py:478
  93.9 5.1 %attend.4 = (bf16[1024,256]{1,0:T(8,128)(2,1)S(1)}, f32[2,8,1024]{2,1,0:T(8,128)S(1)}) custom-call(s32[1]{0:T(128)} %copy.47.count, s32[1024,1]{1,0:T(8,128)S(1)} %copy.34.seg_column, s32[1,1024]{1,0:T(1,128)S(1)} %bitcast.67, bf16[1024,768]{1,0:T(8,128)(2,1)S(1)} %get-tuple-element.83.query, bf16[1024,768]{1,0:T(8,128)(2,1)S(1)} %get-tuple-element.84.key, ...), custom_call_target="tpu_custom_call" | custom-call | flops 9166666752 | bytes 1048576 | tf_op jit(solution)/shard_map/attend/pallas_call | solution.py:478
  99.2 3.9 %collective-permute-done.24 = bf16[384,768]{1,0:T(8,128)(2,1)S(1)} collective-permute-done((bf16[384,768]{1,0:T(8,128)(2,1)S(1)}, bf16[384,768]{1,0:T(8,128)(2,1)S(1)}, u32[]{:S(2)}, u32[]{:S(2)}) %collective-permute-start.24) | collective-permute-done | bytes 589856 | tf_op jit(solution)/shard_map/ppermute | solution.py:84
  103.8 5.1 %attend.5 = (bf16[1024,256]{1,0:T(8,128)(2,1)S(1)}, f32[2,8,1024]{2,1,0:T(8,128)S(1)}) custom-call(s32[1]{0:T(128)} %copy.47.count, s32[1024,1]{1,0:T(8,128)S(1)} %copy.34.seg_column, s32[1,1024]{1,0:T(1,128)S(1)} %bitcast.68, bf16[1024,768]{1,0:T(8,128)(2,1)S(1)} %get-tuple-element.83.query, bf16[1024,768]{1,0:T(8,128)(2,1)S(1)} %get-tuple-element.84.key, ...), custom_call_target="tpu_custom_call" | custom-call | flops 9166666752 | bytes 1048576 | tf_op jit(solution)/shard_map/attend/pallas_call | solution.py:478
  109.0 37.1 %middle.1 = (bf16[1024,768]{1,0:T(8,128)(2,1)}, bf16[1024,768]{1,0:T(8,128)(2,1)S(1)}, bf16[1024,3072]{1,0:T(8,128)(2,1)}, bf16[1024,3072]{1,0:T(8,128)(2,1)}, b...) custom-call(s32[1]{0:T(128)} %copy.47.count, ...), custom_call_target="tpu_custom_call" | custom-call | flops 44000002048 | bytes 1048576 | tf_op jit(solution)/shard_map/middle/pallas_call | solution.py:809
  146.1 2.8 copy-done.11
  148.9 15.5 %ffn_terms.1 = (bf16[2,8,192,768]{3,2,1,0:T(8,128)(2,1)S(1)}, bf16[2,8,192,768]{3,2,1,0:T(8,128)(2,1)S(1)}) custom-call(s32[4]{0:T(128)S(1)} %pad_add_fusion.me_ref.me, bf16[1024,768]{1,0:T(8,128)(2,1)S(1)} %get-tuple-element.103.hidden_ref, bf16[1024,3072]{1,0:T(8,128)(2,1)S(1)} %copy-done.11, ...), custom_call_target="tpu_custom_call" | custom-call | flops 16499999744 | bytes 1048576 | tf_op jit(solution)/shard_map/ffn_terms/pallas_call | solution.py:933
  165.0 4.0 %attend_back.2 = (bf16[3,1024,128]{2,1,0:T(8,128)(2,1)S(1)}, f32[8,128]{1,0:T(8,128)S(1)}) custom-call(s32[1]{0:T(128)} %copy.47.count, s32[1024,1]{1,0:T(8,128)S(1)} %copy.34.seg_column, s32[1,1024]{1,0:T(1,128)S(1)} %bitcast.70, bf16[1024,768]{1,0:T(8,128)(2,1)S(1)} %get-tuple-element.83.query, bf16[1024,768]{1,0:T(8,128)(2,1)S(1)} %get-tuple-element.84.key, ...), custom_call_target="tpu_custom_call" | custom-call | flops 13200000000 | bytes 1048576 | tf_op jit(solution)/shard_map/attend_back/pallas_call | solution.py:554
  168.9 3.5 %collective-permute-done.29.refs_1_.refs_3_ = bf16[2,4,2,192,768]{4,3,2,1,0:T(8,128)(2,1)S(1)} collective-permute-done((bf16[2,4,2,192,768]{4,3,2,1,0:T(8,128)(2,1)S(1)}, bf16[2,4,2,192,768]{4,3,2,1,0:T(8,128)(2,1)S(1)}, u32[]{:S(2)}, u32[]{:S(2)}) %collective-permute-start.29) | collective-permute-done | bytes 4718624 | tf_op jit(solution)/shard_map/ppermute | solution.py:84
  172.4 3.0 %add_routed.6 = (bf16[4,2,192,768]{3,2,1,0:T(8,128)(2,1)S(1)}, bf16[4,2,192,768]{3,2,1,0:T(8,128)(2,1)S(1)}) custom-call(s32[4]{0:T(128)S(1)} %pad_add_fusion.me_ref.me, bf16[2,4,2,192,768]{4,3,2,1,0:T(8,128)(2,1)S(1)} %bitcast.92, bf16[2,4,2,192,768]{4,3,2,1,0:T(8,128)(2,1)S(1)} %collective-permute-done.29.refs_1_.refs_3_, ...), custom_call_target="tpu_custom_call" | custom-call | flops 5280000000 | bytes 1048576 | tf_op jit(solution)/shard_map/add_routed/pallas_call | solution.py:188
  177.2 20.3 %attend_back.3 = (bf16[3,1024,640]{2,1,0:T(8,128)(2,1)S(1)}, f32[8,640]{1,0:T(8,128)S(1)}) custom-call(s32[1]{0:T(128)} %copy.47.count, s32[1024,1]{1,0:T(8,128)S(1)} %copy.34.seg_column, s32[1,1024]{1,0:T(1,128)S(1)} %bitcast.71, bf16[1024,768]{1,0:T(8,128)(2,1)S(1)} %get-tuple-element.83.query, bf16[1024,768]{1,0:T(8,128)(2,1)S(1)} %get-tuple-element.84.key, ...), custom_call_target="tpu_custom_call" | custom-call | flops 16499999744 | bytes 1048576 | tf_op jit(solution)/shard_map/attend_back/pallas_call | solution.py:554
  197.6 7.3 %attn_terms.1 = (bf16[2,8,112,768]{3,2,1,0:T(8,128)(2,1)S(1)}, bf16[2,8,112,768]{3,2,1,0:T(8,128)(2,1)S(1)}) custom-call(s32[4]{0:T(128)S(1)} %pad_add_fusion.me_ref.me, bf16[1024,768]{1,0:T(8,128)(2,1)S(1)} %copy-done.4, f32[16,768]{1,0:T(8,128)S(1)} %fusion.7.vectors_ref, bf16[1024,768]{1,0:T(8,128)(2,1)S(1)} %copy-done.12, ...), custom_call_target="tpu_custom_call" | custom-call | flops 6600000000 | bytes 1048576 | tf_op jit(solution)/shard_map/attn_terms/pallas_call | solution.py:1014
  208.3 5.7 %token_grad.1 = bf16[1024,768]{1,0:T(8,128)(2,1)} custom-call(f32[1024,768]{1,0:T(8,128)S(1)} %copy-done.1, bf16[3072,768]{1,0:T(8,128)(2,1)S(1)} %bitcast.62, bf16[3,1024,128]{2,1,0:T(8,128)(2,1)S(1)} %get-tuple-element.108.refs_3_.refs_0_, bf16[3,1024,640]{2,1,0:T(8,128)(2,1)S(1)} %get-tuple-element.112.refs_4_.refs_1_, ...), custom_call_target="tpu_custom_call" | custom-call | flops 2200000000 | bytes 1048576 | tf_op jit(solution)/shard_map/token_grad/pallas_call | solution.py:1053
  216.2 6.7 %collective-permute-done.32.refs_1_.refs_3_.refs_5_.refs_7_ = bf16[4,192,768]{2,1,0:T(8,128)(2,1)S(1)} collective-permute-done((bf16[4,192,768]{2,1,0:T(8,128)(2,1)S(1)}, bf16[4,192,768]{2,1,0:T(8,128)(2,1)S(1)}, u32[]{:S(2)}, u32[]{:S(2)}) %collective-permute-start.32) | collective-permute-done | bytes 1179680 | tf_op jit(solution)/shard_map/ppermute | solution.py:84
  226.4 11.0 %collective-permute-done.34 = bf16[1,192,768]{2,1,0:T(8,128)(2,1)S(1)} collective-permute-done((bf16[1,192,768]{2,1,0:T(8,128)(2,1)S(1)}, bf16[1,192,768]{2,1,0:T(8,128)(2,1)S(1)}, u32[]{:S(2)}, u32[]{:S(2)}) %collective-permute-start.34) | collective-permute-done | bytes 294944 | tf_op jit(solution)/shard_map/ppermute | solution.py:84
  237.4 6.2 %collective-permute-done.35 = bf16[1,192,768]{2,1,0:T(8,128)(2,1)S(1)} collective-permute-done((bf16[1,192,768]{2,1,0:T(8,128)(2,1)S(1)}, bf16[1,192,768]{2,1,0:T(8,128)(2,1)S(1)}, u32[]{:S(2)}, u32[]{:S(2)}) %collective-permute-start.35) | collective-permute-done | bytes 294944 | tf_op jit(solution)/shard_map/ppermute | solution.py:84
  251.8 3.2 %collective-permute-done.41 = bf16[1,192,768]{2,1,0:T(8,128)(2,1)S(1)} collective-permute-done((bf16[1,192,768]{2,1,0:T(8,128)(2,1)S(1)}, bf16[1,192,768]{2,1,0:T(8,128)(2,1)S(1)}, u32[]{:S(2)}, u32[]{:S(2)}) %collective-permute-start.41) | collective-permute-done | bytes 294944 | tf_op jit(solution)/shard_map/ppermute | solution.py:84
  260.2 3.2 %collective-permute-start.38 = (bf16[1,112,768]{2,1,0:T(8,128)(2,1)S(1)}, bf16[1,112,768]{2,1,0:T(8,128)(2,1)S(1)}, u32[]{:S(2)}, u32[]{:S(2)}) collective-permute-start(bf16[1,112,768]{2,1,0:T(8,128)(2,1)S(1)} %get-tuple-element.136), channel_id=1, source_target_pairs={{0,4},{1,5},{2,6},{3,7},{4,0},{5,1},{6,2},{7,3},{8,12},{9,13},{10,... | collective-permute-start | bytes 516104 | tf_op jit(solution)/shard_map/ppermute | solution.py:84
  263.9 4.3 %collective-permute-start.42 = (f32[7,768]{1,0:T(8,128)S(1)}, f32[7,768]{1,0:T(8,128)S(1)}, u32[]{:S(2)}, u32[]{:S(2)}) collective-permute-start(f32[7,768]{1,0:T(8,128)S(1)} %slice.133), channel_id=1, source_target_pairs={{1,0},{2,1},{3,2},{4,3},{5,4},{6,5},{7,6},{8,7},{9,8},{10,9},{11,1... | collective-permute-start | bytes 64520 | tf_op jit(solution)/shard_map/ppermute | solution.py:298
  268.2 6.5 %collective-permute-done.39 = bf16[1,112,768]{2,1,0:T(8,128)(2,1)S(1)} collective-permute-done((bf16[1,112,768]{2,1,0:T(8,128)(2,1)S(1)}, bf16[1,112,768]{2,1,0:T(8,128)(2,1)S(1)}, u32[]{:S(2)}, u32[]{:S(2)}) %collective-permute-start.39) | collective-permute-done | bytes 172064 | tf_op jit(solution)/shard_map/ppermute | solution.py:84
  275.5 6.0 %collective-permute-start.40 = (f32[5,768]{1,0:T(8,128)S(1)}, f32[5,768]{1,0:T(8,128)S(1)}, u32[]{:S(2)}, u32[]{:S(2)}) collective-permute-start(f32[5,768]{1,0:T(8,128)S(1)} %slice_bitcast_fusion.2), channel_id=1, source_target_pairs={{1,0},{2,1},{3,2},{4,3},{5,4},{6,5},{7,6},{8,7},{9,8},{10,9},{11,1... | collective-permute-start | bytes 46088 | tf_op jit(solution)/shard_map/ppermute | solution.py:298
  281.6 3.5 %subtract_multiply_fusion = (f32[147624]{0:T(1024)}, f32[147624]{0:T(1024)}, f32[147624]{0:T(1024)}, f32[147624]{0:T(1024)}, f32[147624]{0:T(1024)}) fusion(f32[147624]{0:T(1024)S(1)} %copy-done.18, f32[147624]{0:T(1024)S(1)} %copy-done.15, f32[147624]{0:T(1024)} %param.21, f32[147624]{0:T(1024)} %param.22, f32[]{:T(128)} %bitcast.38, ...), kind=kLoop, calls=%fused_computation.7 | loop fusion | flops 2657232 | bytes 5904968 | tf_op jit(solution)/shard_map/mul | solution.py:1077
  (178 shorter events, 68.6 us)
Async XLA Ops:
  11.0 14.3 %collective-permute-start.3 = (bf16[112,768]{1,0:T(8,128)(2,1)S(1)}, bf16[112,768]{1,0:T(8,128)(2,1)S(1)}, u32[]{:S(2)}, u32[]{:S(2)}) collective-permute-start(bf16[112,768]{1,0:T(8,128)(2,1)S(1)} %constant_dynamic-update-slice_fusion), channel_id=1, source_target_pairs={{0,6},{1,7},{2,0},{3,1},{4,2},{5,3},{6,4},{7,5},{8,14},{9,15},{10,... | collective-permute-start | bytes 516104 | tf_op jit(solution)/shard_map/ppermute | solution.py:84
  11.4 13.9 %collective-permute-start.2 = (bf16[112,768]{1,0:T(8,128)(2,1)S(1)}, bf16[112,768]{1,0:T(8,128)(2,1)S(1)}, u32[]{:S(2)}, u32[]{:S(2)}) collective-permute-start(bf16[112,768]{1,0:T(8,128)(2,1)S(1)} %constant_dynamic-update-slice_fusion), channel_id=1, source_target_pairs={{0,4},{1,5},{2,6},{3,7},{4,0},{5,1},{6,2},{7,3},{8,12},{9,13},{10,... | collective-permute-start | bytes 516104 | tf_op jit(solution)/shard_map/ppermute | solution.py:84
  16.3 10.4 %collective-permute-start.5 = (bf16[5376]{0:T(1024)(128)(2,1)S(1)}, bf16[5376]{0:T(1024)(128)(2,1)S(1)}, u32[]{:S(2)}, u32[]{:S(2)}) collective-permute-start(bf16[5376]{0:T(1024)(128)(2,1)S(1)} %slice.100), channel_id=1, source_target_pairs={{0,1},{1,2},{2,3},{3,4},{4,5},{5,6},{6,7},{7,8},{8,9},{9,10},{10,1... | collective-permute-start | bytes 32264 | tf_op jit(solution)/shard_map/ppermute | solution.py:290
  25.5 10.2 %collective-permute-start.4 = (bf16[400,768]{1,0:T(8,128)(2,1)S(1)}, bf16[400,768]{1,0:T(8,128)(2,1)S(1)}, u32[]{:S(2)}, u32[]{:S(2)}) collective-permute-start(bf16[400,768]{1,0:T(8,128)(2,1)S(1)} %pad_maximum_fusion.1), channel_id=1, source_target_pairs={{0,1},{1,0},{2,3},{3,2},{4,5},{5,4},{6,7},{7,6},{8,24},{9,25},{10,... | collective-permute-start | bytes 1843208 | tf_op jit(solution)/shard_map/ppermute | solution.py:84
  27.5 12.8 %collective-permute-start.6 = (bf16[96,768]{1,0:T(8,128)(2,1)S(1)}, bf16[96,768]{1,0:T(8,128)(2,1)S(1)}, u32[]{:S(2)}, u32[]{:S(2)}) collective-permute-start(bf16[96,768]{1,0:T(8,128)(2,1)S(1)} %get-tuple-element.77.refs_0_), channel_id=1, source_target_pairs={{0,2},{1,3},{2,4},{3,5},{4,6},{5,7},{6,0},{7,1},{8,10},{9,11},{10,... | collective-permute-start | bytes 442376 | tf_op jit(solution)/shard_map/ppermute | solution.py:84
  30.0 12.1 %collective-permute-start.7 = (bf16[96,768]{1,0:T(8,128)(2,1)S(1)}, bf16[96,768]{1,0:T(8,128)(2,1)S(1)}, u32[]{:S(2)}, u32[]{:S(2)}) collective-permute-start(bf16[96,768]{1,0:T(8,128)(2,1)S(1)} %get-tuple-element.77.refs_0_), channel_id=1, source_target_pairs={{0,4},{1,5},{2,6},{3,7},{4,0},{5,1},{6,2},{7,3},{8,12},{9,13},{10,... | collective-permute-start | bytes 442376 | tf_op jit(solution)/shard_map/ppermute | solution.py:84
  32.6 11.5 %collective-permute-start.8 = (bf16[96,768]{1,0:T(8,128)(2,1)S(1)}, bf16[96,768]{1,0:T(8,128)(2,1)S(1)}, u32[]{:S(2)}, u32[]{:S(2)}) collective-permute-start(bf16[96,768]{1,0:T(8,128)(2,1)S(1)} %get-tuple-element.77.refs_0_), channel_id=1, source_target_pairs={{0,6},{1,7},{2,0},{3,1},{4,2},{5,3},{6,4},{7,5},{8,14},{9,15},{10,... | collective-permute-start | bytes 442376 | tf_op jit(solution)/shard_map/ppermute | solution.py:84
  44.1 22.9 %collective-permute-start.9 = (bf16[784,768]{1,0:T(8,128)(2,1)S(1)}, bf16[784,768]{1,0:T(8,128)(2,1)}, u32[]{:S(2)}, u32[]{:S(2)}) collective-permute-start(bf16[784,768]{1,0:T(8,128)(2,1)S(1)} %pad_maximum_fusion.refs_0_), channel_id=1, source_target_pairs={{0,16},{1,17},{2,18},{3,19},{4,20},{5,21},{6,22},{7,23},{8,9},{9,8... | collective-permute-start | bytes 3612680 | tf_op jit(solution)/shard_map/ppermute | solution.py:84
  46.7 17.7 %collective-permute-start.10 = (bf16[384,768]{1,0:T(8,128)(2,1)}, bf16[384,768]{1,0:T(8,128)(2,1)S(1)}, u32[]{:S(2)}, u32[]{:S(2)}) collective-permute-start(bf16[384,768]{1,0:T(8,128)(2,1)} %bitcast.12), channel_id=1, source_target_pairs={{0,1},{1,0},{2,3},{3,2},{4,5},{5,4},{6,7},{7,6},{8,24},{9,25},{10,... | collective-permute-start | bytes 1769480 | tf_op jit(solution)/shard_map/ppermute | solution.py:84
  49.1 10.1 %collective-permute-start.11 = (bf16[96,768]{1,0:T(8,128)(2,1)S(1)}, bf16[96,768]{1,0:T(8,128)(2,1)S(1)}, u32[]{:S(2)}, u32[]{:S(2)}) collective-permute-start(bf16[96,768]{1,0:T(8,128)(2,1)S(1)} %get-tuple-element.79.refs_0_), channel_id=1, source_target_pairs={{0,2},{1,3},{2,4},{3,5},{4,6},{5,7},{6,0},{7,1},{8,10},{9,11},{10,... | collective-permute-start | bytes 442376 | tf_op jit(solution)/shard_map/ppermute | solution.py:84
  49.1 11.6 %collective-permute-start.12 = (bf16[96,768]{1,0:T(8,128)(2,1)S(1)}, bf16[96,768]{1,0:T(8,128)(2,1)S(1)}, u32[]{:S(2)}, u32[]{:S(2)}) collective-permute-start(bf16[96,768]{1,0:T(8,128)(2,1)S(1)} %get-tuple-element.79.refs_0_), channel_id=1, source_target_pairs={{0,4},{1,5},{2,6},{3,7},{4,0},{5,1},{6,2},{7,3},{8,12},{9,13},{10,... | collective-permute-start | bytes 442376 | tf_op jit(solution)/shard_map/ppermute | solution.py:84
  50.7 11.5 %collective-permute-start.13 = (bf16[96,768]{1,0:T(8,128)(2,1)S(1)}, bf16[96,768]{1,0:T(8,128)(2,1)S(1)}, u32[]{:S(2)}, u32[]{:S(2)}) collective-permute-start(bf16[96,768]{1,0:T(8,128)(2,1)S(1)} %get-tuple-element.79.refs_0_), channel_id=1, source_target_pairs={{0,6},{1,7},{2,0},{3,1},{4,2},{5,3},{6,4},{7,5},{8,14},{9,15},{10,... | collective-permute-start | bytes 442376 | tf_op jit(solution)/shard_map/ppermute | solution.py:84
  59.1 13.6 %collective-permute-start.14 = (bf16[784,768]{1,0:T(8,128)(2,1)S(1)}, bf16[784,768]{1,0:T(8,128)(2,1)}, u32[]{:S(2)}, u32[]{:S(2)}) collective-permute-start(bf16[784,768]{1,0:T(8,128)(2,1)S(1)} %pad_maximum_fusion.refs_0_), channel_id=1, source_target_pairs={{0,8},{1,9},{2,10},{3,11},{4,12},{5,13},{6,14},{7,15},{8,0},{9,1},... | collective-permute-start | bytes 3612680 | tf_op jit(solution)/shard_map/ppermute | solution.py:84
  67.7 25.6 %collective-permute-start.18 = (bf16[384,768]{1,0:T(8,128)(2,1)}, bf16[384,768]{1,0:T(8,128)(2,1)S(1)}, u32[]{:S(2)}, u32[]{:S(2)}) collective-permute-start(bf16[384,768]{1,0:T(8,128)(2,1)} %bitcast.12), channel_id=1, source_target_pairs={{0,16},{1,17},{2,18},{3,19},{4,20},{5,21},{6,22},{7,23},{8,9},{9,8... | collective-permute-start | bytes 1769480 | tf_op jit(solution)/shard_map/ppermute | solution.py:84
  68.1 25.2 %collective-permute-start.19 = (bf16[384,768]{1,0:T(8,128)(2,1)}, bf16[384,768]{1,0:T(8,128)(2,1)S(1)}, u32[]{:S(2)}, u32[]{:S(2)}) collective-permute-start(bf16[384,768]{1,0:T(8,128)(2,1)} %copy-done.5), channel_id=1, source_target_pairs={{0,16},{1,17},{2,18},{3,19},{4,20},{5,21},{6,22},{7,23},{8,9},{9,8... | collective-permute-start | bytes 1769480 | tf_op jit(solution)/shard_map/ppermute | solution.py:84
  71.1 16.5 %collective-permute-start.17 = (bf16[384,768]{1,0:T(8,128)(2,1)}, bf16[384,768]{1,0:T(8,128)(2,1)S(1)}, u32[]{:S(2)}, u32[]{:S(2)}) collective-permute-start(bf16[384,768]{1,0:T(8,128)(2,1)} %bitcast.75), channel_id=1, source_target_pairs={{0,1},{1,0},{2,3},{3,2},{4,5},{5,4},{6,7},{7,6},{8,24},{9,25},{10,... | collective-permute-start | bytes 1769480 | tf_op jit(solution)/shard_map/ppermute | solution.py:84
  82.4 16.7 %collective-permute-start.23 = (bf16[384,768]{1,0:T(8,128)(2,1)S(1)}, bf16[384,768]{1,0:T(8,128)(2,1)S(1)}, u32[]{:S(2)}, u32[]{:S(2)}) collective-permute-start(bf16[384,768]{1,0:T(8,128)(2,1)S(1)} %bitcast.77), channel_id=1, source_target_pairs={{0,16},{1,17},{2,18},{3,19},{4,20},{5,21},{6,22},{7,23},{8,9},{9,8... | collective-permute-start | bytes 1769480 | tf_op jit(solution)/shard_map/ppermute | solution.py:84
  83.4 25.5 %collective-permute-start.25 = (bf16[384,768]{1,0:T(8,128)(2,1)S(1)}, bf16[384,768]{1,0:T(8,128)(2,1)S(1)}, u32[]{:S(2)}, u32[]{:S(2)}) collective-permute-start(bf16[384,768]{1,0:T(8,128)(2,1)S(1)} %bitcast.78), channel_id=1, source_target_pairs={{0,8},{1,9},{2,10},{3,11},{4,12},{5,13},{6,14},{7,15},{8,0},{9,1},... | collective-permute-start | bytes 1769480 | tf_op jit(solution)/shard_map/ppermute | solution.py:84
  87.5 15.6 %collective-permute-start.24 = (bf16[384,768]{1,0:T(8,128)(2,1)S(1)}, bf16[384,768]{1,0:T(8,128)(2,1)S(1)}, u32[]{:S(2)}, u32[]{:S(2)}) collective-permute-start(bf16[384,768]{1,0:T(8,128)(2,1)S(1)} %collective-permute-done.17.refs_0_), channel_id=1, source_target_pairs={{0,16},{1,17},{2,18},{3,19},{4,20},{5,21},{6,22},{7,23},{8,9},{9,8... | collective-permute-start | bytes 1769480 | tf_op jit(solution)/shard_map/ppermute | solution.py:84
  93.3 9.9 %collective-permute-start.20 = (bf16[384,768]{1,0:T(8,128)(2,1)S(1)}, bf16[384,768]{1,0:T(8,128)(2,1)S(1)}, u32[]{:S(2)}, u32[]{:S(2)}) collective-permute-start(bf16[384,768]{1,0:T(8,128)(2,1)S(1)} %collective-permute-done.18), channel_id=1, source_target_pairs={{0,8},{1,9},{2,10},{3,11},{4,12},{5,13},{6,14},{7,15},{8,0},{9,1},... | collective-permute-start | bytes 1769480 | tf_op jit(solution)/shard_map/ppermute | solution.py:84
  93.5 10.2 %collective-permute-start.21 = (bf16[384,768]{1,0:T(8,128)(2,1)S(1)}, bf16[384,768]{1,0:T(8,128)(2,1)S(1)}, u32[]{:S(2)}, u32[]{:S(2)}) collective-permute-start(bf16[384,768]{1,0:T(8,128)(2,1)S(1)} %copy-done.6), channel_id=1, source_target_pairs={{0,8},{1,9},{2,10},{3,11},{4,12},{5,13},{6,14},{7,15},{8,0},{9,1},... | collective-permute-start | bytes 1769480 | tf_op jit(solution)/shard_map/ppermute | solution.py:84
  99.1 9.9 %collective-permute-start.27 = (bf16[384,768]{1,0:T(8,128)(2,1)S(1)}, bf16[384,768]{1,0:T(8,128)(2,1)S(1)}, u32[]{:S(2)}, u32[]{:S(2)}) collective-permute-start(bf16[384,768]{1,0:T(8,128)(2,1)S(1)} %collective-permute-done.17.refs_0_), channel_id=1, source_target_pairs={{0,8},{1,9},{2,10},{3,11},{4,12},{5,13},{6,14},{7,15},{8,0},{9,1},... | collective-permute-start | bytes 1769480 | tf_op jit(solution)/shard_map/ppermute | solution.py:84
  175.4 29.6 %collective-permute-start.30 = (bf16[4,2,192,768]{3,2,1,0:T(8,128)(2,1)S(1)}, bf16[4,2,192,768]{3,2,1,0:T(8,128)(2,1)S(1)}, u32[]{:S(2)}, u32[]{:S(2)}) collective-permute-start(bf16[4,2,192,768]{3,2,1,0:T(8,128)(2,1)S(1)} %get-tuple-element.111.refs_0_), channel_id=1, source_target_pairs={{0,1},{1,0},{2,3},{3,2},{4,5},{5,4},{6,7},{7,6},{8,24},{9,25},{10,... | collective-permute-start | bytes 7077896 | tf_op jit(solution)/shard_map/ppermute | solution.py:84
  206.6 16.3 %collective-permute-start.32 = (bf16[4,192,768]{2,1,0:T(8,128)(2,1)S(1)}, bf16[4,192,768]{2,1,0:T(8,128)(2,1)S(1)}, u32[]{:S(2)}, u32[]{:S(2)}) collective-permute-start(bf16[4,192,768]{2,1,0:T(8,128)(2,1)S(1)} %get-tuple-element.120.refs_3_), channel_id=1, source_target_pairs={{0,16},{1,17},{2,18},{3,19},{4,20},{5,21},{6,22},{7,23},{8,9},{9,8... | collective-permute-start | bytes 3538952 | tf_op jit(solution)/shard_map/ppermute | solution.py:84
  223.7 19.9 %collective-permute-start.33 = (bf16[4,2,112,768]{3,2,1,0:T(8,128)(2,1)S(1)}, bf16[4,2,112,768]{3,2,1,0:T(8,128)(2,1)S(1)}, u32[]{:S(2)}, u32[]{:S(2)}) collective-permute-start(bf16[4,2,112,768]{3,2,1,0:T(8,128)(2,1)S(1)} %get-tuple-element.130), channel_id=1, source_target_pairs={{0,1},{1,0},{2,3},{3,2},{4,5},{5,4},{6,7},{7,6},{8,24},{9,25},{10,... | collective-permute-start | bytes 4128776 | tf_op jit(solution)/shard_map/ppermute | solution.py:84
  224.8 12.6 %collective-permute-start.34 = (bf16[1,192,768]{2,1,0:T(8,128)(2,1)S(1)}, bf16[1,192,768]{2,1,0:T(8,128)(2,1)S(1)}, u32[]{:S(2)}, u32[]{:S(2)}) collective-permute-start(bf16[1,192,768]{2,1,0:T(8,128)(2,1)S(1)} %get-tuple-element.128), channel_id=1, source_target_pairs={{0,4},{1,5},{2,6},{3,7},{4,0},{5,1},{6,2},{7,3},{8,12},{9,13},{10,... | collective-permute-start | bytes 884744 | tf_op jit(solution)/shard_map/ppermute | solution.py:84
  226.3 17.4 %collective-permute-start.35 = (bf16[1,192,768]{2,1,0:T(8,128)(2,1)S(1)}, bf16[1,192,768]{2,1,0:T(8,128)(2,1)S(1)}, u32[]{:S(2)}, u32[]{:S(2)}) collective-permute-start(bf16[1,192,768]{2,1,0:T(8,128)(2,1)S(1)} %get-tuple-element.127), channel_id=1, source_target_pairs={{0,2},{1,3},{2,4},{3,5},{4,6},{5,7},{6,0},{7,1},{8,10},{9,11},{10,... | collective-permute-start | bytes 884744 | tf_op jit(solution)/shard_map/ppermute | solution.py:84
  244.9 14.5 %collective-permute-start.36 = (bf16[4,112,768]{2,1,0:T(8,128)(2,1)S(1)}, bf16[4,112,768]{2,1,0:T(8,128)(2,1)S(1)}, u32[]{:S(2)}, u32[]{:S(2)}) collective-permute-start(bf16[4,112,768]{2,1,0:T(8,128)(2,1)S(1)} %get-tuple-element.133), channel_id=1, source_target_pairs={{0,16},{1,17},{2,18},{3,19},{4,20},{5,21},{6,22},{7,23},{8,9},{9,8... | collective-permute-start | bytes 2064392 | tf_op jit(solution)/shard_map/ppermute | solution.py:84
  260.1 14.6 %collective-permute-start.39 = (bf16[1,112,768]{2,1,0:T(8,128)(2,1)S(1)}, bf16[1,112,768]{2,1,0:T(8,128)(2,1)S(1)}, u32[]{:S(2)}, u32[]{:S(2)}) collective-permute-start(bf16[1,112,768]{2,1,0:T(8,128)(2,1)S(1)} %get-tuple-element.137), channel_id=1, source_target_pairs={{0,6},{1,7},{2,0},{3,1},{4,2},{5,3},{6,4},{7,5},{8,14},{9,15},{10,... | collective-permute-start | bytes 516104 | tf_op jit(solution)/shard_map/ppermute | solution.py:84
  260.2 14.5 %collective-permute-start.38 = (bf16[1,112,768]{2,1,0:T(8,128)(2,1)S(1)}, bf16[1,112,768]{2,1,0:T(8,128)(2,1)S(1)}, u32[]{:S(2)}, u32[]{:S(2)}) collective-permute-start(bf16[1,112,768]{2,1,0:T(8,128)(2,1)S(1)} %get-tuple-element.136), channel_id=1, source_target_pairs={{0,4},{1,5},{2,6},{3,7},{4,0},{5,1},{6,2},{7,3},{8,12},{9,13},{10,... | collective-permute-start | bytes 516104 | tf_op jit(solution)/shard_map/ppermute | solution.py:84
  263.4 12.0 %collective-permute-start.37 = (bf16[1,112,768]{2,1,0:T(8,128)(2,1)S(1)}, bf16[1,112,768]{2,1,0:T(8,128)(2,1)S(1)}, u32[]{:S(2)}, u32[]{:S(2)}) collective-permute-start(bf16[1,112,768]{2,1,0:T(8,128)(2,1)S(1)} %get-tuple-element.135), channel_id=1, source_target_pairs={{0,2},{1,3},{2,4},{3,5},{4,6},{5,7},{6,0},{7,1},{8,10},{9,11},{10,... | collective-permute-start | bytes 516104 | tf_op jit(solution)/shard_map/ppermute | solution.py:84
  263.9 17.6 %collective-permute-start.42 = (f32[7,768]{1,0:T(8,128)S(1)}, f32[7,768]{1,0:T(8,128)S(1)}, u32[]{:S(2)}, u32[]{:S(2)}) collective-permute-start(f32[7,768]{1,0:T(8,128)S(1)} %slice.133), channel_id=1, source_target_pairs={{1,0},{2,1},{3,2},{4,3},{5,4},{6,5},{7,6},{8,7},{9,8},{10,9},{11,1... | collective-permute-start | bytes 64520 | tf_op jit(solution)/shard_map/ppermute | solution.py:298
  (36 other events, 264.3 us)

commit v3 on v2

--- a/solution.py
+++ b/solution.py
@@ -33,7 +33,7 @@
 FFN_ROWS = 2 * FF
 ATTN_TAIL = 5 * D
 FFN_TAIL = FF + 3 * D
-AHEAD_PAIRS = (2, 2, 2)
+AHEAD_PAIRS = (3, 2, 1)
 PAIRS = (1, 5)
 VEC_ROWS = 16
 COUNT_ROW = 12

time: 292 us -> 290 us (level)
  transfers between devices with their start and end apart: 43 -> 43, of which waited for: 21 -> 22; matrix products, arithmetic and copies ran while one was open for 4% -> 4% of each run, Pallas kernels for 23% -> 23%
where the time goes in v3:
time: 290 us; the launch traced here: 286 us
  Pallas kernels  125 us (43%)
  waiting for transfers between devices  72.2 us (25%)
  starting transfers between devices  60.3 us (21%)
  local copies, waits for them, and re-layouts  14.4 us (5%)
  other arithmetic  8.81 us (3%)
  between operations  4.95 us (2%)
    ppermute x39, waiting for transfers between devices, send(): return lax.ppermute(array, AXES, self.rotation(axis, step))  70.2 us
    pallas_call x1, Pallas kernels, middle(): pl.pallas_call(functools.partial(middle_kernel, fetch, len(sources)), gri...  37.1 us
    ppermute x39, starting transfers between devices, send(): return lax.ppermute(array, AXES, self.rotation(axis, step))  36.7 us
    pallas_call x2, Pallas kernels, attend_back(): pl.pallas_call(attend_back_kernel, grid=(pairs,), in_specs=attend_specs()...  24.3 us
    pallas_call x1, Pallas kernels, ffn_terms(): pl.pallas_call(kernel, grid=(2 * UP_CHUNKS,), in_specs=[pl.BlockSpec(memo...  15.6 us
    pallas_call x3, Pallas kernels, attend(): pl.pallas_call(attend_kernel, grid=(pairs,), in_specs=attend_specs() + [p...  15.1 us
    ppermute x2, starting transfers between devices, to_rows(): lax.ppermute(flat[-tail:], AXES, [(i, i + 1) for i in range(count - 1)])  12.4 us
    ppermute x2, starting transfers between devices, to_flat(): lax.ppermute(block[:tail // D], AXES, [(i + 1, i) for i in range(count -...  11.1 us
  transfers between devices with their start and end apart: 43, of which 22 were waited for; matrix products, arithmetic and copies ran while one was open for 4% of the time, Pallas kernels for 23%

profile of v3, /device:TPU:8, one launch (start us, length us, event | category | flops | bytes accessed | tf_op | source)
XLA Modules:
  0.0 286.1 jit_solution(15182438020156909170)
XLA Ops:
  1.5 3.4 %collective-permute-start = (bf16[3840]{0:T(1024)(128)(2,1)S(1)}, bf16[3840]{0:T(1024)(128)(2,1)S(1)}, u32[]{:S(2)}, u32[]{:S(2)}) collective-permute-start(bf16[3840]{0:T(1024)(128)(2,1)S(1)} %slice.161), channel_id=1, source_target_pairs={{0,1},{1,2},{2,3},{3,4},{4,5},{5,6},{6,7},{7,8},{8,9},{9,10},{10,1... | collective-permute-start | bytes 23048 | tf_op jit(solution)/shard_map/ppermute | solution.py:290
  11.4 2.6 collective-permute-start.2
  16.3 9.0 %collective-permute-start.5 = (bf16[5376]{0:T(1024)(128)(2,1)S(1)}, bf16[5376]{0:T(1024)(128)(2,1)S(1)}, u32[]{:S(2)}, u32[]{:S(2)}) collective-permute-start(bf16[5376]{0:T(1024)(128)(2,1)S(1)} %slice.100), channel_id=1, source_target_pairs={{0,1},{1,2},{2,3},{3,4},{4,5},{5,6},{6,7},{7,8},{8,9},{9,10},{10,1... | collective-permute-start | bytes 32264 | tf_op jit(solution)/shard_map/ppermute | solution.py:290
  27.5 2.5 collective-permute-start.6
  30.0 2.6 collective-permute-start.7
  33.2 2.5 collective-permute-done.4
  35.8 4.5 %collective-permute-done.6.refs_1_ = bf16[96,768]{1,0:T(8,128)(2,1)S(1)} collective-permute-done((bf16[96,768]{1,0:T(8,128)(2,1)S(1)}, bf16[96,768]{1,0:T(8,128)(2,1)S(1)}, u32[]{:S(2)}, u32[]{:S(2)}) %collective-permute-start.6) | collective-permute-done | bytes 147488 | tf_op jit(solution)/shard_map/ppermute | solution.py:84
  52.7 6.5 %collective-permute-done.11.refs_1_ = bf16[96,768]{1,0:T(8,128)(2,1)S(1)} collective-permute-done((bf16[96,768]{1,0:T(8,128)(2,1)S(1)}, bf16[96,768]{1,0:T(8,128)(2,1)S(1)}, u32[]{:S(2)}, u32[]{:S(2)}) %collective-permute-start.11) | collective-permute-done | bytes 147488 | tf_op jit(solution)/shard_map/ppermute | solution.py:84
  64.3 2.7 collective-permute-done.9.refs_1_
  74.9 7.5 %project.1 = (bf16[1024,768]{1,0:T(8,128)(2,1)S(1)}, bf16[1024,768]{1,0:T(8,128)(2,1)S(1)}, bf16[1024,768]{1,0:T(8,128)(2,1)S(1)}, f32[16,768]{1,0:T(8,128)S(1)}, bf16[3072,768]{1,0:T(8,128)(2,1)S(1)}) custom-call(s32[4]{0:T(128)S(1)} %pad_add_fusion.me_ref.me, bf16[1024,768]{1,0:T(8,128)(2,1)S(1)} %copy-done.3, ...), custom_call_target="tpu_custom_call" | custom-call | flops 8800000000 | bytes 1048576 | tf_op jit(solution)/shard_map/project/pallas_call | solution.py:357
  83.4 4.1 %collective-permute-done.17.refs_0_ = bf16[384,768]{1,0:T(8,128)(2,1)S(1)} collective-permute-done((bf16[384,768]{1,0:T(8,128)(2,1)}, bf16[384,768]{1,0:T(8,128)(2,1)S(1)}, u32[]{:S(2)}, u32[]{:S(2)}) %collective-permute-start.17) | collective-permute-done | bytes 589856 | tf_op jit(solution)/shard_map/ppermute | solution.py:84
  88.2 7.5 %attend.3 = (bf16[1024,384]{1,0:T(8,128)(2,1)S(1)}, f32[3,8,1024]{2,1,0:T(8,128)S(1)}) custom-call(s32[1]{0:T(128)} %copy.47.count, s32[1024,1]{1,0:T(8,128)S(1)} %copy.34.seg_column, s32[1,1024]{1,0:T(1,128)S(1)} %bitcast.66, bf16[1024,768]{1,0:T(8,128)(2,1)S(1)} %get-tuple-element.83.query, bf16[1024,768]{1,0:T(8,128)(2,1)S(1)} %get-tuple-element.84.key, ...), custom_call_target="tpu_custom_call" | custom-call | flops 13749999616 | bytes 1048576 | tf_op jit(solution)/shard_map/attend/pallas_call | solution.py:478
  96.3 5.1 %attend.4 = (bf16[1024,256]{1,0:T(8,128)(2,1)S(1)}, f32[2,8,1024]{2,1,0:T(8,128)S(1)}) custom-call(s32[1]{0:T(128)} %copy.47.count, s32[1024,1]{1,0:T(8,128)S(1)} %copy.34.seg_column, s32[1,1024]{1,0:T(1,128)S(1)} %bitcast.67, bf16[1024,768]{1,0:T(8,128)(2,1)S(1)} %get-tuple-element.83.query, bf16[1024,768]{1,0:T(8,128)(2,1)S(1)} %get-tuple-element.84.key, ...), custom_call_target="tpu_custom_call" | custom-call | flops 9166666752 | bytes 1048576 | tf_op jit(solution)/shard_map/attend/pallas_call | solution.py:478
  103.8 2.4 attend.5
  106.9 37.1 %middle.1 = (bf16[1024,768]{1,0:T(8,128)(2,1)}, bf16[1024,768]{1,0:T(8,128)(2,1)S(1)}, bf16[1024,3072]{1,0:T(8,128)(2,1)}, bf16[1024,3072]{1,0:T(8,128)(2,1)}, b...) custom-call(s32[1]{0:T(128)} %copy.47.count, ...), custom_call_target="tpu_custom_call" | custom-call | flops 44000002048 | bytes 1048576 | tf_op jit(solution)/shard_map/middle/pallas_call | solution.py:809
  144.0 2.8 copy-done.11
  146.7 15.6 %ffn_terms.1 = (bf16[2,8,192,768]{3,2,1,0:T(8,128)(2,1)S(1)}, bf16[2,8,192,768]{3,2,1,0:T(8,128)(2,1)S(1)}) custom-call(s32[4]{0:T(128)S(1)} %pad_add_fusion.me_ref.me, bf16[1024,768]{1,0:T(8,128)(2,1)S(1)} %get-tuple-element.103.hidden_ref, bf16[1024,3072]{1,0:T(8,128)(2,1)S(1)} %copy-done.11, ...), custom_call_target="tpu_custom_call" | custom-call | flops 16499999744 | bytes 1048576 | tf_op jit(solution)/shard_map/ffn_terms/pallas_call | solution.py:933
  162.5 4.0 %attend_back.2 = (bf16[3,1024,128]{2,1,0:T(8,128)(2,1)S(1)}, f32[8,128]{1,0:T(8,128)S(1)}) custom-call(s32[1]{0:T(128)} %copy.47.count, s32[1024,1]{1,0:T(8,128)S(1)} %copy.34.seg_column, s32[1,1024]{1,0:T(1,128)S(1)} %bitcast.70, bf16[1024,768]{1,0:T(8,128)(2,1)S(1)} %get-tuple-element.83.query, bf16[1024,768]{1,0:T(8,128)(2,1)S(1)} %get-tuple-element.84.key, ...), custom_call_target="tpu_custom_call" | custom-call | flops 13200000000 | bytes 1048576 | tf_op jit(solution)/shard_map/attend_back/pallas_call | solution.py:554
  166.5 3.8 %collective-permute-done.29.refs_1_.refs_3_ = bf16[2,4,2,192,768]{4,3,2,1,0:T(8,128)(2,1)S(1)} collective-permute-done((bf16[2,4,2,192,768]{4,3,2,1,0:T(8,128)(2,1)S(1)}, bf16[2,4,2,192,768]{4,3,2,1,0:T(8,128)(2,1)S(1)}, u32[]{:S(2)}, u32[]{:S(2)}) %collective-permute-start.29) | collective-permute-done | bytes 4718624 | tf_op jit(solution)/shard_map/ppermute | solution.py:84
  170.3 3.0 %add_routed.6 = (bf16[4,2,192,768]{3,2,1,0:T(8,128)(2,1)S(1)}, bf16[4,2,192,768]{3,2,1,0:T(8,128)(2,1)S(1)}) custom-call(s32[4]{0:T(128)S(1)} %pad_add_fusion.me_ref.me, bf16[2,4,2,192,768]{4,3,2,1,0:T(8,128)(2,1)S(1)} %bitcast.92, bf16[2,4,2,192,768]{4,3,2,1,0:T(8,128)(2,1)S(1)} %collective-permute-done.29.refs_1_.refs_3_, ...), custom_call_target="tpu_custom_call" | custom-call | flops 5280000000 | bytes 1048576 | tf_op jit(solution)/shard_map/add_routed/pallas_call | solution.py:188
  175.0 20.3 %attend_back.3 = (bf16[3,1024,640]{2,1,0:T(8,128)(2,1)S(1)}, f32[8,640]{1,0:T(8,128)S(1)}) custom-call(s32[1]{0:T(128)} %copy.47.count, s32[1024,1]{1,0:T(8,128)S(1)} %copy.34.seg_column, s32[1,1024]{1,0:T(1,128)S(1)} %bitcast.71, bf16[1024,768]{1,0:T(8,128)(2,1)S(1)} %get-tuple-element.83.query, bf16[1024,768]{1,0:T(8,128)(2,1)S(1)} %get-tuple-element.84.key, ...), custom_call_target="tpu_custom_call" | custom-call | flops 16499999744 | bytes 1048576 | tf_op jit(solution)/shard_map/attend_back/pallas_call | solution.py:554
  195.4 7.3 %attn_terms.1 = (bf16[2,8,112,768]{3,2,1,0:T(8,128)(2,1)S(1)}, bf16[2,8,112,768]{3,2,1,0:T(8,128)(2,1)S(1)}) custom-call(s32[4]{0:T(128)S(1)} %pad_add_fusion.me_ref.me, bf16[1024,768]{1,0:T(8,128)(2,1)S(1)} %copy-done.4, f32[16,768]{1,0:T(8,128)S(1)} %fusion.7.vectors_ref, bf16[1024,768]{1,0:T(8,128)(2,1)S(1)} %copy-done.12, ...), custom_call_target="tpu_custom_call" | custom-call | flops 6600000000 | bytes 1048576 | tf_op jit(solution)/shard_map/attn_terms/pallas_call | solution.py:1014
  206.2 5.7 %token_grad.1 = bf16[1024,768]{1,0:T(8,128)(2,1)} custom-call(f32[1024,768]{1,0:T(8,128)S(1)} %copy-done.1, bf16[3072,768]{1,0:T(8,128)(2,1)S(1)} %bitcast.62, bf16[3,1024,128]{2,1,0:T(8,128)(2,1)S(1)} %get-tuple-element.108.refs_3_.refs_0_, bf16[3,1024,640]{2,1,0:T(8,128)(2,1)S(1)} %get-tuple-element.112.refs_4_.refs_1_, ...), custom_call_target="tpu_custom_call" | custom-call | flops 2200000000 | bytes 1048576 | tf_op jit(solution)/shard_map/token_grad/pallas_call | solution.py:1053
  214.0 6.7 %collective-permute-done.32.refs_1_.refs_3_.refs_5_.refs_7_ = bf16[4,192,768]{2,1,0:T(8,128)(2,1)S(1)} collective-permute-done((bf16[4,192,768]{2,1,0:T(8,128)(2,1)S(1)}, bf16[4,192,768]{2,1,0:T(8,128)(2,1)S(1)}, u32[]{:S(2)}, u32[]{:S(2)}) %collective-permute-start.32) | collective-permute-done | bytes 1179680 | tf_op jit(solution)/shard_map/ppermute | solution.py:84
  224.2 11.0 %collective-permute-done.34 = bf16[1,192,768]{2,1,0:T(8,128)(2,1)S(1)} collective-permute-done((bf16[1,192,768]{2,1,0:T(8,128)(2,1)S(1)}, bf16[1,192,768]{2,1,0:T(8,128)(2,1)S(1)}, u32[]{:S(2)}, u32[]{:S(2)}) %collective-permute-start.34) | collective-permute-done | bytes 294944 | tf_op jit(solution)/shard_map/ppermute | solution.py:84
  235.2 6.2 %collective-permute-done.35 = bf16[1,192,768]{2,1,0:T(8,128)(2,1)S(1)} collective-permute-done((bf16[1,192,768]{2,1,0:T(8,128)(2,1)S(1)}, bf16[1,192,768]{2,1,0:T(8,128)(2,1)S(1)}, u32[]{:S(2)}, u32[]{:S(2)}) %collective-permute-start.35) | collective-permute-done | bytes 294944 | tf_op jit(solution)/shard_map/ppermute | solution.py:84
  249.6 3.0 %collective-permute-done.41 = bf16[1,192,768]{2,1,0:T(8,128)(2,1)S(1)} collective-permute-done((bf16[1,192,768]{2,1,0:T(8,128)(2,1)S(1)}, bf16[1,192,768]{2,1,0:T(8,128)(2,1)S(1)}, u32[]{:S(2)}, u32[]{:S(2)}) %collective-permute-start.41) | collective-permute-done | bytes 294944 | tf_op jit(solution)/shard_map/ppermute | solution.py:84
  257.8 3.2 %collective-permute-start.38 = (bf16[1,112,768]{2,1,0:T(8,128)(2,1)S(1)}, bf16[1,112,768]{2,1,0:T(8,128)(2,1)S(1)}, u32[]{:S(2)}, u32[]{:S(2)}) collective-permute-start(bf16[1,112,768]{2,1,0:T(8,128)(2,1)S(1)} %get-tuple-element.136), channel_id=1, source_target_pairs={{0,4},{1,5},{2,6},{3,7},{4,0},{5,1},{6,2},{7,3},{8,12},{9,13},{10,... | collective-permute-start | bytes 516104 | tf_op jit(solution)/shard_map/ppermute | solution.py:84
  261.5 4.5 %collective-permute-start.42 = (f32[7,768]{1,0:T(8,128)S(1)}, f32[7,768]{1,0:T(8,128)S(1)}, u32[]{:S(2)}, u32[]{:S(2)}) collective-permute-start(f32[7,768]{1,0:T(8,128)S(1)} %slice.133), channel_id=1, source_target_pairs={{1,0},{2,1},{3,2},{4,3},{5,4},{6,5},{7,6},{8,7},{9,8},{10,9},{11,1... | collective-permute-start | bytes 64520 | tf_op jit(solution)/shard_map/ppermute | solution.py:298
  266.0 6.0 %collective-permute-done.39 = bf16[1,112,768]{2,1,0:T(8,128)(2,1)S(1)} collective-permute-done((bf16[1,112,768]{2,1,0:T(8,128)(2,1)S(1)}, bf16[1,112,768]{2,1,0:T(8,128)(2,1)S(1)}, u32[]{:S(2)}, u32[]{:S(2)}) %collective-permute-start.39) | collective-permute-done | bytes 172064 | tf_op jit(solution)/shard_map/ppermute | solution.py:84
  272.9 6.6 %collective-permute-start.40 = (f32[5,768]{1,0:T(8,128)S(1)}, f32[5,768]{1,0:T(8,128)S(1)}, u32[]{:S(2)}, u32[]{:S(2)}) collective-permute-start(f32[5,768]{1,0:T(8,128)S(1)} %slice_bitcast_fusion.2), channel_id=1, source_target_pairs={{1,0},{2,1},{3,2},{4,3},{5,4},{6,5},{7,6},{8,7},{9,8},{10,9},{11,1... | collective-permute-start | bytes 46088 | tf_op jit(solution)/shard_map/ppermute | solution.py:298
  279.7 3.5 %subtract_multiply_fusion = (f32[147624]{0:T(1024)}, f32[147624]{0:T(1024)}, f32[147624]{0:T(1024)}, f32[147624]{0:T(1024)}, f32[147624]{0:T(1024)}) fusion(f32[147624]{0:T(1024)S(1)} %copy-done.18, f32[147624]{0:T(1024)S(1)} %copy-done.15, f32[147624]{0:T(1024)} %param.21, f32[147624]{0:T(1024)} %param.22, f32[]{:T(128)} %bitcast.38, ...), kind=kLoop, calls=%fused_computation.7 | loop fusion | flops 2657232 | bytes 5904968 | tf_op jit(solution)/shard_map/mul | solution.py:1077
  (178 shorter events, 68.1 us)
Async XLA Ops:
  11.0 14.3 %collective-permute-start.3 = (bf16[112,768]{1,0:T(8,128)(2,1)S(1)}, bf16[112,768]{1,0:T(8,128)(2,1)S(1)}, u32[]{:S(2)}, u32[]{:S(2)}) collective-permute-start(bf16[112,768]{1,0:T(8,128)(2,1)S(1)} %constant_dynamic-update-slice_fusion), channel_id=1, source_target_pairs={{0,6},{1,7},{2,0},{3,1},{4,2},{5,3},{6,4},{7,5},{8,14},{9,15},{10,... | collective-permute-start | bytes 516104 | tf_op jit(solution)/shard_map/ppermute | solution.py:84
  11.4 13.9 %collective-permute-start.2 = (bf16[112,768]{1,0:T(8,128)(2,1)S(1)}, bf16[112,768]{1,0:T(8,128)(2,1)S(1)}, u32[]{:S(2)}, u32[]{:S(2)}) collective-permute-start(bf16[112,768]{1,0:T(8,128)(2,1)S(1)} %constant_dynamic-update-slice_fusion), channel_id=1, source_target_pairs={{0,4},{1,5},{2,6},{3,7},{4,0},{5,1},{6,2},{7,3},{8,12},{9,13},{10,... | collective-permute-start | bytes 516104 | tf_op jit(solution)/shard_map/ppermute | solution.py:84
  16.3 10.4 %collective-permute-start.5 = (bf16[5376]{0:T(1024)(128)(2,1)S(1)}, bf16[5376]{0:T(1024)(128)(2,1)S(1)}, u32[]{:S(2)}, u32[]{:S(2)}) collective-permute-start(bf16[5376]{0:T(1024)(128)(2,1)S(1)} %slice.100), channel_id=1, source_target_pairs={{0,1},{1,2},{2,3},{3,4},{4,5},{5,6},{6,7},{7,8},{8,9},{9,10},{10,1... | collective-permute-start | bytes 32264 | tf_op jit(solution)/shard_map/ppermute | solution.py:290
  25.5 10.2 %collective-permute-start.4 = (bf16[400,768]{1,0:T(8,128)(2,1)S(1)}, bf16[400,768]{1,0:T(8,128)(2,1)S(1)}, u32[]{:S(2)}, u32[]{:S(2)}) collective-permute-start(bf16[400,768]{1,0:T(8,128)(2,1)S(1)} %pad_maximum_fusion.1), channel_id=1, source_target_pairs={{0,1},{1,0},{2,3},{3,2},{4,5},{5,4},{6,7},{7,6},{8,24},{9,25},{10,... | collective-permute-start | bytes 1843208 | tf_op jit(solution)/shard_map/ppermute | solution.py:84
  27.5 12.8 %collective-permute-start.6 = (bf16[96,768]{1,0:T(8,128)(2,1)S(1)}, bf16[96,768]{1,0:T(8,128)(2,1)S(1)}, u32[]{:S(2)}, u32[]{:S(2)}) collective-permute-start(bf16[96,768]{1,0:T(8,128)(2,1)S(1)} %get-tuple-element.77.refs_0_), channel_id=1, source_target_pairs={{0,2},{1,3},{2,4},{3,5},{4,6},{5,7},{6,0},{7,1},{8,10},{9,11},{10,... | collective-permute-start | bytes 442376 | tf_op jit(solution)/shard_map/ppermute | solution.py:84
  30.0 12.1 %collective-permute-start.7 = (bf16[96,768]{1,0:T(8,128)(2,1)S(1)}, bf16[96,768]{1,0:T(8,128)(2,1)S(1)}, u32[]{:S(2)}, u32[]{:S(2)}) collective-permute-start(bf16[96,768]{1,0:T(8,128)(2,1)S(1)} %get-tuple-element.77.refs_0_), channel_id=1, source_target_pairs={{0,4},{1,5},{2,6},{3,7},{4,0},{5,1},{6,2},{7,3},{8,12},{9,13},{10,... | collective-permute-start | bytes 442376 | tf_op jit(solution)/shard_map/ppermute | solution.py:84
  32.6 11.5 %collective-permute-start.8 = (bf16[96,768]{1,0:T(8,128)(2,1)S(1)}, bf16[96,768]{1,0:T(8,128)(2,1)S(1)}, u32[]{:S(2)}, u32[]{:S(2)}) collective-permute-start(bf16[96,768]{1,0:T(8,128)(2,1)S(1)} %get-tuple-element.77.refs_0_), channel_id=1, source_target_pairs={{0,6},{1,7},{2,0},{3,1},{4,2},{5,3},{6,4},{7,5},{8,14},{9,15},{10,... | collective-permute-start | bytes 442376 | tf_op jit(solution)/shard_map/ppermute | solution.py:84
  44.1 22.9 %collective-permute-start.9 = (bf16[784,768]{1,0:T(8,128)(2,1)S(1)}, bf16[784,768]{1,0:T(8,128)(2,1)}, u32[]{:S(2)}, u32[]{:S(2)}) collective-permute-start(bf16[784,768]{1,0:T(8,128)(2,1)S(1)} %pad_maximum_fusion.refs_0_), channel_id=1, source_target_pairs={{0,16},{1,17},{2,18},{3,19},{4,20},{5,21},{6,22},{7,23},{8,9},{9,8... | collective-permute-start | bytes 3612680 | tf_op jit(solution)/shard_map/ppermute | solution.py:84
  46.7 17.7 %collective-permute-start.10 = (bf16[384,768]{1,0:T(8,128)(2,1)}, bf16[384,768]{1,0:T(8,128)(2,1)S(1)}, u32[]{:S(2)}, u32[]{:S(2)}) collective-permute-start(bf16[384,768]{1,0:T(8,128)(2,1)} %bitcast.12), channel_id=1, source_target_pairs={{0,1},{1,0},{2,3},{3,2},{4,5},{5,4},{6,7},{7,6},{8,24},{9,25},{10,... | collective-permute-start | bytes 1769480 | tf_op jit(solution)/shard_map/ppermute | solution.py:84
  49.1 10.1 %collective-permute-start.11 = (bf16[96,768]{1,0:T(8,128)(2,1)S(1)}, bf16[96,768]{1,0:T(8,128)(2,1)S(1)}, u32[]{:S(2)}, u32[]{:S(2)}) collective-permute-start(bf16[96,768]{1,0:T(8,128)(2,1)S(1)} %get-tuple-element.79.refs_0_), channel_id=1, source_target_pairs={{0,2},{1,3},{2,4},{3,5},{4,6},{5,7},{6,0},{7,1},{8,10},{9,11},{10,... | collective-permute-start | bytes 442376 | tf_op jit(solution)/shard_map/ppermute | solution.py:84
  49.1 11.6 %collective-permute-start.12 = (bf16[96,768]{1,0:T(8,128)(2,1)S(1)}, bf16[96,768]{1,0:T(8,128)(2,1)S(1)}, u32[]{:S(2)}, u32[]{:S(2)}) collective-permute-start(bf16[96,768]{1,0:T(8,128)(2,1)S(1)} %get-tuple-element.79.refs_0_), channel_id=1, source_target_pairs={{0,4},{1,5},{2,6},{3,7},{4,0},{5,1},{6,2},{7,3},{8,12},{9,13},{10,... | collective-permute-start | bytes 442376 | tf_op jit(solution)/shard_map/ppermute | solution.py:84
  50.7 11.5 %collective-permute-start.13 = (bf16[96,768]{1,0:T(8,128)(2,1)S(1)}, bf16[96,768]{1,0:T(8,128)(2,1)S(1)}, u32[]{:S(2)}, u32[]{:S(2)}) collective-permute-start(bf16[96,768]{1,0:T(8,128)(2,1)S(1)} %get-tuple-element.79.refs_0_), channel_id=1, source_target_pairs={{0,6},{1,7},{2,0},{3,1},{4,2},{5,3},{6,4},{7,5},{8,14},{9,15},{10,... | collective-permute-start | bytes 442376 | tf_op jit(solution)/shard_map/ppermute | solution.py:84
  59.1 13.6 %collective-permute-start.14 = (bf16[784,768]{1,0:T(8,128)(2,1)S(1)}, bf16[784,768]{1,0:T(8,128)(2,1)}, u32[]{:S(2)}, u32[]{:S(2)}) collective-permute-start(bf16[784,768]{1,0:T(8,128)(2,1)S(1)} %pad_maximum_fusion.refs_0_), channel_id=1, source_target_pairs={{0,8},{1,9},{2,10},{3,11},{4,12},{5,13},{6,14},{7,15},{8,0},{9,1},... | collective-permute-start | bytes 3612680 | tf_op jit(solution)/shard_map/ppermute | solution.py:84
  67.7 27.9 %collective-permute-start.18 = (bf16[384,768]{1,0:T(8,128)(2,1)}, bf16[384,768]{1,0:T(8,128)(2,1)S(1)}, u32[]{:S(2)}, u32[]{:S(2)}) collective-permute-start(bf16[384,768]{1,0:T(8,128)(2,1)} %bitcast.12), channel_id=1, source_target_pairs={{0,16},{1,17},{2,18},{3,19},{4,20},{5,21},{6,22},{7,23},{8,9},{9,8... | collective-permute-start | bytes 1769480 | tf_op jit(solution)/shard_map/ppermute | solution.py:84
  68.1 27.6 %collective-permute-start.19 = (bf16[384,768]{1,0:T(8,128)(2,1)}, bf16[384,768]{1,0:T(8,128)(2,1)S(1)}, u32[]{:S(2)}, u32[]{:S(2)}) collective-permute-start(bf16[384,768]{1,0:T(8,128)(2,1)} %copy-done.5), channel_id=1, source_target_pairs={{0,16},{1,17},{2,18},{3,19},{4,20},{5,21},{6,22},{7,23},{8,9},{9,8... | collective-permute-start | bytes 1769480 | tf_op jit(solution)/shard_map/ppermute | solution.py:84
  71.1 16.5 %collective-permute-start.17 = (bf16[384,768]{1,0:T(8,128)(2,1)}, bf16[384,768]{1,0:T(8,128)(2,1)S(1)}, u32[]{:S(2)}, u32[]{:S(2)}) collective-permute-start(bf16[384,768]{1,0:T(8,128)(2,1)} %bitcast.75), channel_id=1, source_target_pairs={{0,1},{1,0},{2,3},{3,2},{4,5},{5,4},{6,7},{7,6},{8,24},{9,25},{10,... | collective-permute-start | bytes 1769480 | tf_op jit(solution)/shard_map/ppermute | solution.py:84
  82.4 19.0 %collective-permute-start.23 = (bf16[384,768]{1,0:T(8,128)(2,1)S(1)}, bf16[384,768]{1,0:T(8,128)(2,1)S(1)}, u32[]{:S(2)}, u32[]{:S(2)}) collective-permute-start(bf16[384,768]{1,0:T(8,128)(2,1)S(1)} %bitcast.77), channel_id=1, source_target_pairs={{0,16},{1,17},{2,18},{3,19},{4,20},{5,21},{6,22},{7,23},{8,9},{9,8... | collective-permute-start | bytes 1769480 | tf_op jit(solution)/shard_map/ppermute | solution.py:84
  83.4 22.8 %collective-permute-start.25 = (bf16[384,768]{1,0:T(8,128)(2,1)S(1)}, bf16[384,768]{1,0:T(8,128)(2,1)S(1)}, u32[]{:S(2)}, u32[]{:S(2)}) collective-permute-start(bf16[384,768]{1,0:T(8,128)(2,1)S(1)} %bitcast.78), channel_id=1, source_target_pairs={{0,8},{1,9},{2,10},{3,11},{4,12},{5,13},{6,14},{7,15},{8,0},{9,1},... | collective-permute-start | bytes 1769480 | tf_op jit(solution)/shard_map/ppermute | solution.py:84
  87.5 15.6 %collective-permute-start.24 = (bf16[384,768]{1,0:T(8,128)(2,1)S(1)}, bf16[384,768]{1,0:T(8,128)(2,1)S(1)}, u32[]{:S(2)}, u32[]{:S(2)}) collective-permute-start(bf16[384,768]{1,0:T(8,128)(2,1)S(1)} %collective-permute-done.17.refs_0_), channel_id=1, source_target_pairs={{0,16},{1,17},{2,18},{3,19},{4,20},{5,21},{6,22},{7,23},{8,9},{9,8... | collective-permute-start | bytes 1769480 | tf_op jit(solution)/shard_map/ppermute | solution.py:84
  173.3 29.6 %collective-permute-start.30 = (bf16[4,2,192,768]{3,2,1,0:T(8,128)(2,1)S(1)}, bf16[4,2,192,768]{3,2,1,0:T(8,128)(2,1)S(1)}, u32[]{:S(2)}, u32[]{:S(2)}) collective-permute-start(bf16[4,2,192,768]{3,2,1,0:T(8,128)(2,1)S(1)} %get-tuple-element.111.refs_0_), channel_id=1, source_target_pairs={{0,1},{1,0},{2,3},{3,2},{4,5},{5,4},{6,7},{7,6},{8,24},{9,25},{10,... | collective-permute-start | bytes 7077896 | tf_op jit(solution)/shard_map/ppermute | solution.py:84
  202.7 9.1 %collective-permute-start.31 = (bf16[2,4,2,112,768]{4,3,2,1,0:T(8,128)(2,1)S(1)}, bf16[2,4,2,112,768]{4,3,2,1,0:T(8,128)(2,1)S(1)}, u32[]{:S(2)}, u32[]{:S(2)}) collective-permute-start(bf16[2,4,2,112,768]{4,3,2,1,0:T(8,128)(2,1)S(1)} %bitcast.63), channel_id=1, source_target_pairs={{0,8},{1,9},{2,10},{3,11},{4,12},{5,13},{6,14},{7,15},{8,0},{9,1},... | collective-permute-start | bytes 8257544 | tf_op jit(solution)/shard_map/ppermute | solution.py:84
  204.4 16.3 %collective-permute-start.32 = (bf16[4,192,768]{2,1,0:T(8,128)(2,1)S(1)}, bf16[4,192,768]{2,1,0:T(8,128)(2,1)S(1)}, u32[]{:S(2)}, u32[]{:S(2)}) collective-permute-start(bf16[4,192,768]{2,1,0:T(8,128)(2,1)S(1)} %get-tuple-element.120.refs_3_), channel_id=1, source_target_pairs={{0,16},{1,17},{2,18},{3,19},{4,20},{5,21},{6,22},{7,23},{8,9},{9,8... | collective-permute-start | bytes 3538952 | tf_op jit(solution)/shard_map/ppermute | solution.py:84
  221.5 19.9 %collective-permute-start.33 = (bf16[4,2,112,768]{3,2,1,0:T(8,128)(2,1)S(1)}, bf16[4,2,112,768]{3,2,1,0:T(8,128)(2,1)S(1)}, u32[]{:S(2)}, u32[]{:S(2)}) collective-permute-start(bf16[4,2,112,768]{3,2,1,0:T(8,128)(2,1)S(1)} %get-tuple-element.130), channel_id=1, source_target_pairs={{0,1},{1,0},{2,3},{3,2},{4,5},{5,4},{6,7},{7,6},{8,24},{9,25},{10,... | collective-permute-start | bytes 4128776 | tf_op jit(solution)/shard_map/ppermute | solution.py:84
  222.6 12.6 %collective-permute-start.34 = (bf16[1,192,768]{2,1,0:T(8,128)(2,1)S(1)}, bf16[1,192,768]{2,1,0:T(8,128)(2,1)S(1)}, u32[]{:S(2)}, u32[]{:S(2)}) collective-permute-start(bf16[1,192,768]{2,1,0:T(8,128)(2,1)S(1)} %get-tuple-element.128), channel_id=1, source_target_pairs={{0,4},{1,5},{2,6},{3,7},{4,0},{5,1},{6,2},{7,3},{8,12},{9,13},{10,... | collective-permute-start | bytes 884744 | tf_op jit(solution)/shard_map/ppermute | solution.py:84
  224.1 17.4 %collective-permute-start.35 = (bf16[1,192,768]{2,1,0:T(8,128)(2,1)S(1)}, bf16[1,192,768]{2,1,0:T(8,128)(2,1)S(1)}, u32[]{:S(2)}, u32[]{:S(2)}) collective-permute-start(bf16[1,192,768]{2,1,0:T(8,128)(2,1)S(1)} %get-tuple-element.127), channel_id=1, source_target_pairs={{0,2},{1,3},{2,4},{3,5},{4,6},{5,7},{6,0},{7,1},{8,10},{9,11},{10,... | collective-permute-start | bytes 884744 | tf_op jit(solution)/shard_map/ppermute | solution.py:84
  242.7 14.3 %collective-permute-start.36 = (bf16[4,112,768]{2,1,0:T(8,128)(2,1)S(1)}, bf16[4,112,768]{2,1,0:T(8,128)(2,1)S(1)}, u32[]{:S(2)}, u32[]{:S(2)}) collective-permute-start(bf16[4,112,768]{2,1,0:T(8,128)(2,1)S(1)} %get-tuple-element.133), channel_id=1, source_target_pairs={{0,16},{1,17},{2,18},{3,19},{4,20},{5,21},{6,22},{7,23},{8,9},{9,8... | collective-permute-start | bytes 2064392 | tf_op jit(solution)/shard_map/ppermute | solution.py:84
  243.8 8.8 %collective-permute-start.41 = (bf16[1,192,768]{2,1,0:T(8,128)(2,1)S(1)}, bf16[1,192,768]{2,1,0:T(8,128)(2,1)S(1)}, u32[]{:S(2)}, u32[]{:S(2)}) collective-permute-start(bf16[1,192,768]{2,1,0:T(8,128)(2,1)S(1)} %get-tuple-element.129), channel_id=1, source_target_pairs={{0,6},{1,7},{2,0},{3,1},{4,2},{5,3},{6,4},{7,5},{8,14},{9,15},{10,... | collective-permute-start | bytes 884744 | tf_op jit(solution)/shard_map/ppermute | solution.py:84
  257.7 14.3 %collective-permute-start.39 = (bf16[1,112,768]{2,1,0:T(8,128)(2,1)S(1)}, bf16[1,112,768]{2,1,0:T(8,128)(2,1)S(1)}, u32[]{:S(2)}, u32[]{:S(2)}) collective-permute-start(bf16[1,112,768]{2,1,0:T(8,128)(2,1)S(1)} %get-tuple-element.137), channel_id=1, source_target_pairs={{0,6},{1,7},{2,0},{3,1},{4,2},{5,3},{6,4},{7,5},{8,14},{9,15},{10,... | collective-permute-start | bytes 516104 | tf_op jit(solution)/shard_map/ppermute | solution.py:84
  257.8 14.2 %collective-permute-start.38 = (bf16[1,112,768]{2,1,0:T(8,128)(2,1)S(1)}, bf16[1,112,768]{2,1,0:T(8,128)(2,1)S(1)}, u32[]{:S(2)}, u32[]{:S(2)}) collective-permute-start(bf16[1,112,768]{2,1,0:T(8,128)(2,1)S(1)} %get-tuple-element.136), channel_id=1, source_target_pairs={{0,4},{1,5},{2,6},{3,7},{4,0},{5,1},{6,2},{7,3},{8,12},{9,13},{10,... | collective-permute-start | bytes 516104 | tf_op jit(solution)/shard_map/ppermute | solution.py:84
  261.0 11.8 %collective-permute-start.37 = (bf16[1,112,768]{2,1,0:T(8,128)(2,1)S(1)}, bf16[1,112,768]{2,1,0:T(8,128)(2,1)S(1)}, u32[]{:S(2)}, u32[]{:S(2)}) collective-permute-start(bf16[1,112,768]{2,1,0:T(8,128)(2,1)S(1)} %get-tuple-element.135), channel_id=1, source_target_pairs={{0,2},{1,3},{2,4},{3,5},{4,6},{5,7},{6,0},{7,1},{8,10},{9,11},{10,... | collective-permute-start | bytes 516104 | tf_op jit(solution)/shard_map/ppermute | solution.py:84
  261.5 18.0 %collective-permute-start.42 = (f32[7,768]{1,0:T(8,128)S(1)}, f32[7,768]{1,0:T(8,128)S(1)}, u32[]{:S(2)}, u32[]{:S(2)}) collective-permute-start(f32[7,768]{1,0:T(8,128)S(1)} %slice.133), channel_id=1, source_target_pairs={{1,0},{2,1},{3,2},{4,3},{5,4},{6,5},{7,6},{8,7},{9,8},{10,9},{11,1... | collective-permute-start | bytes 64520 | tf_op jit(solution)/shard_map/ppermute | solution.py:298
  272.9 10.3 %collective-permute-start.40 = (f32[5,768]{1,0:T(8,128)S(1)}, f32[5,768]{1,0:T(8,128)S(1)}, u32[]{:S(2)}, u32[]{:S(2)}) collective-permute-start(f32[5,768]{1,0:T(8,128)S(1)} %slice_bitcast_fusion.2), channel_id=1, source_target_pairs={{1,0},{2,1},{3,2},{4,3},{5,4},{6,5},{7,6},{8,7},{9,8},{10,9},{11,1... | collective-permute-start | bytes 46088 | tf_op jit(solution)/shard_map/ppermute | solution.py:298
  (36 other events, 243.4 us)

commit v4 on v3

--- a/solution.py
+++ b/solution.py
@@ -209,7 +209,7 @@
         return self.places.send(give, "c", 1)
 
     def first(self, keep, arrived):
-        deep = 2
+        deep = 1
 
         def route(far):
             def pick_block(z, e, me):

time: 290 us -> 289 us (level)
  no operation moved by 1% of the time
where the time goes in v4:
time: 289 us; the launch traced here: 285 us
  Pallas kernels  123 us (43%)
  waiting for transfers between devices  72.9 us (25%)
  starting transfers between devices  60.3 us (21%)
  local copies, waits for them, and re-layouts  14.4 us (5%)
  other arithmetic  8.81 us (3%)
  between operations  4.95 us (2%)
    ppermute x39, waiting for transfers between devices, send(): return lax.ppermute(array, AXES, self.rotation(axis, step))  70.9 us
    pallas_call x1, Pallas kernels, middle(): pl.pallas_call(functools.partial(middle_kernel, fetch, len(sources)), gri...  37.1 us
    ppermute x39, starting transfers between devices, send(): return lax.ppermute(array, AXES, self.rotation(axis, step))  36.7 us
    pallas_call x2, Pallas kernels, attend_back(): pl.pallas_call(attend_back_kernel, grid=(pairs,), in_specs=attend_specs()...  24.3 us
    pallas_call x1, Pallas kernels, ffn_terms(): pl.pallas_call(kernel, grid=(2 * UP_CHUNKS,), in_specs=[pl.BlockSpec(memo...  15.6 us
    pallas_call x3, Pallas kernels, attend(): pl.pallas_call(attend_kernel, grid=(pairs,), in_specs=attend_specs() + [p...  15.1 us
    ppermute x2, starting transfers between devices, to_rows(): lax.ppermute(flat[-tail:], AXES, [(i, i + 1) for i in range(count - 1)])  12.4 us
    ppermute x2, starting transfers between devices, to_flat(): lax.ppermute(block[:tail // D], AXES, [(i + 1, i) for i in range(count -...  11.2 us
  transfers between devices with their start and end apart: 43, of which 22 were waited for; matrix products, arithmetic and copies ran while one was open for 4% of the time, Pallas kernels for 23%

profile of v4, /device:TPU:8, one launch (start us, length us, event | category | flops | bytes accessed | tf_op | source)
XLA Modules:
  0.0 284.9 jit_solution(6048595287373995116)
XLA Ops:
  1.5 3.4 %collective-permute-start = (bf16[3840]{0:T(1024)(128)(2,1)S(1)}, bf16[3840]{0:T(1024)(128)(2,1)S(1)}, u32[]{:S(2)}, u32[]{:S(2)}) collective-permute-start(bf16[3840]{0:T(1024)(128)(2,1)S(1)} %slice.161), channel_id=1, source_target_pairs={{0,1},{1,2},{2,3},{3,4},{4,5},{5,6},{6,7},{7,8},{8,9},{9,10},{10,1... | collective-permute-start | bytes 23048 | tf_op jit(solution)/shard_map/ppermute | solution.py:290
  11.4 2.6 collective-permute-start.2
  16.3 9.0 %collective-permute-start.5 = (bf16[5376]{0:T(1024)(128)(2,1)S(1)}, bf16[5376]{0:T(1024)(128)(2,1)S(1)}, u32[]{:S(2)}, u32[]{:S(2)}) collective-permute-start(bf16[5376]{0:T(1024)(128)(2,1)S(1)} %slice.100), channel_id=1, source_target_pairs={{0,1},{1,2},{2,3},{3,4},{4,5},{5,6},{6,7},{7,8},{8,9},{9,10},{10,1... | collective-permute-start | bytes 32264 | tf_op jit(solution)/shard_map/ppermute | solution.py:290
  27.5 2.5 collective-permute-start.6
  30.0 2.6 collective-permute-start.7
  33.2 2.5 collective-permute-done.4
  35.8 4.5 %collective-permute-done.6.refs_1_ = bf16[96,768]{1,0:T(8,128)(2,1)S(1)} collective-permute-done((bf16[96,768]{1,0:T(8,128)(2,1)S(1)}, bf16[96,768]{1,0:T(8,128)(2,1)S(1)}, u32[]{:S(2)}, u32[]{:S(2)}) %collective-permute-start.6) | collective-permute-done | bytes 147488 | tf_op jit(solution)/shard_map/ppermute | solution.py:84
  46.7 2.4 collective-permute-start.10
  52.7 6.5 %collective-permute-done.11.refs_1_ = bf16[96,768]{1,0:T(8,128)(2,1)S(1)} collective-permute-done((bf16[96,768]{1,0:T(8,128)(2,1)S(1)}, bf16[96,768]{1,0:T(8,128)(2,1)S(1)}, u32[]{:S(2)}, u32[]{:S(2)}) %collective-permute-start.11) | collective-permute-done | bytes 147488 | tf_op jit(solution)/shard_map/ppermute | solution.py:84
  64.3 2.7 collective-permute-done.9.refs_1_
  74.9 7.5 %project.1 = (bf16[1024,768]{1,0:T(8,128)(2,1)S(1)}, bf16[1024,768]{1,0:T(8,128)(2,1)S(1)}, bf16[1024,768]{1,0:T(8,128)(2,1)S(1)}, f32[16,768]{1,0:T(8,128)S(1)}, bf16[3072,768]{1,0:T(8,128)(2,1)S(1)}) custom-call(s32[4]{0:T(128)S(1)} %pad_add_fusion.me_ref.me, bf16[1024,768]{1,0:T(8,128)(2,1)S(1)} %copy-done.3, ...), custom_call_target="tpu_custom_call" | custom-call | flops 8800000000 | bytes 1048576 | tf_op jit(solution)/shard_map/project/pallas_call | solution.py:357
  83.4 4.1 %collective-permute-done.17.refs_0_ = bf16[384,768]{1,0:T(8,128)(2,1)S(1)} collective-permute-done((bf16[384,768]{1,0:T(8,128)(2,1)}, bf16[384,768]{1,0:T(8,128)(2,1)S(1)}, u32[]{:S(2)}, u32[]{:S(2)}) %collective-permute-start.17) | collective-permute-done | bytes 589856 | tf_op jit(solution)/shard_map/ppermute | solution.py:84
  88.2 7.5 %attend.3 = (bf16[1024,384]{1,0:T(8,128)(2,1)S(1)}, f32[3,8,1024]{2,1,0:T(8,128)S(1)}) custom-call(s32[1]{0:T(128)} %copy.47.count, s32[1024,1]{1,0:T(8,128)S(1)} %copy.34.seg_column, s32[1,1024]{1,0:T(1,128)S(1)} %bitcast.66, bf16[1024,768]{1,0:T(8,128)(2,1)S(1)} %get-tuple-element.83.query, bf16[1024,768]{1,0:T(8,128)(2,1)S(1)} %get-tuple-element.84.key, ...), custom_call_target="tpu_custom_call" | custom-call | flops 13749999616 | bytes 1048576 | tf_op jit(solution)/shard_map/attend/pallas_call | solution.py:478
  96.3 5.1 %attend.4 = (bf16[1024,256]{1,0:T(8,128)(2,1)S(1)}, f32[2,8,1024]{2,1,0:T(8,128)S(1)}) custom-call(s32[1]{0:T(128)} %copy.47.count, s32[1024,1]{1,0:T(8,128)S(1)} %copy.34.seg_column, s32[1,1024]{1,0:T(1,128)S(1)} %bitcast.67, bf16[1024,768]{1,0:T(8,128)(2,1)S(1)} %get-tuple-element.83.query, bf16[1024,768]{1,0:T(8,128)(2,1)S(1)} %get-tuple-element.84.key, ...), custom_call_target="tpu_custom_call" | custom-call | flops 9166666752 | bytes 1048576 | tf_op jit(solution)/shard_map/attend/pallas_call | solution.py:478
  103.8 2.4 attend.5
  106.9 37.1 %middle.1 = (bf16[1024,768]{1,0:T(8,128)(2,1)}, bf16[1024,768]{1,0:T(8,128)(2,1)S(1)}, bf16[1024,3072]{1,0:T(8,128)(2,1)}, bf16[1024,3072]{1,0:T(8,128)(2,1)}, b...) custom-call(s32[1]{0:T(128)} %copy.47.count, ...), custom_call_target="tpu_custom_call" | custom-call | flops 44000002048 | bytes 1048576 | tf_op jit(solution)/shard_map/middle/pallas_call | solution.py:809
  144.0 2.8 copy-done.11
  146.7 15.6 %ffn_terms.1 = (bf16[2,8,192,768]{3,2,1,0:T(8,128)(2,1)S(1)}, bf16[2,8,192,768]{3,2,1,0:T(8,128)(2,1)S(1)}) custom-call(s32[4]{0:T(128)S(1)} %pad_add_fusion.me_ref.me, bf16[1024,768]{1,0:T(8,128)(2,1)S(1)} %get-tuple-element.103.hidden_ref, bf16[1024,3072]{1,0:T(8,128)(2,1)S(1)} %copy-done.11, ...), custom_call_target="tpu_custom_call" | custom-call | flops 16499999744 | bytes 1048576 | tf_op jit(solution)/shard_map/ffn_terms/pallas_call | solution.py:933
  162.5 4.0 %attend_back.2 = (bf16[3,1024,128]{2,1,0:T(8,128)(2,1)S(1)}, f32[8,128]{1,0:T(8,128)S(1)}) custom-call(s32[1]{0:T(128)} %copy.47.count, s32[1024,1]{1,0:T(8,128)S(1)} %copy.34.seg_column, s32[1,1024]{1,0:T(1,128)S(1)} %bitcast.70, bf16[1024,768]{1,0:T(8,128)(2,1)S(1)} %get-tuple-element.83.query, bf16[1024,768]{1,0:T(8,128)(2,1)S(1)} %get-tuple-element.84.key, ...), custom_call_target="tpu_custom_call" | custom-call | flops 13200000000 | bytes 1048576 | tf_op jit(solution)/shard_map/attend_back/pallas_call | solution.py:554
  166.5 3.8 %collective-permute-done.29.refs_1_.refs_3_ = bf16[2,4,2,192,768]{4,3,2,1,0:T(8,128)(2,1)S(1)} collective-permute-done((bf16[2,4,2,192,768]{4,3,2,1,0:T(8,128)(2,1)S(1)}, bf16[2,4,2,192,768]{4,3,2,1,0:T(8,128)(2,1)S(1)}, u32[]{:S(2)}, u32[]{:S(2)}) %collective-permute-start.29) | collective-permute-done | bytes 4718624 | tf_op jit(solution)/shard_map/ppermute | solution.py:84
  173.9 20.4 %attend_back.3 = (bf16[3,1024,640]{2,1,0:T(8,128)(2,1)S(1)}, f32[8,640]{1,0:T(8,128)S(1)}) custom-call(s32[1]{0:T(128)} %copy.47.count, s32[1024,1]{1,0:T(8,128)S(1)} %copy.34.seg_column, s32[1,1024]{1,0:T(1,128)S(1)} %bitcast.71, bf16[1024,768]{1,0:T(8,128)(2,1)S(1)} %get-tuple-element.83.query, bf16[1024,768]{1,0:T(8,128)(2,1)S(1)} %get-tuple-element.84.key, ...), custom_call_target="tpu_custom_call" | custom-call | flops 16499999744 | bytes 1048576 | tf_op jit(solution)/shard_map/attend_back/pallas_call | solution.py:554
  194.3 7.3 %attn_terms.1 = (bf16[2,8,112,768]{3,2,1,0:T(8,128)(2,1)S(1)}, bf16[2,8,112,768]{3,2,1,0:T(8,128)(2,1)S(1)}) custom-call(s32[4]{0:T(128)S(1)} %pad_add_fusion.me_ref.me, bf16[1024,768]{1,0:T(8,128)(2,1)S(1)} %copy-done.4, f32[16,768]{1,0:T(8,128)S(1)} %fusion.7.vectors_ref, bf16[1024,768]{1,0:T(8,128)(2,1)S(1)} %copy-done.12, ...), custom_call_target="tpu_custom_call" | custom-call | flops 6600000000 | bytes 1048576 | tf_op jit(solution)/shard_map/attn_terms/pallas_call | solution.py:1014
  205.0 5.7 %token_grad.1 = bf16[1024,768]{1,0:T(8,128)(2,1)} custom-call(f32[1024,768]{1,0:T(8,128)S(1)} %copy-done.1, bf16[3072,768]{1,0:T(8,128)(2,1)S(1)} %bitcast.62, bf16[3,1024,128]{2,1,0:T(8,128)(2,1)S(1)} %get-tuple-element.108.refs_3_.refs_0_, bf16[3,1024,640]{2,1,0:T(8,128)(2,1)S(1)} %get-tuple-element.112.refs_4_.refs_1_, ...), custom_call_target="tpu_custom_call" | custom-call | flops 2200000000 | bytes 1048576 | tf_op jit(solution)/shard_map/token_grad/pallas_call | solution.py:1053
  212.1 7.5 %collective-permute-done.32.refs_1_.refs_3_.refs_5_.refs_7_ = bf16[4,192,768]{2,1,0:T(8,128)(2,1)S(1)} collective-permute-done((bf16[4,192,768]{2,1,0:T(8,128)(2,1)S(1)}, bf16[4,192,768]{2,1,0:T(8,128)(2,1)S(1)}, u32[]{:S(2)}, u32[]{:S(2)}) %collective-permute-start.32) | collective-permute-done | bytes 1179680 | tf_op jit(solution)/shard_map/ppermute | solution.py:84
  223.1 11.0 %collective-permute-done.34 = bf16[1,192,768]{2,1,0:T(8,128)(2,1)S(1)} collective-permute-done((bf16[1,192,768]{2,1,0:T(8,128)(2,1)S(1)}, bf16[1,192,768]{2,1,0:T(8,128)(2,1)S(1)}, u32[]{:S(2)}, u32[]{:S(2)}) %collective-permute-start.34) | collective-permute-done | bytes 294944 | tf_op jit(solution)/shard_map/ppermute | solution.py:84
  234.1 6.2 %collective-permute-done.35 = bf16[1,192,768]{2,1,0:T(8,128)(2,1)S(1)} collective-permute-done((bf16[1,192,768]{2,1,0:T(8,128)(2,1)S(1)}, bf16[1,192,768]{2,1,0:T(8,128)(2,1)S(1)}, u32[]{:S(2)}, u32[]{:S(2)}) %collective-permute-start.35) | collective-permute-done | bytes 294944 | tf_op jit(solution)/shard_map/ppermute | solution.py:84
  248.4 3.0 %collective-permute-done.41 = bf16[1,192,768]{2,1,0:T(8,128)(2,1)S(1)} collective-permute-done((bf16[1,192,768]{2,1,0:T(8,128)(2,1)S(1)}, bf16[1,192,768]{2,1,0:T(8,128)(2,1)S(1)}, u32[]{:S(2)}, u32[]{:S(2)}) %collective-permute-start.41) | collective-permute-done | bytes 294944 | tf_op jit(solution)/shard_map/ppermute | solution.py:84
  256.6 3.2 %collective-permute-start.38 = (bf16[1,112,768]{2,1,0:T(8,128)(2,1)S(1)}, bf16[1,112,768]{2,1,0:T(8,128)(2,1)S(1)}, u32[]{:S(2)}, u32[]{:S(2)}) collective-permute-start(bf16[1,112,768]{2,1,0:T(8,128)(2,1)S(1)} %get-tuple-element.136), channel_id=1, source_target_pairs={{0,4},{1,5},{2,6},{3,7},{4,0},{5,1},{6,2},{7,3},{8,12},{9,13},{10,... | collective-permute-start | bytes 516104 | tf_op jit(solution)/shard_map/ppermute | solution.py:84
  260.3 4.5 %collective-permute-start.42 = (f32[7,768]{1,0:T(8,128)S(1)}, f32[7,768]{1,0:T(8,128)S(1)}, u32[]{:S(2)}, u32[]{:S(2)}) collective-permute-start(f32[7,768]{1,0:T(8,128)S(1)} %slice.133), channel_id=1, source_target_pairs={{1,0},{2,1},{3,2},{4,3},{5,4},{6,5},{7,6},{8,7},{9,8},{10,9},{11,1... | collective-permute-start | bytes 64520 | tf_op jit(solution)/shard_map/ppermute | solution.py:298
  264.9 6.0 %collective-permute-done.39 = bf16[1,112,768]{2,1,0:T(8,128)(2,1)S(1)} collective-permute-done((bf16[1,112,768]{2,1,0:T(8,128)(2,1)S(1)}, bf16[1,112,768]{2,1,0:T(8,128)(2,1)S(1)}, u32[]{:S(2)}, u32[]{:S(2)}) %collective-permute-start.39) | collective-permute-done | bytes 172064 | tf_op jit(solution)/shard_map/ppermute | solution.py:84
  271.7 6.7 %collective-permute-start.40 = (f32[5,768]{1,0:T(8,128)S(1)}, f32[5,768]{1,0:T(8,128)S(1)}, u32[]{:S(2)}, u32[]{:S(2)}) collective-permute-start(f32[5,768]{1,0:T(8,128)S(1)} %slice_bitcast_fusion.2), channel_id=1, source_target_pairs={{1,0},{2,1},{3,2},{4,3},{5,4},{6,5},{7,6},{8,7},{9,8},{10,9},{11,1... | collective-permute-start | bytes 46088 | tf_op jit(solution)/shard_map/ppermute | solution.py:298
  278.5 3.5 %subtract_multiply_fusion = (f32[147624]{0:T(1024)}, f32[147624]{0:T(1024)}, f32[147624]{0:T(1024)}, f32[147624]{0:T(1024)}, f32[147624]{0:T(1024)}) fusion(f32[147624]{0:T(1024)S(1)} %copy-done.18, f32[147624]{0:T(1024)S(1)} %copy-done.15, f32[147624]{0:T(1024)} %param.21, f32[147624]{0:T(1024)} %param.22, f32[]{:T(128)} %bitcast.38, ...), kind=kLoop, calls=%fused_computation.7 | loop fusion | flops 2657232 | bytes 5904968 | tf_op jit(solution)/shard_map/mul | solution.py:1077
  (178 shorter events, 66.7 us)
Async XLA Ops:
  11.0 14.3 %collective-permute-start.3 = (bf16[112,768]{1,0:T(8,128)(2,1)S(1)}, bf16[112,768]{1,0:T(8,128)(2,1)S(1)}, u32[]{:S(2)}, u32[]{:S(2)}) collective-permute-start(bf16[112,768]{1,0:T(8,128)(2,1)S(1)} %constant_dynamic-update-slice_fusion), channel_id=1, source_target_pairs={{0,6},{1,7},{2,0},{3,1},{4,2},{5,3},{6,4},{7,5},{8,14},{9,15},{10,... | collective-permute-start | bytes 516104 | tf_op jit(solution)/shard_map/ppermute | solution.py:84
  11.4 13.9 %collective-permute-start.2 = (bf16[112,768]{1,0:T(8,128)(2,1)S(1)}, bf16[112,768]{1,0:T(8,128)(2,1)S(1)}, u32[]{:S(2)}, u32[]{:S(2)}) collective-permute-start(bf16[112,768]{1,0:T(8,128)(2,1)S(1)} %constant_dynamic-update-slice_fusion), channel_id=1, source_target_pairs={{0,4},{1,5},{2,6},{3,7},{4,0},{5,1},{6,2},{7,3},{8,12},{9,13},{10,... | collective-permute-start | bytes 516104 | tf_op jit(solution)/shard_map/ppermute | solution.py:84
  16.3 10.4 %collective-permute-start.5 = (bf16[5376]{0:T(1024)(128)(2,1)S(1)}, bf16[5376]{0:T(1024)(128)(2,1)S(1)}, u32[]{:S(2)}, u32[]{:S(2)}) collective-permute-start(bf16[5376]{0:T(1024)(128)(2,1)S(1)} %slice.100), channel_id=1, source_target_pairs={{0,1},{1,2},{2,3},{3,4},{4,5},{5,6},{6,7},{7,8},{8,9},{9,10},{10,1... | collective-permute-start | bytes 32264 | tf_op jit(solution)/shard_map/ppermute | solution.py:290
  25.5 10.2 %collective-permute-start.4 = (bf16[400,768]{1,0:T(8,128)(2,1)S(1)}, bf16[400,768]{1,0:T(8,128)(2,1)S(1)}, u32[]{:S(2)}, u32[]{:S(2)}) collective-permute-start(bf16[400,768]{1,0:T(8,128)(2,1)S(1)} %pad_maximum_fusion.1), channel_id=1, source_target_pairs={{0,1},{1,0},{2,3},{3,2},{4,5},{5,4},{6,7},{7,6},{8,24},{9,25},{10,... | collective-permute-start | bytes 1843208 | tf_op jit(solution)/shard_map/ppermute | solution.py:84
  27.5 12.8 %collective-permute-start.6 = (bf16[96,768]{1,0:T(8,128)(2,1)S(1)}, bf16[96,768]{1,0:T(8,128)(2,1)S(1)}, u32[]{:S(2)}, u32[]{:S(2)}) collective-permute-start(bf16[96,768]{1,0:T(8,128)(2,1)S(1)} %get-tuple-element.77.refs_0_), channel_id=1, source_target_pairs={{0,2},{1,3},{2,4},{3,5},{4,6},{5,7},{6,0},{7,1},{8,10},{9,11},{10,... | collective-permute-start | bytes 442376 | tf_op jit(solution)/shard_map/ppermute | solution.py:84
  30.0 12.1 %collective-permute-start.7 = (bf16[96,768]{1,0:T(8,128)(2,1)S(1)}, bf16[96,768]{1,0:T(8,128)(2,1)S(1)}, u32[]{:S(2)}, u32[]{:S(2)}) collective-permute-start(bf16[96,768]{1,0:T(8,128)(2,1)S(1)} %get-tuple-element.77.refs_0_), channel_id=1, source_target_pairs={{0,4},{1,5},{2,6},{3,7},{4,0},{5,1},{6,2},{7,3},{8,12},{9,13},{10,... | collective-permute-start | bytes 442376 | tf_op jit(solution)/shard_map/ppermute | solution.py:84
  32.6 11.5 %collective-permute-start.8 = (bf16[96,768]{1,0:T(8,128)(2,1)S(1)}, bf16[96,768]{1,0:T(8,128)(2,1)S(1)}, u32[]{:S(2)}, u32[]{:S(2)}) collective-permute-start(bf16[96,768]{1,0:T(8,128)(2,1)S(1)} %get-tuple-element.77.refs_0_), channel_id=1, source_target_pairs={{0,6},{1,7},{2,0},{3,1},{4,2},{5,3},{6,4},{7,5},{8,14},{9,15},{10,... | collective-permute-start | bytes 442376 | tf_op jit(solution)/shard_map/ppermute | solution.py:84
  44.1 22.9 %collective-permute-start.9 = (bf16[784,768]{1,0:T(8,128)(2,1)S(1)}, bf16[784,768]{1,0:T(8,128)(2,1)}, u32[]{:S(2)}, u32[]{:S(2)}) collective-permute-start(bf16[784,768]{1,0:T(8,128)(2,1)S(1)} %pad_maximum_fusion.refs_0_), channel_id=1, source_target_pairs={{0,16},{1,17},{2,18},{3,19},{4,20},{5,21},{6,22},{7,23},{8,9},{9,8... | collective-permute-start | bytes 3612680 | tf_op jit(solution)/shard_map/ppermute | solution.py:84
  46.7 17.7 %collective-permute-start.10 = (bf16[384,768]{1,0:T(8,128)(2,1)}, bf16[384,768]{1,0:T(8,128)(2,1)S(1)}, u32[]{:S(2)}, u32[]{:S(2)}) collective-permute-start(bf16[384,768]{1,0:T(8,128)(2,1)} %bitcast.12), channel_id=1, source_target_pairs={{0,1},{1,0},{2,3},{3,2},{4,5},{5,4},{6,7},{7,6},{8,24},{9,25},{10,... | collective-permute-start | bytes 1769480 | tf_op jit(solution)/shard_map/ppermute | solution.py:84
  49.1 10.1 %collective-permute-start.11 = (bf16[96,768]{1,0:T(8,128)(2,1)S(1)}, bf16[96,768]{1,0:T(8,128)(2,1)S(1)}, u32[]{:S(2)}, u32[]{:S(2)}) collective-permute-start(bf16[96,768]{1,0:T(8,128)(2,1)S(1)} %get-tuple-element.79.refs_0_), channel_id=1, source_target_pairs={{0,2},{1,3},{2,4},{3,5},{4,6},{5,7},{6,0},{7,1},{8,10},{9,11},{10,... | collective-permute-start | bytes 442376 | tf_op jit(solution)/shard_map/ppermute | solution.py:84
  49.1 11.6 %collective-permute-start.12 = (bf16[96,768]{1,0:T(8,128)(2,1)S(1)}, bf16[96,768]{1,0:T(8,128)(2,1)S(1)}, u32[]{:S(2)}, u32[]{:S(2)}) collective-permute-start(bf16[96,768]{1,0:T(8,128)(2,1)S(1)} %get-tuple-element.79.refs_0_), channel_id=1, source_target_pairs={{0,4},{1,5},{2,6},{3,7},{4,0},{5,1},{6,2},{7,3},{8,12},{9,13},{10,... | collective-permute-start | bytes 442376 | tf_op jit(solution)/shard_map/ppermute | solution.py:84
  50.7 11.5 %collective-permute-start.13 = (bf16[96,768]{1,0:T(8,128)(2,1)S(1)}, bf16[96,768]{1,0:T(8,128)(2,1)S(1)}, u32[]{:S(2)}, u32[]{:S(2)}) collective-permute-start(bf16[96,768]{1,0:T(8,128)(2,1)S(1)} %get-tuple-element.79.refs_0_), channel_id=1, source_target_pairs={{0,6},{1,7},{2,0},{3,1},{4,2},{5,3},{6,4},{7,5},{8,14},{9,15},{10,... | collective-permute-start | bytes 442376 | tf_op jit(solution)/shard_map/ppermute | solution.py:84
  59.1 13.6 %collective-permute-start.14 = (bf16[784,768]{1,0:T(8,128)(2,1)S(1)}, bf16[784,768]{1,0:T(8,128)(2,1)}, u32[]{:S(2)}, u32[]{:S(2)}) collective-permute-start(bf16[784,768]{1,0:T(8,128)(2,1)S(1)} %pad_maximum_fusion.refs_0_), channel_id=1, source_target_pairs={{0,8},{1,9},{2,10},{3,11},{4,12},{5,13},{6,14},{7,15},{8,0},{9,1},... | collective-permute-start | bytes 3612680 | tf_op jit(solution)/shard_map/ppermute | solution.py:84
  67.7 27.9 %collective-permute-start.18 = (bf16[384,768]{1,0:T(8,128)(2,1)}, bf16[384,768]{1,0:T(8,128)(2,1)S(1)}, u32[]{:S(2)}, u32[]{:S(2)}) collective-permute-start(bf16[384,768]{1,0:T(8,128)(2,1)} %bitcast.12), channel_id=1, source_target_pairs={{0,16},{1,17},{2,18},{3,19},{4,20},{5,21},{6,22},{7,23},{8,9},{9,8... | collective-permute-start | bytes 1769480 | tf_op jit(solution)/shard_map/ppermute | solution.py:84
  68.1 27.6 %collective-permute-start.19 = (bf16[384,768]{1,0:T(8,128)(2,1)}, bf16[384,768]{1,0:T(8,128)(2,1)S(1)}, u32[]{:S(2)}, u32[]{:S(2)}) collective-permute-start(bf16[384,768]{1,0:T(8,128)(2,1)} %copy-done.5), channel_id=1, source_target_pairs={{0,16},{1,17},{2,18},{3,19},{4,20},{5,21},{6,22},{7,23},{8,9},{9,8... | collective-permute-start | bytes 1769480 | tf_op jit(solution)/shard_map/ppermute | solution.py:84
  71.1 16.5 %collective-permute-start.17 = (bf16[384,768]{1,0:T(8,128)(2,1)}, bf16[384,768]{1,0:T(8,128)(2,1)S(1)}, u32[]{:S(2)}, u32[]{:S(2)}) collective-permute-start(bf16[384,768]{1,0:T(8,128)(2,1)} %bitcast.75), channel_id=1, source_target_pairs={{0,1},{1,0},{2,3},{3,2},{4,5},{5,4},{6,7},{7,6},{8,24},{9,25},{10,... | collective-permute-start | bytes 1769480 | tf_op jit(solution)/shard_map/ppermute | solution.py:84
  82.4 19.0 %collective-permute-start.23 = (bf16[384,768]{1,0:T(8,128)(2,1)S(1)}, bf16[384,768]{1,0:T(8,128)(2,1)S(1)}, u32[]{:S(2)}, u32[]{:S(2)}) collective-permute-start(bf16[384,768]{1,0:T(8,128)(2,1)S(1)} %bitcast.77), channel_id=1, source_target_pairs={{0,16},{1,17},{2,18},{3,19},{4,20},{5,21},{6,22},{7,23},{8,9},{9,8... | collective-permute-start | bytes 1769480 | tf_op jit(solution)/shard_map/ppermute | solution.py:84
  83.4 22.8 %collective-permute-start.25 = (bf16[384,768]{1,0:T(8,128)(2,1)S(1)}, bf16[384,768]{1,0:T(8,128)(2,1)S(1)}, u32[]{:S(2)}, u32[]{:S(2)}) collective-permute-start(bf16[384,768]{1,0:T(8,128)(2,1)S(1)} %bitcast.78), channel_id=1, source_target_pairs={{0,8},{1,9},{2,10},{3,11},{4,12},{5,13},{6,14},{7,15},{8,0},{9,1},... | collective-permute-start | bytes 1769480 | tf_op jit(solution)/shard_map/ppermute | solution.py:84
  87.5 15.6 %collective-permute-start.24 = (bf16[384,768]{1,0:T(8,128)(2,1)S(1)}, bf16[384,768]{1,0:T(8,128)(2,1)S(1)}, u32[]{:S(2)}, u32[]{:S(2)}) collective-permute-start(bf16[384,768]{1,0:T(8,128)(2,1)S(1)} %collective-permute-done.17.refs_0_), channel_id=1, source_target_pairs={{0,16},{1,17},{2,18},{3,19},{4,20},{5,21},{6,22},{7,23},{8,9},{9,8... | collective-permute-start | bytes 1769480 | tf_op jit(solution)/shard_map/ppermute | solution.py:84
  172.1 29.6 %collective-permute-start.30 = (bf16[4,2,192,768]{3,2,1,0:T(8,128)(2,1)S(1)}, bf16[4,2,192,768]{3,2,1,0:T(8,128)(2,1)S(1)}, u32[]{:S(2)}, u32[]{:S(2)}) collective-permute-start(bf16[4,2,192,768]{3,2,1,0:T(8,128)(2,1)S(1)} %get-tuple-element.111.refs_0_), channel_id=1, source_target_pairs={{0,1},{1,0},{2,3},{3,2},{4,5},{5,4},{6,7},{7,6},{8,24},{9,25},{10,... | collective-permute-start | bytes 7077896 | tf_op jit(solution)/shard_map/ppermute | solution.py:84
  201.6 9.1 %collective-permute-start.31 = (bf16[2,4,2,112,768]{4,3,2,1,0:T(8,128)(2,1)S(1)}, bf16[2,4,2,112,768]{4,3,2,1,0:T(8,128)(2,1)S(1)}, u32[]{:S(2)}, u32[]{:S(2)}) collective-permute-start(bf16[2,4,2,112,768]{4,3,2,1,0:T(8,128)(2,1)S(1)} %bitcast.63), channel_id=1, source_target_pairs={{0,8},{1,9},{2,10},{3,11},{4,12},{5,13},{6,14},{7,15},{8,0},{9,1},... | collective-permute-start | bytes 8257544 | tf_op jit(solution)/shard_map/ppermute | solution.py:84
  203.3 16.3 %collective-permute-start.32 = (bf16[4,192,768]{2,1,0:T(8,128)(2,1)S(1)}, bf16[4,192,768]{2,1,0:T(8,128)(2,1)S(1)}, u32[]{:S(2)}, u32[]{:S(2)}) collective-permute-start(bf16[4,192,768]{2,1,0:T(8,128)(2,1)S(1)} %get-tuple-element.120.refs_3_), channel_id=1, source_target_pairs={{0,16},{1,17},{2,18},{3,19},{4,20},{5,21},{6,22},{7,23},{8,9},{9,8... | collective-permute-start | bytes 3538952 | tf_op jit(solution)/shard_map/ppermute | solution.py:84
  220.4 19.9 %collective-permute-start.33 = (bf16[4,2,112,768]{3,2,1,0:T(8,128)(2,1)S(1)}, bf16[4,2,112,768]{3,2,1,0:T(8,128)(2,1)S(1)}, u32[]{:S(2)}, u32[]{:S(2)}) collective-permute-start(bf16[4,2,112,768]{3,2,1,0:T(8,128)(2,1)S(1)} %get-tuple-element.130), channel_id=1, source_target_pairs={{0,1},{1,0},{2,3},{3,2},{4,5},{5,4},{6,7},{7,6},{8,24},{9,25},{10,... | collective-permute-start | bytes 4128776 | tf_op jit(solution)/shard_map/ppermute | solution.py:84
  221.4 12.6 %collective-permute-start.34 = (bf16[1,192,768]{2,1,0:T(8,128)(2,1)S(1)}, bf16[1,192,768]{2,1,0:T(8,128)(2,1)S(1)}, u32[]{:S(2)}, u32[]{:S(2)}) collective-permute-start(bf16[1,192,768]{2,1,0:T(8,128)(2,1)S(1)} %get-tuple-element.128), channel_id=1, source_target_pairs={{0,4},{1,5},{2,6},{3,7},{4,0},{5,1},{6,2},{7,3},{8,12},{9,13},{10,... | collective-permute-start | bytes 884744 | tf_op jit(solution)/shard_map/ppermute | solution.py:84
  222.9 17.4 %collective-permute-start.35 = (bf16[1,192,768]{2,1,0:T(8,128)(2,1)S(1)}, bf16[1,192,768]{2,1,0:T(8,128)(2,1)S(1)}, u32[]{:S(2)}, u32[]{:S(2)}) collective-permute-start(bf16[1,192,768]{2,1,0:T(8,128)(2,1)S(1)} %get-tuple-element.127), channel_id=1, source_target_pairs={{0,2},{1,3},{2,4},{3,5},{4,6},{5,7},{6,0},{7,1},{8,10},{9,11},{10,... | collective-permute-start | bytes 884744 | tf_op jit(solution)/shard_map/ppermute | solution.py:84
  241.5 14.3 %collective-permute-start.36 = (bf16[4,112,768]{2,1,0:T(8,128)(2,1)S(1)}, bf16[4,112,768]{2,1,0:T(8,128)(2,1)S(1)}, u32[]{:S(2)}, u32[]{:S(2)}) collective-permute-start(bf16[4,112,768]{2,1,0:T(8,128)(2,1)S(1)} %get-tuple-element.133), channel_id=1, source_target_pairs={{0,16},{1,17},{2,18},{3,19},{4,20},{5,21},{6,22},{7,23},{8,9},{9,8... | collective-permute-start | bytes 2064392 | tf_op jit(solution)/shard_map/ppermute | solution.py:84
  242.7 8.8 %collective-permute-start.41 = (bf16[1,192,768]{2,1,0:T(8,128)(2,1)S(1)}, bf16[1,192,768]{2,1,0:T(8,128)(2,1)S(1)}, u32[]{:S(2)}, u32[]{:S(2)}) collective-permute-start(bf16[1,192,768]{2,1,0:T(8,128)(2,1)S(1)} %get-tuple-element.129), channel_id=1, source_target_pairs={{0,6},{1,7},{2,0},{3,1},{4,2},{5,3},{6,4},{7,5},{8,14},{9,15},{10,... | collective-permute-start | bytes 884744 | tf_op jit(solution)/shard_map/ppermute | solution.py:84
  256.6 14.3 %collective-permute-start.39 = (bf16[1,112,768]{2,1,0:T(8,128)(2,1)S(1)}, bf16[1,112,768]{2,1,0:T(8,128)(2,1)S(1)}, u32[]{:S(2)}, u32[]{:S(2)}) collective-permute-start(bf16[1,112,768]{2,1,0:T(8,128)(2,1)S(1)} %get-tuple-element.137), channel_id=1, source_target_pairs={{0,6},{1,7},{2,0},{3,1},{4,2},{5,3},{6,4},{7,5},{8,14},{9,15},{10,... | collective-permute-start | bytes 516104 | tf_op jit(solution)/shard_map/ppermute | solution.py:84
  256.6 14.2 %collective-permute-start.38 = (bf16[1,112,768]{2,1,0:T(8,128)(2,1)S(1)}, bf16[1,112,768]{2,1,0:T(8,128)(2,1)S(1)}, u32[]{:S(2)}, u32[]{:S(2)}) collective-permute-start(bf16[1,112,768]{2,1,0:T(8,128)(2,1)S(1)} %get-tuple-element.136), channel_id=1, source_target_pairs={{0,4},{1,5},{2,6},{3,7},{4,0},{5,1},{6,2},{7,3},{8,12},{9,13},{10,... | collective-permute-start | bytes 516104 | tf_op jit(solution)/shard_map/ppermute | solution.py:84
  259.8 11.8 %collective-permute-start.37 = (bf16[1,112,768]{2,1,0:T(8,128)(2,1)S(1)}, bf16[1,112,768]{2,1,0:T(8,128)(2,1)S(1)}, u32[]{:S(2)}, u32[]{:S(2)}) collective-permute-start(bf16[1,112,768]{2,1,0:T(8,128)(2,1)S(1)} %get-tuple-element.135), channel_id=1, source_target_pairs={{0,2},{1,3},{2,4},{3,5},{4,6},{5,7},{6,0},{7,1},{8,10},{9,11},{10,... | collective-permute-start | bytes 516104 | tf_op jit(solution)/shard_map/ppermute | solution.py:84
  260.3 18.0 %collective-permute-start.42 = (f32[7,768]{1,0:T(8,128)S(1)}, f32[7,768]{1,0:T(8,128)S(1)}, u32[]{:S(2)}, u32[]{:S(2)}) collective-permute-start(f32[7,768]{1,0:T(8,128)S(1)} %slice.133), channel_id=1, source_target_pairs={{1,0},{2,1},{3,2},{4,3},{5,4},{6,5},{7,6},{8,7},{9,8},{10,9},{11,1... | collective-permute-start | bytes 64520 | tf_op jit(solution)/shard_map/ppermute | solution.py:298
  271.7 10.3 %collective-permute-start.40 = (f32[5,768]{1,0:T(8,128)S(1)}, f32[5,768]{1,0:T(8,128)S(1)}, u32[]{:S(2)}, u32[]{:S(2)}) collective-permute-start(f32[5,768]{1,0:T(8,128)S(1)} %slice_bitcast_fusion.2), channel_id=1, source_target_pairs={{1,0},{2,1},{3,2},{4,3},{5,4},{6,5},{7,6},{8,7},{9,8},{10,9},{11,1... | collective-permute-start | bytes 46088 | tf_op jit(solution)/shard_map/ppermute | solution.py:298
  (36 other events, 243.5 us)
